TPU v7x, 128 devices: a whole 4x4x4 slice. The times are simulated.
128 devices in a mesh: dp: 8 (over x, core), blk: 16 (over y, z).
Axes of the slice: x: 4, y: 4, z: 4, core: 2. Of those that a mesh axis runs over, the one named last changes fastest.
Arguments:
- inputs: bfloat16 [8, 2048, 768], P('dp', 'blk'), may hold values from -6 to 6
- aug_source: int32 [8, 2048], P('dp', 'blk'), may hold values from 0 to 127
- aug_flags: int32 [8, 2048], P('dp', 'blk'), may hold values 0 or 1
- lengths: int32 [8], P('dp'), may hold values from 1921 to 2048, as said below
- head_flags: int32 [6], replicated, may hold values from 0 to 1, as said below
- cotangent: bfloat16 [8, 2048, 768], P('dp', 'blk'), may hold values from -6 to 6
- qkv_teacher: bfloat16 [768, 2304], replicated, may hold values from -0.21875 to 0.21875
- qv_bias_teacher: float32 [1536], replicated, may hold values from -1.5 to 1.5
- out_teacher: bfloat16 [768, 768], replicated, may hold values from -2.5 to 2.5
- up_teacher: bfloat16 [768, 3072], replicated, may hold values from -0.21875 to 0.21875
- down_teacher: bfloat16 [3072, 768], replicated, may hold values from -0.109375 to 0.109375
- up_bias_teacher: float32 [3072], replicated, may hold values from -1.5 to 1.5
- vectors_teacher: float32 [6, 768], replicated, may hold values from -1.5 to 1.5, as said below
- qkv_student: bfloat16 [768, 1152], replicated, may hold values from -0.21875 to 0.21875
- qv_bias_student: float32 [768], replicated, may hold values from -1.5 to 1.5
- out_student: bfloat16 [384, 768], replicated, may hold values from -3.5 to 3.5
- up_student: bfloat16 [768, 1536], replicated, may hold values from -0.21875 to 0.21875
- down_student: bfloat16 [1536, 768], replicated, may hold values from -0.15625 to 0.15625
- up_bias_student: float32 [1536], replicated, may hold values from -1.5 to 1.5
- vectors_student: float32 [6, 768], replicated, may hold values from -1.5 to 1.5, as said below
Outputs:
- output: float32 [8, 2048, 768], P('dp', 'blk')
- grad_inputs: float32 [8, 2048, 768], P('dp', 'blk')
- grad_qkv_teacher: float32 [768, 2304], P(('dp', 'blk'))
- grad_qv_bias_teacher: float32 [1536], P(('dp', 'blk'))
- grad_out_teacher: float32 [768, 768], P(None, ('dp', 'blk'))
- grad_up_teacher: float32 [768, 3072], P(('dp', 'blk'))
- grad_down_teacher: float32 [3072, 768], P(None, ('dp', 'blk'))
- grad_up_bias_teacher: float32 [3072], P(('dp', 'blk'))
- grad_vectors_teacher: float32 [6, 768], P(None, ('dp', 'blk'))
- grad_qkv_student: float32 [768, 1152], P(('dp', 'blk'))
- grad_qv_bias_student: float32 [768], P(('dp', 'blk'))
- grad_out_student: float32 [384, 768], P(None, ('dp', 'blk'))
- grad_up_student: float32 [768, 1536], P(('dp', 'blk'))
- grad_down_student: float32 [1536, 768], P(None, ('dp', 'blk'))
- grad_up_bias_student: float32 [1536], P(('dp', 'blk'))
- grad_vectors_student: float32 [6, 768], P(None, ('dp', 'blk'))
Inputs may be any that keep to these rules, and one draw needn't show every extreme that they name: `lengths`: among the 1 sequence of each index of dp, one has more than 1920 tokens valid; some sequence has all 2048 tokens valid. `head_flags`: at least one head has flag 1 and at least one has flag 0. `vectors_teacher`: rows 1 and 4 lie in 0.5 to 1.5. `vectors_student`: rows 1 and 4 lie in 0.5 to 1.5.
All inputs are finite; a program needn't handle non-finite values. No bound on the sum of `aug_flags` on one device may be relied on, other than what follows from the above.
Results may differ from a plain program's by a relative error of at most 0.035.
Values may be sent and summed in bfloat16 or wider, within the bound.
A program may use at most 192 MiB of HBM per device.

v0:
```python
import jax
import jax.numpy as jnp
from jax import lax
from jax.sharding import PartitionSpec as P

HDIM = 64


MASK_FILL = -1e30


def from_behind(block, axis, distance):
    devices = range(lax.axis_size(axis))
    route = [((i - distance) % len(devices), i) for i in devices]
    return lax.ppermute(block, axis, route)


def layer_norm(values, norm_gain, norm_shift):
    center = values - jnp.mean(values, axis=-1, keepdims=True)
    spread = jnp.mean(center * center, axis=-1, keepdims=True)
    return center * lax.rsqrt(spread + 1e-06) * norm_gain + norm_shift


def gelu_exact(values):
    return jax.nn.gelu(values, approximate=False)


def outer_rows(left_side, right_side):
    return lax.dot_general(
        left_side, right_side, (((0,), (0,)), ((), ())), preferred_element_type=jnp.float32
    )


def times_transpose(left_side, right_side):
    return lax.dot_general(
        left_side, right_side, (((1,), (1,)), ((), ())), preferred_element_type=jnp.float32
    )


def to_heads(matrix, seq_count, head_count):
    return matrix.reshape(seq_count, -1, head_count, HDIM)


def key_mask(lengths, owner_index, block_len):
    places = owner_index * block_len + jnp.arange(block_len)
    return places[None, :] < lengths[:, None]


def block_scores(queries, keys_now, key_valid):
    raw_scores = (
        jnp.einsum("sqhd,skhd->shqk", queries, keys_now, preferred_element_type=jnp.float32) * 0.125
    )
    return jnp.where(key_valid[:, None, None, :], raw_scores, MASK_FILL)


def block_probs(queries, keys_now, key_valid, log_total):
    return jnp.exp(block_scores(queries, keys_now, key_valid) - log_total[..., None])


def cycle_loop(absorb, carried, rotating, rotate):
    cycle_size = lax.axis_size("blk")
    position = lax.axis_index("blk")
    carried = absorb(carried, rotating, position)

    def one_turn(turn_index, bundle):
        moved_keys = rotate(bundle[1])
        return (absorb(bundle[0], moved_keys, (position - turn_index) % cycle_size), moved_keys)

    return lax.fori_loop(1, cycle_size, one_turn, (carried, rotating))[0]


def cycle_return(absorb, carried, keys_part, grads_part, rotate_keys, rotate_grads):
    cycle_size = lax.axis_size("blk")
    position = lax.axis_index("blk")
    carried, grads_part = absorb(carried, keys_part, grads_part, position)

    def one_turn(turn_index, bundle):
        keys_now = rotate_keys(bundle[1])
        grads_now = rotate_grads(bundle[2])
        carried_now, grads_now = absorb(
            bundle[0], keys_now, grads_now, (position - turn_index) % cycle_size
        )
        return (carried_now, keys_now, grads_now)

    carried, _, grads_part = lax.fori_loop(
        1, cycle_size, one_turn, (carried, keys_part, grads_part)
    )
    return (carried, rotate_grads(grads_part))


def attend_forward(queries, rotating, rotate, lengths, head_count):
    seq_count, block_len = (queries.shape[0], queries.shape[1])

    def absorb(carried, current, owner_index):
        maximum, row_total, weighted = carried
        keys_now = to_heads(current[0], seq_count, head_count)
        values_now = to_heads(current[1], seq_count, head_count)
        scores = block_scores(queries, keys_now, key_mask(lengths, owner_index, block_len))
        new_max = jnp.maximum(maximum, jnp.max(scores, axis=-1))
        factor = jnp.exp(maximum - new_max)
        weights = jnp.exp(scores - new_max[..., None])
        row_total = row_total * factor + jnp.sum(weights, axis=-1)
        update = jnp.einsum(
            "shqk,skhd->shqd",
            weights.astype(jnp.bfloat16),
            values_now,
            preferred_element_type=jnp.float32,
        )
        return (new_max, row_total, weighted * factor[..., None] + update)

    initial = (
        jnp.full((seq_count, head_count, block_len), MASK_FILL, jnp.float32),
        jnp.zeros((seq_count, head_count, block_len), jnp.float32),
        jnp.zeros((seq_count, head_count, block_len, HDIM), jnp.float32),
    )
    maximum, row_total, weighted = cycle_loop(absorb, initial, rotating, rotate)
    attended = (weighted / row_total[..., None]).transpose(0, 2, 1, 3)
    return (attended, maximum + jnp.log(row_total))


def qkv_forward(hidden_low, weight, bias_pair, head_span):
    joined = jnp.dot(hidden_low, weight, preferred_element_type=jnp.float32)
    queries = (joined[:, :head_span] + bias_pair[:head_span]).astype(jnp.bfloat16)
    keys_flat = joined[:, head_span : 2 * head_span].astype(jnp.bfloat16)
    values = (joined[:, 2 * head_span :] + bias_pair[head_span:]).astype(jnp.bfloat16)
    return (queries, keys_flat, values)


def qkv_backward(hidden_low, weight, grad_queries, grad_keys, grad_values):
    head_span = grad_queries.shape[1]
    joined = jnp.concatenate([grad_queries, grad_keys, grad_values], axis=1).astype(jnp.bfloat16)
    grad_weight = outer_rows(hidden_low, joined)
    low_sums = jnp.sum(joined.astype(jnp.float32), axis=0)
    grad_bias = jnp.concatenate([low_sums[:head_span], low_sums[2 * head_span :]])
    return (grad_weight, grad_bias, times_transpose(joined, weight))


def dense_forward(residual, attended, out_weight, up_weight, down_weight, up_bias, vectors):
    attended_low = attended.astype(jnp.bfloat16)
    first_sum = residual + (
        jnp.dot(attended_low, out_weight, preferred_element_type=jnp.float32) + vectors[0]
    )
    normed, first_back = jax.vjp(layer_norm, first_sum, vectors[1], vectors[2])
    normed_low = normed.astype(jnp.bfloat16)
    upward = jnp.dot(normed_low, up_weight, preferred_element_type=jnp.float32) + up_bias
    activated, gelu_back = jax.vjp(gelu_exact, upward)
    activated_low = activated.astype(jnp.bfloat16)
    second_sum = normed + (
        jnp.dot(activated_low, down_weight, preferred_element_type=jnp.float32) + vectors[3]
    )
    result, second_back = jax.vjp(layer_norm, second_sum, vectors[4], vectors[5])
    return (result, (attended_low, normed_low, activated_low, first_back, gelu_back, second_back))


def dense_backward(grad_result, kept, out_weight, up_weight, down_weight):
    attended_low, normed_low, activated_low, first_back, gelu_back, second_back = kept
    grad_second, grad_gain_two, grad_shift_two = second_back(grad_result)
    down_low = grad_second.astype(jnp.bfloat16)
    grad_down = outer_rows(activated_low, down_low)
    (grad_upward,) = gelu_back(times_transpose(down_low, down_weight))
    upward_low = grad_upward.astype(jnp.bfloat16)
    grad_up = outer_rows(normed_low, upward_low)
    grad_first, grad_gain_one, grad_shift_one = first_back(
        grad_second + times_transpose(upward_low, up_weight)
    )
    first_low = grad_first.astype(jnp.bfloat16)
    grad_out = outer_rows(attended_low, first_low)
    grad_attended = times_transpose(first_low, out_weight).astype(jnp.bfloat16)
    grad_vectors = jnp.stack(
        [
            jnp.sum(grad_first, axis=0),
            grad_gain_one,
            grad_shift_one,
            jnp.sum(grad_second, axis=0),
            grad_gain_two,
            grad_shift_two,
        ]
    )
    return (
        grad_first,
        grad_attended,
        (grad_out, grad_up, grad_down, jnp.sum(grad_upward, axis=0), grad_vectors),
    )


def per_device(
    inputs,
    aug_source,
    aug_flags,
    lengths,
    head_flags,
    cotangent,
    qkv_teacher,
    qv_bias_teacher,
    out_teacher,
    up_teacher,
    down_teacher,
    up_bias_teacher,
    vectors_teacher,
    qkv_student,
    qv_bias_student,
    out_student,
    up_student,
    down_student,
    up_bias_student,
    vectors_student,
):
    seq_count, block_len, model_width = inputs.shape
    row_count = seq_count * block_len
    cycle_size = lax.axis_size("blk")
    position = lax.axis_index("blk")
    teacher_width = qkv_teacher.shape[1] // 3
    student_width = qkv_student.shape[1] // 3
    teacher_heads = teacher_width // HDIM
    student_heads = student_width // HDIM
    places = position * block_len + jnp.arange(block_len)
    query_valid = (places[None, :] < lengths[:, None]).astype(jnp.float32)
    map_weight = (
        2.0
        * block_len
        * cycle_size
        * head_flags.astype(jnp.float32)[None, :, None]
        * query_valid[:, None, :]
    )
    replaced = aug_flags == 1
    chooser = jnp.logical_and(
        aug_source[:, :, None] == jnp.arange(block_len)[None, None, :], replaced[:, :, None]
    )
    taken_rows = jnp.einsum(
        "sqj,sjd->sqd", chooser.astype(jnp.bfloat16), inputs, preferred_element_type=jnp.float32
    )
    augmented = jnp.where(replaced[:, :, None], taken_rows, inputs.astype(jnp.float32)).reshape(
        row_count, model_width
    )

    def teacher_rotation(rotating):
        return from_behind((rotating[0], rotating[1]), "blk", 1)

    def student_rotation(rotating):
        return from_behind((rotating[0], rotating[1]), "blk", 1)

    def map_rotation(rotating):
        return from_behind((rotating[0], rotating[1]), "blk", 1)

    def student_key_rotation(rotating):
        return from_behind((rotating[0], rotating[1], rotating[2]), "blk", 1)

    def student_grad_rotation(rotating):
        return (
            from_behind(rotating[0].astype(jnp.bfloat16), "blk", 1).astype(jnp.float32),
            from_behind(rotating[1].astype(jnp.bfloat16), "blk", 1).astype(jnp.float32),
        )

    def teacher_key_rotation(rotating):
        return from_behind((rotating[0], rotating[1], rotating[2]), "blk", 1)

    def teacher_grad_rotation(rotating):
        return (
            from_behind(rotating[0].astype(jnp.bfloat16), "blk", 1).astype(jnp.float32),
            from_behind(rotating[1].astype(jnp.bfloat16), "blk", 1).astype(jnp.float32),
        )

    teacher_low = augmented.astype(jnp.bfloat16)
    teacher_query, teacher_key, teacher_value = qkv_forward(
        teacher_low, qkv_teacher, qv_bias_teacher, teacher_width
    )
    teacher_query_heads = to_heads(teacher_query, seq_count, teacher_heads)
    teacher_key_blocks = teacher_key.reshape(seq_count, block_len, teacher_width)
    teacher_value_blocks = teacher_value.reshape(seq_count, block_len, teacher_width)
    teacher_attended, teacher_logsum = attend_forward(
        teacher_query_heads,
        (teacher_key_blocks, teacher_value_blocks),
        teacher_rotation,
        lengths,
        teacher_heads,
    )
    hidden, teacher_kept = dense_forward(
        augmented,
        teacher_attended.reshape(row_count, teacher_width),
        out_teacher,
        up_teacher,
        down_teacher,
        up_bias_teacher,
        vectors_teacher,
    )
    student_low = hidden.astype(jnp.bfloat16)
    student_query, student_key, student_value = qkv_forward(
        student_low, qkv_student, qv_bias_student, student_width
    )
    student_query_heads = to_heads(student_query, seq_count, student_heads)
    student_key_blocks = student_key.reshape(seq_count, block_len, student_width)
    student_value_blocks = student_value.reshape(seq_count, block_len, student_width)
    student_attended, student_logsum = attend_forward(
        student_query_heads,
        (student_key_blocks, student_value_blocks),
        student_rotation,
        lengths,
        student_heads,
    )
    output, student_kept = dense_forward(
        hidden,
        student_attended.reshape(row_count, student_width),
        out_student,
        up_student,
        down_student,
        up_bias_student,
        vectors_student,
    )
    teacher_query_part = teacher_query_heads[:, :, :student_heads]
    teacher_logsum_part = teacher_logsum[:, :student_heads]
    teacher_key_part = teacher_key_blocks[:, :, :student_width]
    grad_output = cotangent.astype(jnp.float32).reshape(row_count, model_width)
    grad_hidden_res, student_grad_flat, student_dense = dense_backward(
        grad_output, student_kept, out_student, up_student, down_student
    )
    student_grad_out = to_heads(student_grad_flat, seq_count, student_heads)
    student_delta = jnp.sum(
        student_grad_out.astype(jnp.float32) * student_attended, axis=-1
    ).transpose(0, 2, 1)

    def absorb_maps(carried, rotating, owner_index):
        key_valid = key_mask(lengths, owner_index, block_len)
        student_probs = block_probs(
            student_query_heads,
            to_heads(rotating[0], seq_count, student_heads),
            key_valid,
            student_logsum,
        )
        teacher_probs = block_probs(
            teacher_query_part,
            to_heads(rotating[1], seq_count, student_heads),
            key_valid,
            teacher_logsum_part,
        )
        prob_gap = student_probs - teacher_probs
        return (
            carried[0] + jnp.sum(student_probs * prob_gap, axis=-1),
            carried[1] + jnp.sum(teacher_probs * prob_gap, axis=-1),
        )

    zero_rows = jnp.zeros((seq_count, student_heads, block_len), jnp.float32)
    student_map_sum, teacher_map_sum = cycle_loop(
        absorb_maps, (zero_rows, zero_rows), (student_key_blocks, teacher_key_part), map_rotation
    )
    student_map_delta = map_weight * student_map_sum
    teacher_map_delta = -map_weight * teacher_map_sum

    def absorb_student(carried, keys_part, grads_part, owner_index):
        key_valid = key_mask(lengths, owner_index, block_len)
        keys_now = to_heads(keys_part[0], seq_count, student_heads)
        values_now = to_heads(keys_part[1], seq_count, student_heads)
        student_probs = block_probs(student_query_heads, keys_now, key_valid, student_logsum)
        teacher_probs = block_probs(
            teacher_query_part,
            to_heads(keys_part[2], seq_count, student_heads),
            key_valid,
            teacher_logsum_part,
        )
        grad_probs = jnp.einsum(
            "sqhd,skhd->shqk", student_grad_out, values_now, preferred_element_type=jnp.float32
        )
        grad_scores = student_probs * (
            grad_probs
            - student_delta[..., None]
            + map_weight[..., None] * (student_probs - teacher_probs)
            - student_map_delta[..., None]
        )
        grad_low = grad_scores.astype(jnp.bfloat16)
        grad_queries = carried + 0.125 * jnp.einsum(
            "shqk,skhd->sqhd", grad_low, keys_now, preferred_element_type=jnp.float32
        )
        key_term = 0.125 * jnp.einsum(
            "shqk,sqhd->skhd", grad_low, student_query_heads, preferred_element_type=jnp.float32
        )
        value_term = jnp.einsum(
            "shqk,sqhd->skhd",
            student_probs.astype(jnp.bfloat16),
            student_grad_out,
            preferred_element_type=jnp.float32,
        )
        return (
            grad_queries,
            (
                grads_part[0] + key_term.reshape(seq_count, block_len, student_width),
                grads_part[1] + value_term.reshape(seq_count, block_len, student_width),
            ),
        )

    student_zero = jnp.zeros((seq_count, block_len, student_width), jnp.float32)
    student_grad_queries, student_grad_kv = cycle_return(
        absorb_student,
        jnp.zeros((seq_count, block_len, student_heads, HDIM), jnp.float32),
        (student_key_blocks, student_value_blocks, teacher_key_part),
        (student_zero, student_zero),
        student_key_rotation,
        student_grad_rotation,
    )
    grad_qkv_s, grad_bias_s, grad_hidden_proj = qkv_backward(
        student_low,
        qkv_student,
        student_grad_queries.reshape(row_count, student_width),
        student_grad_kv[0].reshape(row_count, student_width),
        student_grad_kv[1].reshape(row_count, student_width),
    )
    grad_hidden = grad_hidden_res + grad_hidden_proj
    grad_aug_res, teacher_grad_flat, teacher_dense = dense_backward(
        grad_hidden, teacher_kept, out_teacher, up_teacher, down_teacher
    )
    teacher_grad_out = to_heads(teacher_grad_flat, seq_count, teacher_heads)
    teacher_delta = jnp.sum(
        teacher_grad_out.astype(jnp.float32) * teacher_attended, axis=-1
    ).transpose(0, 2, 1)

    def absorb_teacher(carried, keys_part, grads_part, owner_index):
        key_valid = key_mask(lengths, owner_index, block_len)
        keys_now = to_heads(keys_part[0], seq_count, teacher_heads)
        values_now = to_heads(keys_part[1], seq_count, teacher_heads)
        teacher_probs = block_probs(teacher_query_heads, keys_now, key_valid, teacher_logsum)
        student_probs = block_probs(
            student_query_heads,
            to_heads(keys_part[2], seq_count, student_heads),
            key_valid,
            student_logsum,
        )
        grad_probs = jnp.einsum(
            "sqhd,skhd->shqk", teacher_grad_out, values_now, preferred_element_type=jnp.float32
        )
        grad_scores = teacher_probs * (grad_probs - teacher_delta[..., None])
        leading = teacher_probs[:, :student_heads]
        extra_term = leading * (
            map_weight[..., None] * (leading - student_probs) - teacher_map_delta[..., None]
        )
        grad_scores = jnp.concatenate(
            [grad_scores[:, :student_heads] + extra_term, grad_scores[:, student_heads:]], axis=1
        )
        grad_low = grad_scores.astype(jnp.bfloat16)
        grad_queries = carried + 0.125 * jnp.einsum(
            "shqk,skhd->sqhd", grad_low, keys_now, preferred_element_type=jnp.float32
        )
        key_term = 0.125 * jnp.einsum(
            "shqk,sqhd->skhd", grad_low, teacher_query_heads, preferred_element_type=jnp.float32
        )
        value_term = jnp.einsum(
            "shqk,sqhd->skhd",
            teacher_probs.astype(jnp.bfloat16),
            teacher_grad_out,
            preferred_element_type=jnp.float32,
        )
        return (
            grad_queries,
            (
                grads_part[0] + key_term.reshape(seq_count, block_len, teacher_width),
                grads_part[1] + value_term.reshape(seq_count, block_len, teacher_width),
            ),
        )

    teacher_zero = jnp.zeros((seq_count, block_len, teacher_width), jnp.float32)
    teacher_grad_queries, teacher_grad_kv = cycle_return(
        absorb_teacher,
        jnp.zeros((seq_count, block_len, teacher_heads, HDIM), jnp.float32),
        (teacher_key_blocks, teacher_value_blocks, student_key_blocks),
        (teacher_zero, teacher_zero),
        teacher_key_rotation,
        teacher_grad_rotation,
    )
    grad_qkv_t, grad_bias_t, grad_aug_proj = qkv_backward(
        teacher_low,
        qkv_teacher,
        teacher_grad_queries.reshape(row_count, teacher_width),
        teacher_grad_kv[0].reshape(row_count, teacher_width),
        teacher_grad_kv[1].reshape(row_count, teacher_width),
    )
    grad_aug = (grad_aug_res + grad_aug_proj).reshape(seq_count, block_len, model_width)
    copied_back = jnp.einsum(
        "sqj,sqd->sjd",
        chooser.astype(jnp.float32),
        grad_aug,
        precision=lax.Precision.HIGHEST,
        preferred_element_type=jnp.float32,
    )
    grad_inputs = jnp.where(replaced[:, :, None], 0.0, grad_aug) + copied_back
    reduced = (
        lax.psum_scatter(grad_qkv_t, ("dp", "blk"), scatter_dimension=0, tiled=True),
        lax.psum_scatter(grad_bias_t, ("dp", "blk"), scatter_dimension=0, tiled=True),
        lax.psum_scatter(teacher_dense[0], ("dp", "blk"), scatter_dimension=1, tiled=True),
        lax.psum_scatter(teacher_dense[1], ("dp", "blk"), scatter_dimension=0, tiled=True),
        lax.psum_scatter(teacher_dense[2], ("dp", "blk"), scatter_dimension=1, tiled=True),
        lax.psum_scatter(teacher_dense[3], ("dp", "blk"), scatter_dimension=0, tiled=True),
        lax.psum_scatter(teacher_dense[4], ("dp", "blk"), scatter_dimension=1, tiled=True),
        lax.psum_scatter(grad_qkv_s, ("dp", "blk"), scatter_dimension=0, tiled=True),
        lax.psum_scatter(grad_bias_s, ("dp", "blk"), scatter_dimension=0, tiled=True),
        lax.psum_scatter(student_dense[0], ("dp", "blk"), scatter_dimension=1, tiled=True),
        lax.psum_scatter(student_dense[1], ("dp", "blk"), scatter_dimension=0, tiled=True),
        lax.psum_scatter(student_dense[2], ("dp", "blk"), scatter_dimension=1, tiled=True),
        lax.psum_scatter(student_dense[3], ("dp", "blk"), scatter_dimension=0, tiled=True),
        lax.psum_scatter(student_dense[4], ("dp", "blk"), scatter_dimension=1, tiled=True),
    )
    return (output.reshape(seq_count, block_len, model_width), grad_inputs) + tuple(reduced)


def solution(mesh):
    placed = (
        P("dp", "blk", None),
        P("dp", "blk"),
        P("dp", "blk"),
        P("dp"),
        P(),
        P("dp", "blk", None),
        P(),
        P(),
        P(),
        P(),
        P(),
        P(),
        P(),
        P(),
        P(),
        P(),
        P(),
        P(),
        P(),
        P(),
    )
    return jax.shard_map(
        per_device,
        mesh=mesh,
        in_specs=placed,
        out_specs=(
            P("dp", "blk", None),
            P("dp", "blk", None),
            P(("dp", "blk"), None),
            P(("dp", "blk")),
            P(None, ("dp", "blk")),
            P(("dp", "blk"), None),
            P(None, ("dp", "blk")),
            P(("dp", "blk")),
            P(None, ("dp", "blk")),
            P(("dp", "blk"), None),
            P(("dp", "blk")),
            P(None, ("dp", "blk")),
            P(("dp", "blk"), None),
            P(None, ("dp", "blk")),
            P(("dp", "blk")),
            P(None, ("dp", "blk")),
        ),
        check_vma=False,
    )
```

profile of v0, /device:TPU:5, one launch (start us, length us, event | category | flops | bytes accessed | tf_op | source)
XLA Modules:
  0.0 3769.9 jit_solution(7511419248982100645)
XLA Ops:
  34.7 242.8 %while.119 = (s32[]{:T(128)}, f32[1,12,128]{2,1,0:T(8,128)S(1)}, f32[1,12,128]{2,1,0:T(8,128)S(1)}, f32[1,12,128,64]{2,3,1,0:T(8,128)}, bf16[1,128,768]{1,2,0:T(...) while((s32[]{:T(128)}, f32[1,12,128]{2,1,0:T(8,128)S(1)}, ...), condition=%wide.region_5.6_spmd, body=%wide.region_2.5_spmd.sunk | while | flops 51909392 | bytes 9339546 | solution.py:69
  225.0 9.2 collective-permute-done
  241.6 9.8 collective-permute-done
  259.3 9.8 collective-permute-done
  321.9 237.6 %while.120 = (s32[]{:T(128)}, f32[1,6,128]{2,1,0:T(8,128)S(1)}, f32[1,6,128]{2,1,0:T(8,128)}, f32[1,6,128,64]{2,3,1,0:T(8,128)}, bf16[1,128,384]{1,2,0:T(8,128)(...) while((s32[]{:T(128)}, f32[1,6,128]{2,1,0:T(8,128)S(1)}, ...), condition=%wide.region_15.16_spmd, body=%wide.region_12.15_spmd.sunk | while | flops 25954832 | bytes 3097186 | solution.py:69
  582.5 212.0 %while.121 = (s32[]{:T(128)}, f32[1,6,128]{2,1,0:T(8,128)}, f32[1,6,128]{2,1,0:T(8,128)S(1)}, bf16[1,128,384]{1,2,0:T(8,128)(2,1)}, bf16[1,128,384]{1,2,0:T(8,12...) while((s32[]{:T(128)}, f32[1,6,128]{2,1,0:T(8,128)}, ...), condition=%wide.region_30.31_spmd, body=%wide.region_27.30_spmd.sunk | while | flops 26247440 | bytes 2415402 | solution.py:69
  722.9 9.5 collective-permute-done.4
  801.6 668.1 %while.122 = (s32[]{:T(128)}, f32[1,128,6,64]{1,3,2,0:T(8,128)}, bf16[1,128,384]{1,2,0:T(8,128)(2,1)}, bf16[1,128,384]{1,2,0:T(8,128)(2,1)}, bf16[1,128,384]{1,2...) while((s32[]{:T(128)}, f32[1,128,6,64]{1,3,2,0:T(8,128)}, ...), condition=%wide.region_32.33_spmd.clone, body=%wide.region_31.32_spmd.clone.sunk | while | flops 77317136 | bytes 10341930 | solution.py:85
  801.6 53.6 %collective-permute-start.10 = (bf16[1,128,384]{1,2,0:T(8,128)(2,1)}, bf16[1,128,384]{1,2,0:T(8,128)(2,1)}, u32[]{:S(2)}, u32[]{:S(2)}) collective-permute-start(bf16[1,128,384]{1,2,0:T(8,128)(2,1)} %get-tuple-element.2651), channel_id=1, source_target_pairs={{15,0},{0,1},{1,2},{2,3},{3,4},{4,5},{5,6},{6,7},{7,8},{8,9},{9,10... | collective-permute-start | bytes 294920 | tf_op jit(solution)/shard_map/while/body/eval_jaxpr/ppermute | solution.py:15
  855.1 8.9 collective-permute-start.9
  869.4 9.6 collective-permute-done.6
  896.4 8.9 collective-permute-start.9
  910.6 9.6 collective-permute-done.6
  937.7 8.9 collective-permute-start.9
  951.9 9.6 collective-permute-done.6
  978.9 8.9 collective-permute-start.9
  993.1 9.6 collective-permute-done.6
  1020.2 8.9 collective-permute-start.9
  1034.4 9.6 collective-permute-done.6
  1061.4 8.9 collective-permute-start.9
  1075.7 9.6 collective-permute-done.6
  1102.7 8.9 collective-permute-start.9
  1116.9 9.6 collective-permute-done.6
  1143.9 8.9 collective-permute-start.9
  1158.2 9.6 collective-permute-done.6
  1185.2 8.9 collective-permute-start.9
  1199.4 9.6 collective-permute-done.6
  1226.4 8.9 collective-permute-start.9
  1240.7 9.6 collective-permute-done.6
  1267.7 8.9 collective-permute-start.9
  1281.9 9.6 collective-permute-done.6
  1308.9 8.9 collective-permute-start.9
  1323.2 9.6 collective-permute-done.6
  1350.2 8.9 collective-permute-start.9
  1364.4 9.6 collective-permute-done.6
  1405.7 9.6 collective-permute-done.6
  1446.9 9.6 collective-permute-done.6
  1512.7 747.6 %while.123 = (s32[]{:T(128)}, f32[1,128,12,64]{1,3,2,0:T(8,128)}, bf16[1,128,768]{1,2,0:T(8,128)(2,1)}, bf16[1,128,768]{1,2,0:T(8,128)(2,1)}, bf16[1,128,384]{1,...) while((s32[]{:T(128)}, f32[1,128,12,64]{1,3,2,0:T(8,128)}, ...), condition=%wide.region_39.40_spmd.clone, body=%wide.region_38.39_spmd.clone.sunk | while | flops 142345232 | bytes 19723928 | solution.py:85
  1513.0 10.3 collective-permute-start.15
  1523.2 8.9 collective-permute-start.14
  1538.5 12.8 collective-permute-done.11
  1588.2 12.8 collective-permute-done.11
  1637.9 12.8 collective-permute-done.11
  1687.6 12.8 collective-permute-done.11
  1737.4 12.8 collective-permute-done.11
  1787.1 12.8 collective-permute-done.11
  1836.8 12.8 collective-permute-done.11
  1886.6 12.8 collective-permute-done.11
  1936.3 12.8 collective-permute-done.11
  1986.0 12.8 collective-permute-done.11
  2035.8 12.8 collective-permute-done.11
  2085.5 12.8 collective-permute-done.11
  2120.0 8.9 collective-permute-start.14
  2135.2 12.8 collective-permute-done.11
  2184.9 12.8 collective-permute-done.11
  2234.7 12.8 collective-permute-done.11
  2279.5 555.6 %fusion.201 = (f32[8,2304]{1,0:T(8,128)}, f32[768,8]{0,1:T(8,128)}, f32[8,3072]{1,0:T(8,128)}, f32[3072,8]{0,1:T(8,128)}, f32[8,1536]{1,0:T(8,128)}, /*index=5*/f32[1536,8]{0,1:T(8,128)}) fusion(f32[768,2304]{1,0:T(8,128)} %fusion.164, f32[768,768]{0,1:T(8,128)} %fusion.192, f32[768,3072]{1,0:T(8,128)} %fusion.139, f32[3072,768]{0,1:T(8,128)} %fusion.190, ...), kind=kCustom, calls=%all-reduce-scatter.6 | all-reduce-scatter fusion | flops 12582913 | bytes 38141952
  3251.5 87.7 %all-reduce.20 = (f32[1536]{0:T(1024)}, f32[3072]{0:T(1024)}, f32[6,768]{1,0:T(8,128)}, f32[768]{0:T(1024)}, f32[1536]{0:T(1024)}, /*index=5*/f32[6,768]{1,0:T(8,128)}) all-reduce(f32[1536]{0:T(1024)S(1)} %pad_maximum_fusion.8, f32[3072]{0:T(1024)} %get-tuple-element.2057, ...), channel_id=3, replica_groups=mesh['dp'=8,'blk'=16] {'dp','blk'}, use_global_device_ids=true, to_apply=%region_42.43.clone | all-reduce | flops 16128 | bytes 129024
  3389.0 47.1 %concatenate.59 = f32[768,262]{0,1:T(8,128)} concatenate(f32[768,6]{0,1:T(8,128)} %copy-done.154, f32[768,8]{0,1:T(8,128)} %copy-done.153, f32[768,8]{0,1:T(8,128)} %copy-done.155, f32[768,8]{0,1:T(8,128)} %copy-done.156, f32[768,8]{0,1:T(8,128)} %copy-done.157, f32[768,8]{0,1:T(8,128)} %copy-done.158, f32[768,8]{0,1:T(8,128)} %copy-done.159, f32[768,8]{0,1:T(8,128)} %copy-done.160, ...), dimensions={1} | concatenate | bytes 1609728
  3448.3 49.9 %concatenate.62 = f32[262,1536]{1,0:T(8,128)} concatenate(f32[6,1536]{1,0:T(8,128)} %copy-done.100, f32[8,1536]{1,0:T(8,128)} %copy-done.97, f32[8,1536]{1,0:T(8,128)} %copy-done.98, f32[8,1536]{1,0:T(8,128)} %copy-done.99, f32[8,1536]{1,0:T(8,128)} %copy-done.101, f32[8,1536]{1,0:T(8,128)} %copy-done.102, f32[8,1536]{1,0:T(8,128)} %copy-done.103, f32[8,1536]{1,0:T(8,128)} %copy-done.104, ...), dimensions={0} | concatenate | bytes 3219456
  3512.9 49.8 %concatenate.63 = f32[1536,262]{0,1:T(8,128)} concatenate(f32[1536,6]{0,1:T(8,128)} %copy-done.96, f32[1536,8]{0,1:T(8,128)} %copy-done.123, f32[1536,8]{0,1:T(8,128)} %copy-done.125, f32[1536,8]{0,1:T(8,128)} %copy-done.127, f32[1536,8]{0,1:T(8,128)} %copy-done.129, f32[1536,8]{0,1:T(8,128)} %copy-done.131, f32[1536,8]{0,1:T(8,128)} %copy-done.133, f32[1536,8]{0,1:T(8,128)} %copy-done.135, ...), dimensions={1} | concatenate | bytes 3219456
  3575.4 54.1 %concatenate.58 = f32[262,2304]{1,0:T(8,128)} concatenate(f32[6,2304]{1,0:T(8,128)} %copy-done.84, f32[8,2304]{1,0:T(8,128)} %collective-permute-done.50, f32[8,2304]{1,0:T(8,128)} %collective-permute-done.49, f32[8,2304]{1,0:T(8,128)} %collective-permute-done.48, f32[8,2304]{1,0:T(8,128)} %collective-permute-done.47, f32[8,2304]{1,0:T(8,128)} %collective-permute-done.46, ...), dimensions={0} | concatenate | bytes 4829184
  3645.0 55.9 %concatenate.60 = f32[262,3072]{1,0:T(8,128)} concatenate(f32[6,3072]{1,0:T(8,128)} %copy-done.83, f32[8,3072]{1,0:T(8,128)} %collective-permute-done.114, f32[8,3072]{1,0:T(8,128)} %collective-permute-done.113, f32[8,3072]{1,0:T(8,128)} %collective-permute-done.112, f32[8,3072]{1,0:T(8,128)} %collective-permute-done.111, f32[8,3072]{1,0:T(8,128)} %collective-permute-done.110, ...), dimensions={0} | concatenate | bytes 6438912
  3701.0 55.9 %concatenate.61 = f32[3072,262]{0,1:T(8,128)} concatenate(f32[3072,6]{0,1:T(8,128)} %copy-done.82, f32[3072,8]{0,1:T(8,128)} %collective-permute-done.146, f32[3072,8]{0,1:T(8,128)} %collective-permute-done.145, f32[3072,8]{0,1:T(8,128)} %collective-permute-done.144, f32[3072,8]{0,1:T(8,128)} %collective-permute-done.143, f32[3072,8]{0,1:T(8,128)} %collective-permute-done.142, ...), dimensions={1} | concatenate | bytes 6438912
  (2664 shorter events, 2214.4 us)
Async XLA Ops:
  7.2 3752.9 %all-reduce.25.cloned.1.call-start = ((), (), s32[]{:S(2)}) async-start(), calls=%async_computation | async-start | bytes 9437184
  801.6 82.8 %collective-permute-start.10 = (bf16[1,128,384]{1,2,0:T(8,128)(2,1)}, bf16[1,128,384]{1,2,0:T(8,128)(2,1)}, u32[]{:S(2)}, u32[]{:S(2)}) collective-permute-start(bf16[1,128,384]{1,2,0:T(8,128)(2,1)} %get-tuple-element.2651), channel_id=1, source_target_pairs={{15,0},{0,1},{1,2},{2,3},{3,4},{4,5},{5,6},{6,7},{7,8},{8,9},{9,10... | collective-permute-start | bytes 294920 | tf_op jit(solution)/shard_map/while/body/eval_jaxpr/ppermute | solution.py:15
  896.4 35.4 collective-permute-start.9
  937.7 35.4 collective-permute-start.9
  1513.0 47.5 %collective-permute-start.15 = (bf16[1,128,768]{1,2,0:T(8,128)(2,1)}, bf16[1,128,768]{1,2,0:T(8,128)(2,1)}, u32[]{:S(2)}, u32[]{:S(2)}) collective-permute-start(bf16[1,128,768]{1,2,0:T(8,128)(2,1)} %get-tuple-element.2720), channel_id=1, source_target_pairs={{15,0},{0,1},{1,2},{2,3},{3,4},{4,5},{5,6},{6,7},{7,8},{8,9},{9,10... | collective-permute-start | bytes 589832 | tf_op jit(solution)/shard_map/while/body/eval_jaxpr/ppermute | solution.py:15
  1523.2 39.2 %collective-permute-start.14 = (bf16[1,128,768]{1,2,0:T(8,128)(2,1)}, bf16[1,128,768]{1,2,0:T(8,128)(2,1)}, u32[]{:S(2)}, u32[]{:S(2)}) collective-permute-start(bf16[1,128,768]{1,2,0:T(8,128)(2,1)} %get-tuple-element.2719), channel_id=1, source_target_pairs={{15,0},{0,1},{1,2},{2,3},{3,4},{4,5},{5,6},{6,7},{7,8},{8,9},{9,10... | collective-permute-start | bytes 589832 | tf_op jit(solution)/shard_map/while/body/eval_jaxpr/ppermute | solution.py:15
  1564.1 46.0 %collective-permute-start.15 = (bf16[1,128,768]{1,2,0:T(8,128)(2,1)}, bf16[1,128,768]{1,2,0:T(8,128)(2,1)}, u32[]{:S(2)}, u32[]{:S(2)}) collective-permute-start(bf16[1,128,768]{1,2,0:T(8,128)(2,1)} %get-tuple-element.2720), channel_id=1, source_target_pairs={{15,0},{0,1},{1,2},{2,3},{3,4},{4,5},{5,6},{6,7},{7,8},{8,9},{9,10... | collective-permute-start | bytes 589832 | tf_op jit(solution)/shard_map/while/body/eval_jaxpr/ppermute | solution.py:15
  1573.0 39.2 %collective-permute-start.14 = (bf16[1,128,768]{1,2,0:T(8,128)(2,1)}, bf16[1,128,768]{1,2,0:T(8,128)(2,1)}, u32[]{:S(2)}, u32[]{:S(2)}) collective-permute-start(bf16[1,128,768]{1,2,0:T(8,128)(2,1)} %get-tuple-element.2719), channel_id=1, source_target_pairs={{15,0},{0,1},{1,2},{2,3},{3,4},{4,5},{5,6},{6,7},{7,8},{8,9},{9,10... | collective-permute-start | bytes 589832 | tf_op jit(solution)/shard_map/while/body/eval_jaxpr/ppermute | solution.py:15
  1613.9 46.0 %collective-permute-start.15 = (bf16[1,128,768]{1,2,0:T(8,128)(2,1)}, bf16[1,128,768]{1,2,0:T(8,128)(2,1)}, u32[]{:S(2)}, u32[]{:S(2)}) collective-permute-start(bf16[1,128,768]{1,2,0:T(8,128)(2,1)} %get-tuple-element.2720), channel_id=1, source_target_pairs={{15,0},{0,1},{1,2},{2,3},{3,4},{4,5},{5,6},{6,7},{7,8},{8,9},{9,10... | collective-permute-start | bytes 589832 | tf_op jit(solution)/shard_map/while/body/eval_jaxpr/ppermute | solution.py:15
  1622.7 39.2 %collective-permute-start.14 = (bf16[1,128,768]{1,2,0:T(8,128)(2,1)}, bf16[1,128,768]{1,2,0:T(8,128)(2,1)}, u32[]{:S(2)}, u32[]{:S(2)}) collective-permute-start(bf16[1,128,768]{1,2,0:T(8,128)(2,1)} %get-tuple-element.2719), channel_id=1, source_target_pairs={{15,0},{0,1},{1,2},{2,3},{3,4},{4,5},{5,6},{6,7},{7,8},{8,9},{9,10... | collective-permute-start | bytes 589832 | tf_op jit(solution)/shard_map/while/body/eval_jaxpr/ppermute | solution.py:15
  1663.6 46.0 %collective-permute-start.15 = (bf16[1,128,768]{1,2,0:T(8,128)(2,1)}, bf16[1,128,768]{1,2,0:T(8,128)(2,1)}, u32[]{:S(2)}, u32[]{:S(2)}) collective-permute-start(bf16[1,128,768]{1,2,0:T(8,128)(2,1)} %get-tuple-element.2720), channel_id=1, source_target_pairs={{15,0},{0,1},{1,2},{2,3},{3,4},{4,5},{5,6},{6,7},{7,8},{8,9},{9,10... | collective-permute-start | bytes 589832 | tf_op jit(solution)/shard_map/while/body/eval_jaxpr/ppermute | solution.py:15
  1672.4 39.2 %collective-permute-start.14 = (bf16[1,128,768]{1,2,0:T(8,128)(2,1)}, bf16[1,128,768]{1,2,0:T(8,128)(2,1)}, u32[]{:S(2)}, u32[]{:S(2)}) collective-permute-start(bf16[1,128,768]{1,2,0:T(8,128)(2,1)} %get-tuple-element.2719), channel_id=1, source_target_pairs={{15,0},{0,1},{1,2},{2,3},{3,4},{4,5},{5,6},{6,7},{7,8},{8,9},{9,10... | collective-permute-start | bytes 589832 | tf_op jit(solution)/shard_map/while/body/eval_jaxpr/ppermute | solution.py:15
  1713.3 46.0 %collective-permute-start.15 = (bf16[1,128,768]{1,2,0:T(8,128)(2,1)}, bf16[1,128,768]{1,2,0:T(8,128)(2,1)}, u32[]{:S(2)}, u32[]{:S(2)}) collective-permute-start(bf16[1,128,768]{1,2,0:T(8,128)(2,1)} %get-tuple-element.2720), channel_id=1, source_target_pairs={{15,0},{0,1},{1,2},{2,3},{3,4},{4,5},{5,6},{6,7},{7,8},{8,9},{9,10... | collective-permute-start | bytes 589832 | tf_op jit(solution)/shard_map/while/body/eval_jaxpr/ppermute | solution.py:15
  1722.1 39.2 %collective-permute-start.14 = (bf16[1,128,768]{1,2,0:T(8,128)(2,1)}, bf16[1,128,768]{1,2,0:T(8,128)(2,1)}, u32[]{:S(2)}, u32[]{:S(2)}) collective-permute-start(bf16[1,128,768]{1,2,0:T(8,128)(2,1)} %get-tuple-element.2719), channel_id=1, source_target_pairs={{15,0},{0,1},{1,2},{2,3},{3,4},{4,5},{5,6},{6,7},{7,8},{8,9},{9,10... | collective-permute-start | bytes 589832 | tf_op jit(solution)/shard_map/while/body/eval_jaxpr/ppermute | solution.py:15
  1763.1 46.0 %collective-permute-start.15 = (bf16[1,128,768]{1,2,0:T(8,128)(2,1)}, bf16[1,128,768]{1,2,0:T(8,128)(2,1)}, u32[]{:S(2)}, u32[]{:S(2)}) collective-permute-start(bf16[1,128,768]{1,2,0:T(8,128)(2,1)} %get-tuple-element.2720), channel_id=1, source_target_pairs={{15,0},{0,1},{1,2},{2,3},{3,4},{4,5},{5,6},{6,7},{7,8},{8,9},{9,10... | collective-permute-start | bytes 589832 | tf_op jit(solution)/shard_map/while/body/eval_jaxpr/ppermute | solution.py:15
  1771.9 39.2 %collective-permute-start.14 = (bf16[1,128,768]{1,2,0:T(8,128)(2,1)}, bf16[1,128,768]{1,2,0:T(8,128)(2,1)}, u32[]{:S(2)}, u32[]{:S(2)}) collective-permute-start(bf16[1,128,768]{1,2,0:T(8,128)(2,1)} %get-tuple-element.2719), channel_id=1, source_target_pairs={{15,0},{0,1},{1,2},{2,3},{3,4},{4,5},{5,6},{6,7},{7,8},{8,9},{9,10... | collective-permute-start | bytes 589832 | tf_op jit(solution)/shard_map/while/body/eval_jaxpr/ppermute | solution.py:15
  1812.8 46.0 %collective-permute-start.15 = (bf16[1,128,768]{1,2,0:T(8,128)(2,1)}, bf16[1,128,768]{1,2,0:T(8,128)(2,1)}, u32[]{:S(2)}, u32[]{:S(2)}) collective-permute-start(bf16[1,128,768]{1,2,0:T(8,128)(2,1)} %get-tuple-element.2720), channel_id=1, source_target_pairs={{15,0},{0,1},{1,2},{2,3},{3,4},{4,5},{5,6},{6,7},{7,8},{8,9},{9,10... | collective-permute-start | bytes 589832 | tf_op jit(solution)/shard_map/while/body/eval_jaxpr/ppermute | solution.py:15
  1821.6 39.2 %collective-permute-start.14 = (bf16[1,128,768]{1,2,0:T(8,128)(2,1)}, bf16[1,128,768]{1,2,0:T(8,128)(2,1)}, u32[]{:S(2)}, u32[]{:S(2)}) collective-permute-start(bf16[1,128,768]{1,2,0:T(8,128)(2,1)} %get-tuple-element.2719), channel_id=1, source_target_pairs={{15,0},{0,1},{1,2},{2,3},{3,4},{4,5},{5,6},{6,7},{7,8},{8,9},{9,10... | collective-permute-start | bytes 589832 | tf_op jit(solution)/shard_map/while/body/eval_jaxpr/ppermute | solution.py:15
  1862.5 46.0 %collective-permute-start.15 = (bf16[1,128,768]{1,2,0:T(8,128)(2,1)}, bf16[1,128,768]{1,2,0:T(8,128)(2,1)}, u32[]{:S(2)}, u32[]{:S(2)}) collective-permute-start(bf16[1,128,768]{1,2,0:T(8,128)(2,1)} %get-tuple-element.2720), channel_id=1, source_target_pairs={{15,0},{0,1},{1,2},{2,3},{3,4},{4,5},{5,6},{6,7},{7,8},{8,9},{9,10... | collective-permute-start | bytes 589832 | tf_op jit(solution)/shard_map/while/body/eval_jaxpr/ppermute | solution.py:15
  1871.3 39.2 %collective-permute-start.14 = (bf16[1,128,768]{1,2,0:T(8,128)(2,1)}, bf16[1,128,768]{1,2,0:T(8,128)(2,1)}, u32[]{:S(2)}, u32[]{:S(2)}) collective-permute-start(bf16[1,128,768]{1,2,0:T(8,128)(2,1)} %get-tuple-element.2719), channel_id=1, source_target_pairs={{15,0},{0,1},{1,2},{2,3},{3,4},{4,5},{5,6},{6,7},{7,8},{8,9},{9,10... | collective-permute-start | bytes 589832 | tf_op jit(solution)/shard_map/while/body/eval_jaxpr/ppermute | solution.py:15
  1912.2 46.0 %collective-permute-start.15 = (bf16[1,128,768]{1,2,0:T(8,128)(2,1)}, bf16[1,128,768]{1,2,0:T(8,128)(2,1)}, u32[]{:S(2)}, u32[]{:S(2)}) collective-permute-start(bf16[1,128,768]{1,2,0:T(8,128)(2,1)} %get-tuple-element.2720), channel_id=1, source_target_pairs={{15,0},{0,1},{1,2},{2,3},{3,4},{4,5},{5,6},{6,7},{7,8},{8,9},{9,10... | collective-permute-start | bytes 589832 | tf_op jit(solution)/shard_map/while/body/eval_jaxpr/ppermute | solution.py:15
  1921.1 39.2 %collective-permute-start.14 = (bf16[1,128,768]{1,2,0:T(8,128)(2,1)}, bf16[1,128,768]{1,2,0:T(8,128)(2,1)}, u32[]{:S(2)}, u32[]{:S(2)}) collective-permute-start(bf16[1,128,768]{1,2,0:T(8,128)(2,1)} %get-tuple-element.2719), channel_id=1, source_target_pairs={{15,0},{0,1},{1,2},{2,3},{3,4},{4,5},{5,6},{6,7},{7,8},{8,9},{9,10... | collective-permute-start | bytes 589832 | tf_op jit(solution)/shard_map/while/body/eval_jaxpr/ppermute | solution.py:15
  1962.0 46.0 %collective-permute-start.15 = (bf16[1,128,768]{1,2,0:T(8,128)(2,1)}, bf16[1,128,768]{1,2,0:T(8,128)(2,1)}, u32[]{:S(2)}, u32[]{:S(2)}) collective-permute-start(bf16[1,128,768]{1,2,0:T(8,128)(2,1)} %get-tuple-element.2720), channel_id=1, source_target_pairs={{15,0},{0,1},{1,2},{2,3},{3,4},{4,5},{5,6},{6,7},{7,8},{8,9},{9,10... | collective-permute-start | bytes 589832 | tf_op jit(solution)/shard_map/while/body/eval_jaxpr/ppermute | solution.py:15
  1970.8 39.2 %collective-permute-start.14 = (bf16[1,128,768]{1,2,0:T(8,128)(2,1)}, bf16[1,128,768]{1,2,0:T(8,128)(2,1)}, u32[]{:S(2)}, u32[]{:S(2)}) collective-permute-start(bf16[1,128,768]{1,2,0:T(8,128)(2,1)} %get-tuple-element.2719), channel_id=1, source_target_pairs={{15,0},{0,1},{1,2},{2,3},{3,4},{4,5},{5,6},{6,7},{7,8},{8,9},{9,10... | collective-permute-start | bytes 589832 | tf_op jit(solution)/shard_map/while/body/eval_jaxpr/ppermute | solution.py:15
  2011.7 46.0 %collective-permute-start.15 = (bf16[1,128,768]{1,2,0:T(8,128)(2,1)}, bf16[1,128,768]{1,2,0:T(8,128)(2,1)}, u32[]{:S(2)}, u32[]{:S(2)}) collective-permute-start(bf16[1,128,768]{1,2,0:T(8,128)(2,1)} %get-tuple-element.2720), channel_id=1, source_target_pairs={{15,0},{0,1},{1,2},{2,3},{3,4},{4,5},{5,6},{6,7},{7,8},{8,9},{9,10... | collective-permute-start | bytes 589832 | tf_op jit(solution)/shard_map/while/body/eval_jaxpr/ppermute | solution.py:15
  2020.5 39.2 %collective-permute-start.14 = (bf16[1,128,768]{1,2,0:T(8,128)(2,1)}, bf16[1,128,768]{1,2,0:T(8,128)(2,1)}, u32[]{:S(2)}, u32[]{:S(2)}) collective-permute-start(bf16[1,128,768]{1,2,0:T(8,128)(2,1)} %get-tuple-element.2719), channel_id=1, source_target_pairs={{15,0},{0,1},{1,2},{2,3},{3,4},{4,5},{5,6},{6,7},{7,8},{8,9},{9,10... | collective-permute-start | bytes 589832 | tf_op jit(solution)/shard_map/while/body/eval_jaxpr/ppermute | solution.py:15
  2061.4 46.0 %collective-permute-start.15 = (bf16[1,128,768]{1,2,0:T(8,128)(2,1)}, bf16[1,128,768]{1,2,0:T(8,128)(2,1)}, u32[]{:S(2)}, u32[]{:S(2)}) collective-permute-start(bf16[1,128,768]{1,2,0:T(8,128)(2,1)} %get-tuple-element.2720), channel_id=1, source_target_pairs={{15,0},{0,1},{1,2},{2,3},{3,4},{4,5},{5,6},{6,7},{7,8},{8,9},{9,10... | collective-permute-start | bytes 589832 | tf_op jit(solution)/shard_map/while/body/eval_jaxpr/ppermute | solution.py:15
  2070.3 39.2 %collective-permute-start.14 = (bf16[1,128,768]{1,2,0:T(8,128)(2,1)}, bf16[1,128,768]{1,2,0:T(8,128)(2,1)}, u32[]{:S(2)}, u32[]{:S(2)}) collective-permute-start(bf16[1,128,768]{1,2,0:T(8,128)(2,1)} %get-tuple-element.2719), channel_id=1, source_target_pairs={{15,0},{0,1},{1,2},{2,3},{3,4},{4,5},{5,6},{6,7},{7,8},{8,9},{9,10... | collective-permute-start | bytes 589832 | tf_op jit(solution)/shard_map/while/body/eval_jaxpr/ppermute | solution.py:15
  2111.2 46.0 %collective-permute-start.15 = (bf16[1,128,768]{1,2,0:T(8,128)(2,1)}, bf16[1,128,768]{1,2,0:T(8,128)(2,1)}, u32[]{:S(2)}, u32[]{:S(2)}) collective-permute-start(bf16[1,128,768]{1,2,0:T(8,128)(2,1)} %get-tuple-element.2720), channel_id=1, source_target_pairs={{15,0},{0,1},{1,2},{2,3},{3,4},{4,5},{5,6},{6,7},{7,8},{8,9},{9,10... | collective-permute-start | bytes 589832 | tf_op jit(solution)/shard_map/while/body/eval_jaxpr/ppermute | solution.py:15
  2120.0 39.2 %collective-permute-start.14 = (bf16[1,128,768]{1,2,0:T(8,128)(2,1)}, bf16[1,128,768]{1,2,0:T(8,128)(2,1)}, u32[]{:S(2)}, u32[]{:S(2)}) collective-permute-start(bf16[1,128,768]{1,2,0:T(8,128)(2,1)} %get-tuple-element.2719), channel_id=1, source_target_pairs={{15,0},{0,1},{1,2},{2,3},{3,4},{4,5},{5,6},{6,7},{7,8},{8,9},{9,10... | collective-permute-start | bytes 589832 | tf_op jit(solution)/shard_map/while/body/eval_jaxpr/ppermute | solution.py:15
  2160.9 46.0 %collective-permute-start.15 = (bf16[1,128,768]{1,2,0:T(8,128)(2,1)}, bf16[1,128,768]{1,2,0:T(8,128)(2,1)}, u32[]{:S(2)}, u32[]{:S(2)}) collective-permute-start(bf16[1,128,768]{1,2,0:T(8,128)(2,1)} %get-tuple-element.2720), channel_id=1, source_target_pairs={{15,0},{0,1},{1,2},{2,3},{3,4},{4,5},{5,6},{6,7},{7,8},{8,9},{9,10... | collective-permute-start | bytes 589832 | tf_op jit(solution)/shard_map/while/body/eval_jaxpr/ppermute | solution.py:15
  2169.7 39.2 %collective-permute-start.14 = (bf16[1,128,768]{1,2,0:T(8,128)(2,1)}, bf16[1,128,768]{1,2,0:T(8,128)(2,1)}, u32[]{:S(2)}, u32[]{:S(2)}) collective-permute-start(bf16[1,128,768]{1,2,0:T(8,128)(2,1)} %get-tuple-element.2719), channel_id=1, source_target_pairs={{15,0},{0,1},{1,2},{2,3},{3,4},{4,5},{5,6},{6,7},{7,8},{8,9},{9,10... | collective-permute-start | bytes 589832 | tf_op jit(solution)/shard_map/while/body/eval_jaxpr/ppermute | solution.py:15
  2210.6 46.0 %collective-permute-start.15 = (bf16[1,128,768]{1,2,0:T(8,128)(2,1)}, bf16[1,128,768]{1,2,0:T(8,128)(2,1)}, u32[]{:S(2)}, u32[]{:S(2)}) collective-permute-start(bf16[1,128,768]{1,2,0:T(8,128)(2,1)} %get-tuple-element.2720), channel_id=1, source_target_pairs={{15,0},{0,1},{1,2},{2,3},{3,4},{4,5},{5,6},{6,7},{7,8},{8,9},{9,10... | collective-permute-start | bytes 589832 | tf_op jit(solution)/shard_map/while/body/eval_jaxpr/ppermute | solution.py:15
  2219.5 39.2 %collective-permute-start.14 = (bf16[1,128,768]{1,2,0:T(8,128)(2,1)}, bf16[1,128,768]{1,2,0:T(8,128)(2,1)}, u32[]{:S(2)}, u32[]{:S(2)}) collective-permute-start(bf16[1,128,768]{1,2,0:T(8,128)(2,1)} %get-tuple-element.2719), channel_id=1, source_target_pairs={{15,0},{0,1},{1,2},{2,3},{3,4},{4,5},{5,6},{6,7},{7,8},{8,9},{9,10... | collective-permute-start | bytes 589832 | tf_op jit(solution)/shard_map/while/body/eval_jaxpr/ppermute | solution.py:15
  3237.6 106.8 %collective-permute-start.92 = (f32[8,3072]{1,0:T(8,128)}, f32[8,3072]{1,0:T(8,128)}, u32[]{:S(2)}, u32[]{:S(2)}) collective-permute-start(f32[8,3072]{1,0:T(8,128)} %get-tuple-element.1988), channel_id=1, source_target_pairs={{0,9},{1,10},{2,11},{3,12},{4,13},{5,14},{6,15},{7,16},{8,17},{9,1... | collective-permute-start | bytes 294920
  3239.5 107.7 %collective-permute-start.91 = (f32[8,3072]{1,0:T(8,128)}, f32[8,3072]{1,0:T(8,128)}, u32[]{:S(2)}, u32[]{:S(2)}) collective-permute-start(f32[8,3072]{1,0:T(8,128)} %get-tuple-element.1988), channel_id=1, source_target_pairs={{0,8},{1,9},{2,10},{3,11},{4,12},{5,13},{6,14},{7,15},{8,16},{9,17... | collective-permute-start | bytes 294920
  3242.1 108.1 %collective-permute-start.90 = (f32[8,3072]{1,0:T(8,128)}, f32[8,3072]{1,0:T(8,128)}, u32[]{:S(2)}, u32[]{:S(2)}) collective-permute-start(f32[8,3072]{1,0:T(8,128)} %get-tuple-element.1988), channel_id=1, source_target_pairs={{0,7},{1,8},{2,9},{3,10},{4,11},{5,12},{6,13},{7,14},{8,15},{9,16}... | collective-permute-start | bytes 294920
  3244.8 108.1 %collective-permute-start.89 = (f32[8,3072]{1,0:T(8,128)}, f32[8,3072]{1,0:T(8,128)}, u32[]{:S(2)}, u32[]{:S(2)}) collective-permute-start(f32[8,3072]{1,0:T(8,128)} %get-tuple-element.1988), channel_id=1, source_target_pairs={{0,6},{1,7},{2,8},{3,9},{4,10},{5,11},{6,12},{7,13},{8,14},{9,15},... | collective-permute-start | bytes 294920
  3247.3 107.8 %collective-permute-start.88 = (f32[8,3072]{1,0:T(8,128)}, f32[8,3072]{1,0:T(8,128)}, u32[]{:S(2)}, u32[]{:S(2)}) collective-permute-start(f32[8,3072]{1,0:T(8,128)} %get-tuple-element.1988), channel_id=1, source_target_pairs={{0,5},{1,6},{2,7},{3,8},{4,9},{5,10},{6,11},{7,12},{8,13},{9,14},{... | collective-permute-start | bytes 294920
  3376.5 59.6 %collective-permute-start.140 = (f32[3072,8]{0,1:T(8,128)}, f32[3072,8]{0,1:T(8,128)}, u32[]{:S(2)}, u32[]{:S(2)}) collective-permute-start(f32[3072,8]{0,1:T(8,128)} %get-tuple-element.1989), channel_id=1, source_target_pairs={{0,25},{1,26},{2,27},{3,28},{4,29},{5,30},{6,31},{7,32},{8,33},{9,... | collective-permute-start | bytes 294920
  3378.4 59.6 %collective-permute-start.139 = (f32[3072,8]{0,1:T(8,128)}, f32[3072,8]{0,1:T(8,128)}, u32[]{:S(2)}, u32[]{:S(2)}) collective-permute-start(f32[3072,8]{0,1:T(8,128)} %get-tuple-element.1989), channel_id=1, source_target_pairs={{0,24},{1,25},{2,26},{3,27},{4,28},{5,29},{6,30},{7,31},{8,32},{9,... | collective-permute-start | bytes 294920
  3380.3 60.7 %collective-permute-start.138 = (f32[3072,8]{0,1:T(8,128)}, f32[3072,8]{0,1:T(8,128)}, u32[]{:S(2)}, u32[]{:S(2)}) collective-permute-start(f32[3072,8]{0,1:T(8,128)} %get-tuple-element.1989), channel_id=1, source_target_pairs={{0,23},{1,24},{2,25},{3,26},{4,27},{5,28},{6,29},{7,30},{8,31},{9,... | collective-permute-start | bytes 294920
  3382.3 60.7 %collective-permute-start.137 = (f32[3072,8]{0,1:T(8,128)}, f32[3072,8]{0,1:T(8,128)}, u32[]{:S(2)}, u32[]{:S(2)}) collective-permute-start(f32[3072,8]{0,1:T(8,128)} %get-tuple-element.1989), channel_id=1, source_target_pairs={{0,22},{1,23},{2,24},{3,25},{4,26},{5,27},{6,28},{7,29},{8,30},{9,... | collective-permute-start | bytes 294920
  3385.7 59.2 %collective-permute-start.136 = (f32[3072,8]{0,1:T(8,128)}, f32[3072,8]{0,1:T(8,128)}, u32[]{:S(2)}, u32[]{:S(2)}) collective-permute-start(f32[3072,8]{0,1:T(8,128)} %get-tuple-element.1989), channel_id=1, source_target_pairs={{0,21},{1,22},{2,23},{3,24},{4,25},{5,26},{6,27},{7,28},{8,29},{9,... | collective-permute-start | bytes 294920
  3436.0 62.1 %collective-permute-start.135 = (f32[3072,8]{0,1:T(8,128)}, f32[3072,8]{0,1:T(8,128)}, u32[]{:S(2)}, u32[]{:S(2)}) collective-permute-start(f32[3072,8]{0,1:T(8,128)} %get-tuple-element.1989), channel_id=1, source_target_pairs={{0,20},{1,21},{2,22},{3,23},{4,24},{5,25},{6,26},{7,27},{8,28},{9,... | collective-permute-start | bytes 294920
  3438.0 63.4 %collective-permute-start.134 = (f32[3072,8]{0,1:T(8,128)}, f32[3072,8]{0,1:T(8,128)}, u32[]{:S(2)}, u32[]{:S(2)}) collective-permute-start(f32[3072,8]{0,1:T(8,128)} %get-tuple-element.1989), channel_id=1, source_target_pairs={{0,19},{1,20},{2,21},{3,22},{4,23},{5,24},{6,25},{7,26},{8,27},{9,... | collective-permute-start | bytes 294920
  3441.1 62.2 %collective-permute-start.133 = (f32[3072,8]{0,1:T(8,128)}, f32[3072,8]{0,1:T(8,128)}, u32[]{:S(2)}, u32[]{:S(2)}) collective-permute-start(f32[3072,8]{0,1:T(8,128)} %get-tuple-element.1989), channel_id=1, source_target_pairs={{0,18},{1,19},{2,20},{3,21},{4,22},{5,23},{6,24},{7,25},{8,26},{9,... | collective-permute-start | bytes 294920
  3443.0 62.2 %collective-permute-start.132 = (f32[3072,8]{0,1:T(8,128)}, f32[3072,8]{0,1:T(8,128)}, u32[]{:S(2)}, u32[]{:S(2)}) collective-permute-start(f32[3072,8]{0,1:T(8,128)} %get-tuple-element.1989), channel_id=1, source_target_pairs={{0,17},{1,18},{2,19},{3,20},{4,21},{5,22},{6,23},{7,24},{8,25},{9,... | collective-permute-start | bytes 294920
  3444.9 62.4 %collective-permute-start.131 = (f32[3072,8]{0,1:T(8,128)}, f32[3072,8]{0,1:T(8,128)}, u32[]{:S(2)}, u32[]{:S(2)}) collective-permute-start(f32[3072,8]{0,1:T(8,128)} %get-tuple-element.1989), channel_id=1, source_target_pairs={{0,16},{1,17},{2,18},{3,19},{4,20},{5,21},{6,22},{7,23},{8,24},{9,... | collective-permute-start | bytes 294920
  3498.1 64.5 %collective-permute-start.130 = (f32[3072,8]{0,1:T(8,128)}, f32[3072,8]{0,1:T(8,128)}, u32[]{:S(2)}, u32[]{:S(2)}) collective-permute-start(f32[3072,8]{0,1:T(8,128)} %get-tuple-element.1989), channel_id=1, source_target_pairs={{0,15},{1,16},{2,17},{3,18},{4,19},{5,20},{6,21},{7,22},{8,23},{9,... | collective-permute-start | bytes 294920
  3501.3 63.3 %collective-permute-start.129 = (f32[3072,8]{0,1:T(8,128)}, f32[3072,8]{0,1:T(8,128)}, u32[]{:S(2)}, u32[]{:S(2)}) collective-permute-start(f32[3072,8]{0,1:T(8,128)} %get-tuple-element.1989), channel_id=1, source_target_pairs={{0,14},{1,15},{2,16},{3,17},{4,18},{5,19},{6,20},{7,21},{8,22},{9,... | collective-permute-start | bytes 294920
  3503.3 63.3 %collective-permute-start.128 = (f32[3072,8]{0,1:T(8,128)}, f32[3072,8]{0,1:T(8,128)}, u32[]{:S(2)}, u32[]{:S(2)}) collective-permute-start(f32[3072,8]{0,1:T(8,128)} %get-tuple-element.1989), channel_id=1, source_target_pairs={{0,13},{1,14},{2,15},{3,16},{4,17},{5,18},{6,19},{7,20},{8,21},{9,... | collective-permute-start | bytes 294920
  3505.2 63.5 %collective-permute-start.127 = (f32[3072,8]{0,1:T(8,128)}, f32[3072,8]{0,1:T(8,128)}, u32[]{:S(2)}, u32[]{:S(2)}) collective-permute-start(f32[3072,8]{0,1:T(8,128)} %get-tuple-element.1989), channel_id=1, source_target_pairs={{0,12},{1,13},{2,14},{3,15},{4,16},{5,17},{6,18},{7,19},{8,20},{9,... | collective-permute-start | bytes 294920
  3507.3 64.5 %collective-permute-start.126 = (f32[3072,8]{0,1:T(8,128)}, f32[3072,8]{0,1:T(8,128)}, u32[]{:S(2)}, u32[]{:S(2)}) collective-permute-start(f32[3072,8]{0,1:T(8,128)} %get-tuple-element.1989), channel_id=1, source_target_pairs={{0,11},{1,12},{2,13},{3,14},{4,15},{5,16},{6,17},{7,18},{8,19},{9,... | collective-permute-start | bytes 294920
  3562.7 66.8 %collective-permute-start.125 = (f32[3072,8]{0,1:T(8,128)}, f32[3072,8]{0,1:T(8,128)}, u32[]{:S(2)}, u32[]{:S(2)}) collective-permute-start(f32[3072,8]{0,1:T(8,128)} %get-tuple-element.1989), channel_id=1, source_target_pairs={{0,10},{1,11},{2,12},{3,13},{4,14},{5,15},{6,16},{7,17},{8,18},{9,... | collective-permute-start | bytes 294920
  3564.6 66.8 %collective-permute-start.124 = (f32[3072,8]{0,1:T(8,128)}, f32[3072,8]{0,1:T(8,128)}, u32[]{:S(2)}, u32[]{:S(2)}) collective-permute-start(f32[3072,8]{0,1:T(8,128)} %get-tuple-element.1989), channel_id=1, source_target_pairs={{0,9},{1,10},{2,11},{3,12},{4,13},{5,14},{6,15},{7,16},{8,17},{9,1... | collective-permute-start | bytes 294920
  3566.6 67.4 %collective-permute-start.123 = (f32[3072,8]{0,1:T(8,128)}, f32[3072,8]{0,1:T(8,128)}, u32[]{:S(2)}, u32[]{:S(2)}) collective-permute-start(f32[3072,8]{0,1:T(8,128)} %get-tuple-element.1989), channel_id=1, source_target_pairs={{0,8},{1,9},{2,10},{3,11},{4,12},{5,13},{6,14},{7,15},{8,16},{9,17... | collective-permute-start | bytes 294920
  3568.8 70.1 %collective-permute-start.122 = (f32[3072,8]{0,1:T(8,128)}, f32[3072,8]{0,1:T(8,128)}, u32[]{:S(2)}, u32[]{:S(2)}) collective-permute-start(f32[3072,8]{0,1:T(8,128)} %get-tuple-element.1989), channel_id=1, source_target_pairs={{0,7},{1,8},{2,9},{3,10},{4,11},{5,12},{6,13},{7,14},{8,15},{9,16}... | collective-permute-start | bytes 294920
  3571.9 68.9 %collective-permute-start.121 = (f32[3072,8]{0,1:T(8,128)}, f32[3072,8]{0,1:T(8,128)}, u32[]{:S(2)}, u32[]{:S(2)}) collective-permute-start(f32[3072,8]{0,1:T(8,128)} %get-tuple-element.1989), channel_id=1, source_target_pairs={{0,6},{1,7},{2,8},{3,9},{4,10},{5,11},{6,12},{7,13},{8,14},{9,15},... | collective-permute-start | bytes 294920
  3629.5 71.5 %collective-permute-start.120 = (f32[3072,8]{0,1:T(8,128)}, f32[3072,8]{0,1:T(8,128)}, u32[]{:S(2)}, u32[]{:S(2)}) collective-permute-start(f32[3072,8]{0,1:T(8,128)} %get-tuple-element.1989), channel_id=1, source_target_pairs={{0,5},{1,6},{2,7},{3,8},{4,9},{5,10},{6,11},{7,12},{8,13},{9,14},{... | collective-permute-start | bytes 294920
  3631.4 69.5 %collective-permute-start.119 = (f32[3072,8]{0,1:T(8,128)}, f32[3072,8]{0,1:T(8,128)}, u32[]{:S(2)}, u32[]{:S(2)}) collective-permute-start(f32[3072,8]{0,1:T(8,128)} %get-tuple-element.1989), channel_id=1, source_target_pairs={{0,4},{1,5},{2,6},{3,7},{4,8},{5,9},{6,10},{7,11},{8,12},{9,13},{1... | collective-permute-start | bytes 294920
  3633.9 67.1 %collective-permute-start.118 = (f32[3072,8]{0,1:T(8,128)}, f32[3072,8]{0,1:T(8,128)}, u32[]{:S(2)}, u32[]{:S(2)}) collective-permute-start(f32[3072,8]{0,1:T(8,128)} %get-tuple-element.1989), channel_id=1, source_target_pairs={{0,3},{1,4},{2,5},{3,6},{4,7},{5,8},{6,9},{7,10},{8,11},{9,12},{10... | collective-permute-start | bytes 294920
  3638.9 62.1 %collective-permute-start.117 = (f32[3072,8]{0,1:T(8,128)}, f32[3072,8]{0,1:T(8,128)}, u32[]{:S(2)}, u32[]{:S(2)}) collective-permute-start(f32[3072,8]{0,1:T(8,128)} %get-tuple-element.1989), channel_id=1, source_target_pairs={{0,2},{1,3},{2,4},{3,5},{4,6},{5,7},{6,8},{7,9},{8,10},{9,11},{10,... | collective-permute-start | bytes 294920
  3640.8 60.2 %collective-permute-start.116 = (f32[3072,8]{0,1:T(8,128)}, f32[3072,8]{0,1:T(8,128)}, u32[]{:S(2)}, u32[]{:S(2)}) collective-permute-start(f32[3072,8]{0,1:T(8,128)} %get-tuple-element.1989), channel_id=1, source_target_pairs={{0,1},{1,2},{2,3},{3,4},{4,5},{5,6},{6,7},{7,8},{8,9},{9,10},{10,1... | collective-permute-start | bytes 294920
  (828 other events, 13361.4 us)
Sparse Core Ops, SparseCore 0:
  3190.9 181.0 all-reduce.24
where the time goes:
time: 3830 us; the launch traced here: 3770 us
  starting transfers between devices  1060 us (28%)
  waiting for transfers between devices  736 us (19%)
  local copies, waits for them, and re-layouts  685 us (18%)
  blocking collectives  643 us (17%)
  matrix products  382 us (10%)
  other arithmetic  231 us (6%)
    ppermute x244, waiting for transfers between devices, from_behind(): return lax.ppermute(block, axis, route)  714 us
    unnamed x2, blocking collectives  643 us
    ppermute x244, starting transfers between devices, from_behind(): return lax.ppermute(block, axis, route)  620 us
    unnamed x193, starting transfers between devices  445 us
    unnamed x463, local copies, waits for them, and re-layouts  359 us
    while x690, local copies, waits for them, and re-layouts  285 us
    dot_general x123, matrix products, block_scores(): jnp.einsum('sqhd,skhd->shqk', queries, keys_now, preferred_element_type=j...  163 us
  transfers between devices with their start and end apart: 437, of which 107 were waited for; matrix products, arithmetic and copies ran while one was open for 24% of the time, Pallas kernels for 0%

commit v1 on v0

v1 whole, which is shorter than its diff:
```python
import jax
import jax.numpy as jnp
from jax import lax
from jax.experimental import pallas as pl
from jax.experimental.pallas import tpu as pltpu
from jax.sharding import PartitionSpec as P

MESH = pl.DeviceIdType.MESH
LOG2E = 1.4426950408889634
C2 = 0.125 * LOG2E
SEQ = 2048
QC = 256
KT = 256
NKT = SEQ // KT
MIB = 1 << 20


def dot(a, b):
    return jnp.dot(a, b, preferred_element_type=jnp.float32)


def place():
    b = lax.axis_index("blk")
    r = lax.rem(lax.rem(b, 4) - b // 4 + 7, 4)
    return b, 3 * (b // 4) + r, r < 3


def owner_of(hh):
    y = hh // 3
    return 4 * y + lax.rem(y + lax.rem(hh, 3) + 1, 4)


def greet_group():
    b = lax.axis_index("blk")
    sem = pltpu.get_barrier_semaphore()

    def hello(i, carry):
        pl.semaphore_signal(
            sem, inc=1, device_id={"blk": lax.rem(b + i, 16)}, device_id_type=MESH
        )
        return carry

    lax.fori_loop(1, 16, hello, 0)
    pl.semaphore_wait(sem, 15)


def copy_to(src, dst, send_sem, recv_sem, d):
    return pltpu.make_async_remote_copy(
        src_ref=src,
        dst_ref=dst,
        send_sem=send_sem,
        recv_sem=recv_sem,
        device_id={"blk": d},
        device_id_type=MESH,
    )


def start_to(src, dst, send_sem, recv_sem, d, b):
    @pl.when(d != b)
    def _():
        copy_to(src, dst, send_sem, recv_sem, d).start()

    @pl.when(d == b)
    def _():
        pltpu.make_async_copy(src, dst, recv_sem).start()


def sent_to(src, dst, send_sem, recv_sem, d, b):
    @pl.when(d != b)
    def _():
        copy_to(src, dst, send_sem, recv_sem, d).wait_send()


def got(dst, recv_sem):
    pltpu.make_async_copy(dst, dst, recv_sem).wait()


def lanes(start, size):
    return pl.ds(pl.multiple_of(start, 128), size)


def fold(v):
    return jnp.sum(v.reshape(v.shape[0] // 8, 8, v.shape[1]), axis=0)


def key_ok(length):
    rows = lax.broadcasted_iota(jnp.int32, (KT, QC), 0) + (SEQ - KT)
    return rows < length


def attn_forward(q_at, kn, vt, s_ref, p_ref, length):
    q = q_at
    m8 = jnp.full((8, QC), -3e38, jnp.float32)
    for t in range(NKT):
        s = dot(kn[t * KT : (t + 1) * KT, :], q)
        if t == NKT - 1:
            s = jnp.where(key_ok(length), s, -1e30)
        s_ref[t * KT : (t + 1) * KT, :] = s
        m8 = jnp.maximum(m8, jnp.max(s.reshape(KT // 8, 8, QC), axis=0))
    mc = jnp.max(m8, axis=0, keepdims=True) * C2
    l8 = jnp.zeros((8, QC), jnp.float32)
    for t in range(NKT):
        p = jnp.exp2(s_ref[t * KT : (t + 1) * KT, :] * C2 - mc)
        l8 = l8 + fold(p)
        p_ref[t * KT : (t + 1) * KT, :] = p.astype(jnp.bfloat16)
    total = jnp.sum(l8, axis=0, keepdims=True)
    o = dot(vt, p_ref[...]) / total
    return o, mc + jnp.log2(total)


def attn_backward(
    q, q2, do, lse, lse2, weight, kn, k2n, vn, kt, length, pf, gf, x_ref, acc
):
    d8 = jnp.zeros((8, QC), jnp.float32)
    ok = key_ok(length)
    for t in range(NKT):
        rows = slice(t * KT, (t + 1) * KT)
        p = jnp.exp2(dot(kn[rows, :], q) * C2 - lse)
        p2 = jnp.exp2(dot(k2n[rows, :], q2) * C2 - lse2)
        if t == NKT - 1:
            p = jnp.where(ok, p, 0.0)
            p2 = jnp.where(ok, p2, 0.0)
        g = dot(vn[rows, :], do) + weight * (p - p2)
        d8 = d8 + fold(p * g)
        pf[rows, :] = p
        gf[rows, :] = g
        x_ref[rows, QC:] = p.astype(jnp.bfloat16)
    delta = jnp.sum(d8, axis=0, keepdims=True)
    for t in range(NKT):
        rows = slice(t * KT, (t + 1) * KT)
        x_ref[rows, :QC] = (pf[rows, :] * (gf[rows, :] - delta)).astype(jnp.bfloat16)
    both = jnp.concatenate([q, do], axis=0).astype(jnp.float32).T
    col = lax.broadcasted_iota(jnp.int32, (QC, 128), 1)
    rhs = jnp.concatenate(
        [jnp.where(col < 64, both, 0.0), jnp.where(col < 64, 0.0, both)], axis=0
    ).astype(jnp.bfloat16)
    for t in range(NKT):
        rows = slice(t * KT, (t + 1) * KT)
        acc[rows, :] += dot(x_ref[rows, :], rhs)
    return dot(kt, x_ref[:, :QC]) * 0.125


def natural(x):
    return x.astype(jnp.float32).T.astype(jnp.bfloat16)


def teacher_forward_kernel(
    len_ref, src, buf, dist, att, lse, lse_d,
    o_buf, kn, s_ref, p_ref,
    send1, recv1, send2, recv2, send3, recv3, lse_sem,
):
    b, hh, owner = place()
    greet_group()

    def out1(j, carry):
        h = lax.rem(j + b, 12)
        start_to(src.at[h], buf.at[:, lanes(b * 128, 128)], send1.at[h], recv1.at[b], owner_of(h), b)
        return carry

    lax.fori_loop(0, 12, out1, 0)

    def out2(j, carry):
        h = lax.rem(j + b, 6)
        start_to(
            src.at[h, 0:128], dist.at[:, lanes(b * 128, 128)], send2.at[h], recv2.at[b], owner_of(h + 6), b
        )
        return carry

    lax.fori_loop(0, 6, out2, 0)

    @pl.when(owner)
    def _():
        def arrive(i, carry):
            got(buf.at[:, lanes(i * 128, 128)], recv1.at[i])
            return carry

        lax.fori_loop(0, 16, arrive, 0)
        kn[...] = natural(buf[64:128, :])
        length = len_ref[0]

        def chunk(c, carry):
            here = lanes(c * QC, QC)
            o, stat = attn_forward(buf[0:64, here], kn, buf[128:192, :], s_ref, p_ref, length)
            o_buf[:, here] = o.astype(jnp.bfloat16)
            lse[:, here] = jnp.broadcast_to(stat, (8, QC))
            for i in range(2):
                d = 2 * c + i
                start_to(
                    o_buf.at[:, lanes(d * 128, 128)], att.at[hh], send3.at[d], recv3.at[hh], d, b
                )
            return carry

        lax.fori_loop(0, SEQ // QC, chunk, 0)

        def done3(d, carry):
            sent_to(o_buf.at[:, lanes(d * 128, 128)], att.at[hh], send3.at[d], recv3.at[hh], d, b)
            return carry

        lax.fori_loop(0, 16, done3, 0)

    @pl.when(owner & (hh < 6))
    def _():
        lse_d[:, 0:1024] = lse[:, 0:1024]
        far = copy_to(
            lse.at[:, 1024:2048], lse_d.at[:, 1024:2048], lse_sem.at[0], lse_sem.at[1], owner_of(hh + 6)
        )
        far.start()
        pltpu.make_async_copy(buf.at[0:128], dist, lse_sem.at[2]).start()
        pltpu.make_async_copy(buf.at[0:128], dist, lse_sem.at[2]).wait()
        far.wait_send()

    @pl.when(owner & (hh >= 6))
    def _():
        def arrive(i, carry):
            got(dist.at[:, lanes(i * 128, 128)], recv2.at[i])
            return carry

        lax.fori_loop(0, 16, arrive, 0)
        got(lse_d.at[:, 1024:2048], lse_sem.at[1])

    def back(h, carry):
        got(att.at[h], recv3.at[h])
        return carry

    lax.fori_loop(0, 12, back, 0)

    def done1(h, carry):
        sent_to(src.at[h], buf.at[:, lanes(b * 128, 128)], send1.at[h], recv1.at[b], owner_of(h), b)
        return carry

    lax.fori_loop(0, 12, done1, 0)

    def done2(h, carry):
        sent_to(
            src.at[h, 0:128], dist.at[:, lanes(b * 128, 128)], send2.at[h], recv2.at[b], owner_of(h + 6), b
        )
        return carry

    lax.fori_loop(0, 6, done2, 0)


def student_forward_kernel(
    len_ref, src, buf, att, lse,
    o_buf, kn, s_ref, p_ref,
    send1, recv1, send3, recv3, lse_sem,
):
    b, hh, owner = place()
    half = hh // 6
    head = lax.rem(hh, 6)
    greet_group()

    def out1(j, carry):
        h = lax.rem(j + b, 12)
        start_to(
            src.at[lax.rem(h, 6)], buf.at[:, lanes(b * 128, 128)], send1.at[h], recv1.at[b], owner_of(h), b
        )
        return carry

    lax.fori_loop(0, 12, out1, 0)

    @pl.when(owner)
    def _():
        def arrive(i, carry):
            got(buf.at[:, lanes(i * 128, 128)], recv1.at[i])
            return carry

        lse[:, 0:1024] = jnp.full((8, 1024), 1e30, jnp.float32)
        lax.fori_loop(0, 16, arrive, 0)
        kn[...] = natural(buf[64:128, :])
        length = len_ref[0]

        def chunk(c, carry):
            here = lanes(half * 1024 + c * QC, QC)
            o, stat = attn_forward(buf[0:64, here], kn, buf[128:192, :], s_ref, p_ref, length)
            o_buf[:, lanes(c * QC, QC)] = o.astype(jnp.bfloat16)
            lse[:, here] = jnp.broadcast_to(stat, (8, QC))
            for i in range(2):
                j = 2 * c + i
                d = 8 * half + j
                start_to(
                    o_buf.at[:, lanes(j * 128, 128)], att.at[head], send3.at[j], recv3.at[head], d, b
                )
            return carry

        lax.fori_loop(0, 1024 // QC, chunk, 0)

        def done3(j, carry):
            d = 8 * half + j
            sent_to(o_buf.at[:, lanes(j * 128, 128)], att.at[head], send3.at[j], recv3.at[head], d, b)
            return carry

        lax.fori_loop(0, 8, done3, 0)

    @pl.when(owner & (hh >= 6))
    def _():
        far = copy_to(
            lse.at[:, 1024:2048], lse.at[:, 1024:2048], lse_sem.at[0], lse_sem.at[1], owner_of(hh - 6)
        )
        far.start()
        far.wait_send()

    @pl.when(owner & (hh < 6))
    def _():
        got(lse.at[:, 1024:2048], lse_sem.at[1])

    def back(h, carry):
        got(att.at[h], recv3.at[h])
        return carry

    lax.fori_loop(0, 6, back, 0)

    def done1(h, carry):
        sent_to(
            src.at[lax.rem(h, 6)], buf.at[:, lanes(b * 128, 128)], send1.at[h], recv1.at[b], owner_of(h), b
        )
        return carry

    lax.fori_loop(0, 12, done1, 0)


def weight_row(len_ref, flag_ref, head, first, use):
    q = lax.broadcasted_iota(jnp.int32, (1, QC), 1) + first
    factor = jnp.where(use, flag_ref[head].astype(jnp.float32) * (2.0 * SEQ), 0.0)
    return jnp.where(q < len_ref[0], factor, 0.0)


def student_backward_kernel(
    len_ref, flag_ref, src, buf, dist, lse, lse_d, dq, dkv,
    do_buf, kn, k2n, vn, pf, gf, x_ref, acc, dq_buf, dkv_buf,
    send1, recv1, send2, recv2, send3, recv3,
):
    b, hh, owner = place()
    half = hh // 6
    head = lax.rem(hh, 6)
    greet_group()

    def out1(j, carry):
        h = lax.rem(j + b, 6)
        start_to(
            src.at[h], do_buf.at[:, lanes(lax.rem(b, 8) * 128, 128)],
            send1.at[h], recv1.at[lax.rem(b, 8)], owner_of(h + 6 * (b // 8)), b,
        )
        return carry

    lax.fori_loop(0, 6, out1, 0)

    @pl.when(owner)
    def _():
        kn[...] = natural(buf[64:128, :])
        vn[...] = natural(buf[128:192, :])
        k2n[...] = natural(dist[64:128, :])
        acc[...] = jnp.zeros_like(acc)

        def arrive(i, carry):
            got(do_buf.at[:, lanes(i * 128, 128)], recv1.at[i])
            return carry

        lax.fori_loop(0, 8, arrive, 0)

        def chunk(c, carry):
            first = half * 1024 + c * QC
            here = lanes(first, QC)
            g = attn_backward(
                buf[0:64, here], dist[0:64, here], do_buf[:, lanes(c * QC, QC)],
                lse[0:1, here], lse_d[0:1, here],
                weight_row(len_ref, flag_ref, head, first, True),
                kn, k2n, vn, buf[64:128, :], len_ref[0], pf, gf, x_ref, acc,
            )
            dq_buf[:, lanes(c * QC, QC)] = g.astype(jnp.bfloat16)
            for i in range(2):
                j = 2 * c + i
                start_to(
                    dq_buf.at[:, lanes(j * 128, 128)], dq.at[head], send2.at[j], recv2.at[head], 8 * half + j, b
                )
            return carry

        lax.fori_loop(0, 1024 // QC, chunk, 0)
        row = lax.broadcasted_iota(jnp.int32, (128, SEQ), 0)
        total = acc[...].T
        dkv_buf[...] = jnp.where(row < 64, total * 0.125, total).astype(jnp.bfloat16)

        def out3(i, carry):
            d = lax.rem(b + i, 16)
            start_to(dkv_buf.at[:, lanes(d * 128, 128)], dkv.at[hh], send3.at[d], recv3.at[hh], d, b)
            return carry

        lax.fori_loop(0, 16, out3, 0)

        def done2(j, carry):
            sent_to(
                dq_buf.at[:, lanes(j * 128, 128)], dq.at[head], send2.at[j], recv2.at[head], 8 * half + j, b
            )
            return carry

        lax.fori_loop(0, 8, done2, 0)

        def done3(d, carry):
            sent_to(dkv_buf.at[:, lanes(d * 128, 128)], dkv.at[hh], send3.at[d], recv3.at[hh], d, b)
            return carry

        lax.fori_loop(0, 16, done3, 0)

    def back2(h, carry):
        got(dq.at[h], recv2.at[h])
        return carry

    lax.fori_loop(0, 6, back2, 0)

    def back3(h, carry):
        got(dkv.at[h], recv3.at[h])
        return carry

    lax.fori_loop(0, 12, back3, 0)

    def done1(h, carry):
        sent_to(
            src.at[h], do_buf.at[:, lanes(lax.rem(b, 8) * 128, 128)],
            send1.at[h], recv1.at[lax.rem(b, 8)], owner_of(h + 6 * (b // 8)), b,
        )
        return carry

    lax.fori_loop(0, 6, done1, 0)


def teacher_backward_kernel(
    len_ref, flag_ref, src, buf, other, lse, lse_s, dqkv,
    do_buf, kn, k2n, vn, pf, gf, x_ref, acc, dq_buf, dkv_buf,
    send1, recv1, send2, recv2, send3, recv3,
):
    b, hh, owner = place()
    greet_group()

    def out1(j, carry):
        h = lax.rem(j + b, 12)
        start_to(src.at[h], do_buf.at[:, lanes(b * 128, 128)], send1.at[h], recv1.at[b], owner_of(h), b)
        return carry

    lax.fori_loop(0, 12, out1, 0)

    @pl.when(owner)
    def _():
        kn[...] = natural(buf[64:128, :])
        vn[...] = natural(buf[128:192, :])
        k2n[...] = natural(other[64:128, :])
        acc[...] = jnp.zeros_like(acc)

        def arrive(i, carry):
            got(do_buf.at[:, lanes(i * 128, 128)], recv1.at[i])
            return carry

        lax.fori_loop(0, 16, arrive, 0)

        def chunk(c, carry):
            first = c * QC
            here = lanes(first, QC)
            g = attn_backward(
                buf[0:64, here], other[0:64, here], do_buf[:, here],
                lse[0:1, here], lse_s[0:1, here],
                weight_row(len_ref, flag_ref, lax.rem(hh, 6), first, hh < 6),
                kn, k2n, vn, buf[64:128, :], len_ref[0], pf, gf, x_ref, acc,
            )
            dq_buf[:, here] = g.astype(jnp.bfloat16)
            for i in range(2):
                d = 2 * c + i
                start_to(
                    dq_buf.at[:, lanes(d * 128, 128)], dqkv.at[hh, 0:64], send2.at[d], recv2.at[hh], d, b
                )
            return carry

        lax.fori_loop(0, SEQ // QC, chunk, 0)
        row = lax.broadcasted_iota(jnp.int32, (128, SEQ), 0)
        total = acc[...].T
        dkv_buf[...] = jnp.where(row < 64, total * 0.125, total).astype(jnp.bfloat16)

        def out3(i, carry):
            d = lax.rem(b + i, 16)
            start_to(
                dkv_buf.at[:, lanes(d * 128, 128)], dqkv.at[hh, 64:192], send3.at[d], recv3.at[hh], d, b
            )
            return carry

        lax.fori_loop(0, 16, out3, 0)

        def done2(d, carry):
            sent_to(
                dq_buf.at[:, lanes(d * 128, 128)], dqkv.at[hh, 0:64], send2.at[d], recv2.at[hh], d, b
            )
            return carry

        lax.fori_loop(0, 16, done2, 0)

        def done3(d, carry):
            sent_to(
                dkv_buf.at[:, lanes(d * 128, 128)], dqkv.at[hh, 64:192], send3.at[d], recv3.at[hh], d, b
            )
            return carry

        lax.fori_loop(0, 16, done3, 0)

    def back(h, carry):
        got(dqkv.at[h, 0:64], recv2.at[h])
        got(dqkv.at[h, 64:192], recv3.at[h])
        return carry

    lax.fori_loop(0, 12, back, 0)

    def done1(h, carry):
        sent_to(src.at[h], do_buf.at[:, lanes(b * 128, 128)], send1.at[h], recv1.at[b], owner_of(h), b)
        return carry

    lax.fori_loop(0, 12, done1, 0)


SMEM = pl.BlockSpec(memory_space=pltpu.SMEM)
VMEM = pl.BlockSpec(memory_space=pltpu.VMEM)
DMA = pltpu.SemaphoreType.DMA
BF = jnp.bfloat16
F32 = jnp.float32


def remote_call(kernel, ident, outs, scratch, n_smem, args):
    return pl.pallas_call(
        kernel,
        out_shape=tuple(jax.ShapeDtypeStruct(s, t) for s, t in outs),
        in_specs=[SMEM] * n_smem + [VMEM] * (len(args) - n_smem),
        out_specs=tuple(VMEM for _ in outs),
        scratch_shapes=scratch,
        compiler_params=pltpu.CompilerParams(
            collective_id=ident, has_side_effects=True, vmem_limit_bytes=40 * MIB
        ),
    )(*args)


def attn_teacher_fwd(lengths, src):
    return remote_call(
        teacher_forward_kernel, 1,
        [((192, SEQ), BF), ((128, SEQ), BF), ((12, 64, 128), BF), ((8, SEQ), F32), ((8, SEQ), F32)],
        [
            pltpu.VMEM((64, SEQ), BF), pltpu.VMEM((SEQ, 64), BF),
            pltpu.VMEM((SEQ, QC), F32), pltpu.VMEM((SEQ, QC), BF),
            DMA((12,)), DMA((16,)), DMA((6,)), DMA((16,)), DMA((16,)), DMA((12,)), DMA((3,)),
        ],
        1, (lengths, src),
    )


def attn_student_fwd(lengths, src):
    return remote_call(
        student_forward_kernel, 2,
        [((192, SEQ), BF), ((6, 64, 128), BF), ((8, SEQ), F32)],
        [
            pltpu.VMEM((64, 1024), BF), pltpu.VMEM((SEQ, 64), BF),
            pltpu.VMEM((SEQ, QC), F32), pltpu.VMEM((SEQ, QC), BF),
            DMA((12,)), DMA((16,)), DMA((8,)), DMA((6,)), DMA((2,)),
        ],
        1, (lengths, src),
    )


def backward_scratch(nq, n1, r1, n2, r2):
    return [
        pltpu.VMEM((64, nq), BF),
        pltpu.VMEM((SEQ, 64), BF), pltpu.VMEM((SEQ, 64), BF), pltpu.VMEM((SEQ, 64), BF),
        pltpu.VMEM((SEQ, QC), F32), pltpu.VMEM((SEQ, QC), F32), pltpu.VMEM((SEQ, 2 * QC), BF),
        pltpu.VMEM((SEQ, 128), F32), pltpu.VMEM((64, nq), BF), pltpu.VMEM((128, SEQ), BF),
        DMA((n1,)), DMA((r1,)), DMA((n2,)), DMA((r2,)), DMA((16,)), DMA((12,)),
    ]


def attn_student_bwd(lengths, flags, src, buf, dist, lse, lse_d):
    return remote_call(
        student_backward_kernel, 3,
        [((6, 64, 128), BF), ((12, 128, 128), BF)],
        backward_scratch(1024, 6, 8, 8, 6),
        2, (lengths, flags, src, buf, dist, lse, lse_d),
    )


def attn_teacher_bwd(lengths, flags, src, buf, other, lse, lse_s):
    return remote_call(
        teacher_backward_kernel, 4,
        [((12, 192, 128), BF)],
        backward_scratch(SEQ, 12, 16, 16, 12),
        2, (lengths, flags, src, buf, other, lse, lse_s),
    )[0]


def layer_norm(values, norm_gain, norm_shift):
    center = values - jnp.mean(values, axis=-1, keepdims=True)
    spread = jnp.mean(center * center, axis=-1, keepdims=True)
    return center * lax.rsqrt(spread + 1e-06) * norm_gain + norm_shift


def gelu_exact(values):
    return jax.nn.gelu(values, approximate=False)


def outer_rows(left_side, right_side):
    return lax.dot_general(
        left_side, right_side, (((0,), (0,)), ((), ())), preferred_element_type=jnp.float32
    )


def times_transpose(left_side, right_side):
    return lax.dot_general(
        left_side, right_side, (((1,), (1,)), ((), ())), preferred_element_type=jnp.float32
    )


def qkv_forward(hidden_low, weight, bias_pair, head_span):
    joined = jnp.dot(hidden_low, weight, preferred_element_type=jnp.float32)
    bias = jnp.concatenate(
        [bias_pair[:head_span], jnp.zeros((head_span,), F32), bias_pair[head_span:]]
    )
    return (joined + bias).astype(BF)


def by_heads(flat, heads):
    return flat.reshape(128, -1, heads, 64).transpose(2, 1, 3, 0).reshape(heads, -1, 128)


def from_heads(blocks, parts):
    heads = blocks.shape[0]
    return blocks.reshape(heads, parts, 64, 128).transpose(3, 1, 0, 2).reshape(128, -1)


def dense_forward(residual, attended_low, out_weight, up_weight, down_weight, up_bias, vectors):
    first_sum = residual + (
        jnp.dot(attended_low, out_weight, preferred_element_type=jnp.float32) + vectors[0]
    )
    normed, first_back = jax.vjp(layer_norm, first_sum, vectors[1], vectors[2])
    normed_low = normed.astype(jnp.bfloat16)
    upward = jnp.dot(normed_low, up_weight, preferred_element_type=jnp.float32) + up_bias
    activated, gelu_back = jax.vjp(gelu_exact, upward)
    activated_low = activated.astype(jnp.bfloat16)
    second_sum = normed + (
        jnp.dot(activated_low, down_weight, preferred_element_type=jnp.float32) + vectors[3]
    )
    result, second_back = jax.vjp(layer_norm, second_sum, vectors[4], vectors[5])
    return (result, (attended_low, normed_low, activated_low, first_back, gelu_back, second_back))


def dense_backward(grad_result, kept, out_weight, up_weight, down_weight):
    attended_low, normed_low, activated_low, first_back, gelu_back, second_back = kept
    grad_second, grad_gain_two, grad_shift_two = second_back(grad_result)
    down_low = grad_second.astype(jnp.bfloat16)
    grad_down = outer_rows(down_low, activated_low)
    (grad_upward,) = gelu_back(times_transpose(down_low, down_weight))
    upward_low = grad_upward.astype(jnp.bfloat16)
    grad_up = outer_rows(normed_low, upward_low)
    grad_first, grad_gain_one, grad_shift_one = first_back(
        grad_second + times_transpose(upward_low, up_weight)
    )
    first_low = grad_first.astype(jnp.bfloat16)
    grad_out = outer_rows(first_low, attended_low)
    grad_attended = times_transpose(first_low, out_weight).astype(jnp.bfloat16)
    grad_vectors = jnp.stack(
        [
            jnp.sum(grad_first, axis=0),
            grad_gain_one,
            grad_shift_one,
            jnp.sum(grad_second, axis=0),
            grad_gain_two,
            grad_shift_two,
        ]
    )
    return (
        grad_first,
        grad_attended,
        (grad_out, grad_up, grad_down, jnp.sum(grad_upward, axis=0), grad_vectors),
    )


def qkv_backward(hidden_low, weight, joined):
    span = weight.shape[1] // 3
    low_sums = jnp.sum(joined.astype(jnp.float32), axis=0)
    grad_bias = jnp.concatenate([low_sums[:span], low_sums[2 * span :]])
    return (outer_rows(hidden_low, joined), grad_bias, times_transpose(joined, weight))


def per_device(
    inputs, aug_source, aug_flags, lengths, head_flags, cotangent,
    qkv_teacher, qv_bias_teacher, out_teacher, up_teacher, down_teacher, up_bias_teacher, vectors_teacher,
    qkv_student, qv_bias_student, out_student, up_student, down_student, up_bias_student, vectors_student,
):
    x_in = inputs[0]
    replaced = aug_flags[0] == 1
    chooser = jnp.logical_and(
        aug_source[0][:, None] == jnp.arange(128)[None, :], replaced[:, None]
    )
    taken = jnp.dot(chooser.astype(BF), x_in, preferred_element_type=F32)
    x0 = jnp.where(replaced[:, None], taken, x_in.astype(F32))
    x0_low = x0.astype(BF)
    qkv_t = qkv_forward(x0_low, qkv_teacher, qv_bias_teacher, 768)
    buf_t, dist, att_t, _, lse_d = (res_t := attn_teacher_fwd(lengths, by_heads(qkv_t, 12)))
    lse_t = res_t[3]
    hidden, kept_t = dense_forward(
        x0, from_heads(att_t, 1), out_teacher, up_teacher, down_teacher, up_bias_teacher, vectors_teacher
    )
    hidden_low = hidden.astype(BF)
    qkv_s = qkv_forward(hidden_low, qkv_student, qv_bias_student, 384)
    buf_s, att_s, lse_s = attn_student_fwd(lengths, by_heads(qkv_s, 6))
    output, kept_s = dense_forward(
        hidden, from_heads(att_s, 1), out_student, up_student, down_student, up_bias_student, vectors_student
    )
    grad_hidden, d_att_s, dense_s = dense_backward(
        cotangent[0].astype(F32), kept_s, out_student, up_student, down_student
    )
    dq_s, dkv_s = attn_student_bwd(lengths, head_flags, by_heads(d_att_s, 6), buf_s, dist, lse_s, lse_d)
    dkv_s = (dkv_s[:6].astype(F32) + dkv_s[6:].astype(F32)).astype(BF)
    joined_s = from_heads(jnp.concatenate([dq_s, dkv_s], axis=1), 3)
    g_qkv_s, g_bias_s, more = qkv_backward(hidden_low, qkv_student, joined_s)
    grad_x0, d_att_t, dense_t = dense_backward(
        grad_hidden + more, kept_t, out_teacher, up_teacher, down_teacher
    )
    dqkv_t = attn_teacher_bwd(lengths, head_flags, by_heads(d_att_t, 12), buf_t, buf_s, lse_t, lse_s)
    joined_t = from_heads(dqkv_t, 3)
    g_qkv_t, g_bias_t, more = qkv_backward(x0_low, qkv_teacher, joined_t)
    grad_aug = grad_x0 + more
    copied = lax.dot_general(
        chooser.astype(F32), grad_aug, (((0,), (0,)), ((), ())),
        precision=lax.Precision.HIGHEST, preferred_element_type=F32,
    )
    grad_inputs = jnp.where(replaced[:, None], 0.0, grad_aug) + copied
    small = jnp.concatenate(
        [
            g_bias_t.reshape(768, 2), dense_t[3].reshape(768, 4), dense_t[4].T,
            g_bias_s.reshape(768, 1), dense_s[3].reshape(768, 2), dense_s[4].T,
        ],
        axis=1,
    )
    wide = [g_qkv_t, dense_t[0], dense_t[1], dense_t[2], g_qkv_s, dense_s[0], dense_s[1], dense_s[2], small]
    cuts = [sum(w.shape[1] for w in wide[:i]) for i in range(10)]
    whole = jnp.concatenate([w.astype(BF) for w in wide], axis=1)
    mine = lax.psum_scatter(whole, ("dp", "blk"), scatter_dimension=0, tiled=True).astype(F32)
    parts = [mine[:, cuts[i] : cuts[i + 1]] for i in range(9)]
    tiny = parts[8]
    return (
        output[None], grad_inputs[None],
        parts[0], tiny[:, 0:2].reshape(12), parts[1].T, parts[2], parts[3].T,
        tiny[:, 2:6].reshape(24), tiny[:, 6:12].T,
        parts[4], tiny[:, 12:13].reshape(6), parts[5].T, parts[6], parts[7].T,
        tiny[:, 13:15].reshape(12), tiny[:, 15:21].T,
    )


def solution(mesh):
    both = ("dp", "blk")
    row, flat, col = P(both, None), P(both), P(None, both)
    tokens, marks = P("dp", "blk", None), P("dp", "blk")
    return jax.shard_map(
        per_device,
        mesh=mesh,
        in_specs=(tokens, marks, marks, P("dp"), P(), tokens) + (P(),) * 14,
        out_specs=(tokens, tokens) + (row, flat, col, row, col, flat, col) * 2,
        check_vma=False,
    )
```

time: 3830 us -> 533 us (0.14); the launches traced: 3770 us -> 523 us
  starting transfers between devices: 1060 us -> 0.04 us
  blocking collectives: 643 us -> 0 us
  local copies, waits for them, and re-layouts: 685 us -> 96.1 us
  waiting for transfers between devices: 736 us -> 230 us
  matrix products: 382 us -> 56.6 us
  other arithmetic: 231 us -> 12.4 us
  Pallas kernels: 0 us -> 111 us
    ppermute x244 -> x0, waiting for transfers between devices: 714 us -> none  [from_behind(): return lax.ppermute(block, axis, route)]
    unnamed x2 -> x0, blocking collectives: 643 us -> none
    ppermute x244 -> x0, starting transfers between devices: 620 us -> none  [from_behind(): return lax.ppermute(block, axis, route)]
    unnamed x193 -> x1, starting transfers between devices: 445 us -> 0.04 us
    unnamed x463 -> x214, local copies, waits for them, and re-layouts: 359 us -> 15.2 us
    dot_general x285 -> x2, matrix products: 313 us -> 2.49 us  [the longest x1 1.3 us: per_device(): taken = jnp.dot(chooser.astype(BF), x_in, preferred_element_type=F32)]
    while x694 -> x0, local copies, waits for them, and re-layouts: 291 us -> none
    unnamed x194 -> x2, waiting for transfers between devices: 22.3 us -> 230 us
  transfers between devices with their start and end apart: 437 -> 1, of which waited for: 107 -> 1; matrix products, arithmetic and copies ran while one was open for 24% -> 1% of each run, Pallas kernels for 0% -> 0%
where the time goes in v1:
time: 533 us; the launch traced here: 523 us
  waiting for transfers between devices  230 us (43%)
  Pallas kernels  111 us (21%)
  local copies, waits for them, and re-layouts  96.1 us (18%)
  matrix products  56.6 us (11%)
  between operations  16.2 us (3%)
  other arithmetic  12.4 us (2%)
    unnamed x2, waiting for transfers between devices  230 us
    pallas_call x4, Pallas kernels, remote_call(): pl.pallas_call(kernel, out_shape=tuple((jax.ShapeDtypeStruct(s, t) for s,...  111 us
    concatenate x1, local copies, waits for them, and re-layouts, per_device(): whole = jnp.concatenate([w.astype(BF) for w in wide], axis=1)  32.9 us
    dot_general x8, matrix products, outer_rows(): lax.dot_general(left_side, right_side, (((0,), (0,)), ((), ())), preferre...  19.6 us
    dot_general x8, matrix products, times_transpose(): lax.dot_general(left_side, right_side, (((1,), (1,)), ((), ())), preferre...  16.6 us
    unnamed x214, local copies, waits for them, and re-layouts  15.2 us
    dot_general x2, matrix products, dense_forward(): jnp.dot(normed_low, up_weight, preferred_element_type=jnp.float32) + up_bias  11.4 us
  transfers between devices with their start and end apart: 1, of which 1 were waited for; matrix products, arithmetic and copies ran while one was open for 1% of the time, Pallas kernels for 0%

profile of v1, /device:TPU:5, one launch (start us, length us, event | category | flops | bytes accessed | tf_op | source)
XLA Modules:
  0.0 522.6 jit_solution(18422271252417606337)
XLA Ops:
  8.0 1.5 fusion.62
  11.0 1.3 convolution_select_fusion
  13.0 1.5 fusion
  14.5 2.1 copy.87
  16.6 1.2 copy.88
  17.8 1.8 slice_reduce_fusion.2
  19.6 26.2 %shard_map.315 = (bf16[192,2048]{1,0:T(8,128)(2,1)S(1)}, bf16[128,2048]{1,0:T(8,128)(2,1)S(1)}, bf16[12,64,128]{2,1,0:T(8,128)(2,1)S(1)}, f32[8,2048]{1,0:T(8,128)S(1)}, f32[8,2048]{1,0:T(8,128)S(1)}) custom-call(s32[1]{0:T(128)S(6)} %copy.106.len_ref, bf16[12,192,128]{2,1,0:T(8,128)(2,1)S(1)} %bitcast.103), custom_call_target="tpu_custom_call" | custom-call | tf_op jit(solution)/shard_map/pallas_call | solution.py:522
  46.7 9.3 %multiply_convert_fusion = (bf16[128,3072]{1,0:T(8,128)(2,1)S(1)}, f32[128,3072]{1,0:T(8,128)}, f32[128,3072]{1,0:T(8,128)}) fusion(f32[3072]{0:T(1024)S(1)} %copy-done.98, bf16[768,3072]{1,0:T(8,128)(2,1)} %param.29, f32[128,768]{1,0:T(8,128)S(1)} %get-tuple-element.153, f32[768]{0:T(1024)S(1)} %get-tuple-element.172, f32[768]{0:T(1024)S(1)} %get-tuple-element.171, ...), kind=kOutput, calls=%fused_computation.15 | convolution fusion | flops 630423552 | bytes 9063424 | tf_op jit(solution)/shard_map/dot_general | solution.py:633
  56.1 0.9 fusion.64
  57.9 1.2 fusion.1
  59.1 1.9 copy.89
  60.9 1.1 copy.90
  62.1 26.1 %shard_map.316 = (bf16[192,2048]{1,0:T(8,128)(2,1)S(1)}, bf16[6,64,128]{2,1,0:T(8,128)(2,1)S(1)}, f32[8,2048]{1,0:T(8,128)S(1)}) custom-call(s32[1]{0:T(128)S(6)} %copy.106.len_ref, bf16[6,192,128]{2,1,0:T(8,128)(2,1)S(1)} %bitcast.104), custom_call_target="tpu_custom_call" | custom-call | tf_op jit(solution)/shard_map/pallas_call | solution.py:522
  88.2 1.9 fusion.65
  90.4 2.1 multiply_convert_fusion.1
  94.4 1.0 fusion.55
  95.4 1.6 fusion.68
  97.0 1.5 multiply_reduce_fusion
  98.6 0.9 fusion.54
  100.3 1.0 convolution_convert_fusion.9
  101.2 1.6 copy.91
  102.9 1.1 copy-done.2
  104.0 1.0 copy-done.10
  105.1 0.9 copy-done.13
  107.7 25.4 %shard_map.317 = (bf16[6,64,128]{2,1,0:T(8,128)(2,1)S(1)}, bf16[12,128,128]{2,1,0:T(8,128)(2,1)S(1)}) custom-call(s32[1]{0:T(128)S(6)} %copy.106.len_ref, s32[6]{0:T(128)S(1)} %copy-done.21, bf16[6,64,128]{2,1,0:T(8,128)(2,1)S(1)} %bitcast.110, bf16[192,2048]{1,0:T(8,128)(2,1)S(1)} %copy-done.2, bf16[128,2048]{1,0:T(8,128)(2,1)S(1)} %copy-done.10, ...), custom_call_target="tpu_custom_call" | custom-call | tf_op jit(solution)/shard_map/pallas_call | solution.py:522
  133.3 1.3 multiply_reduce_fusion.1
  135.2 5.2 fusion.67
  140.4 2.4 multiply_reduce_fusion.2
  143.1 1.2 convolution_convert_fusion.8
  144.3 1.5 convolution_convert_fusion.6
  145.8 3.7 convolution_convert_fusion.1
  149.5 3.7 convolution_convert_fusion
  153.3 2.0 convolution_convert_fusion.5
  155.3 1.2 convolution_convert_fusion.7
  156.6 2.3 convolution_convert_fusion.4
  158.9 2.3 convolution_convert_fusion.3
  161.2 1.7 copy.93
  162.9 1.1 copy-done.3
  164.0 0.9 copy-done.4
  165.0 1.1 copy-done.6
  167.8 33.5 %shard_map.318 = bf16[12,192,128]{2,1,0:T(8,128)(2,1)S(1)} custom-call(s32[1]{0:T(128)S(6)} %copy.106.len_ref, s32[6]{0:T(128)S(1)} %copy-done.21, bf16[12,64,128]{2,1,0:T(8,128)(2,1)S(1)} %bitcast.105, bf16[192,2048]{1,0:T(8,128)(2,1)S(1)} %copy-done.6, bf16[192,2048]{1,0:T(8,128)(2,1)S(1)} %copy-done.3, f32[8,2048]{1,0:T(8,128)S(1)} %copy-done.18, ...), custom_call_target="tpu_custom_call" | custom-call | tf_op jit(solution)/shard_map/pallas_call | solution.py:522
  205.5 2.9 convolution_convert_fusion.2
  208.3 2.4 copy.98
  211.3 1.5 slice.154
  212.8 0.9 slice.152
  213.7 1.8 reshape.286
  216.2 1.3 reshape.287
  217.5 1.3 reshape.288
  218.7 1.3 stack.41
  220.0 1.3 reshape.289
  221.2 1.2 reshape.290
  225.8 1.8 reshape.292
  228.3 1.2 reshape.293
  229.5 1.3 reshape.294
  230.8 1.3 stack.44
  232.0 1.3 reshape.295
  233.3 1.0 reduce.5
  236.5 1.7 pad_maximum_fusion.1
  238.1 32.9 %concatenate.29 = bf16[768,13845]{1,0:T(8,128)(2,1)} concatenate(bf16[768,2304]{1,0:T(8,128)(2,1)} %convolution_convert_fusion.2, bf16[768,768]{1,0:T(8,128)(2,1)} %copy.98, bf16[768,3072]{1,0:T(8,128)(2,1)} %convolution_convert_fusion.1, bf16[768,3072]{1,0:T(8,128)(2,1)} %convolution_convert_fusion, bf16[768,1152]{1,0:T(8,128)(2,1)} %convolution_convert_fusion.5, ...), dimensions={1} | concatenate | bytes 42531840 | tf_op jit(solution)/shard_map/concatenate | solution.py:734
  271.7 2.5 convolution_add_fusion.7
  274.2 1.2 fusion.8
  275.4 230.0 %all-reduce.3.cloned.1.call-done = bf16[768,13845]{1,0:T(8,128)(2,1)} async-done(((bf16[768,13845]{1,0:T(8,128)(2,1)}), bf16[768,13845]{1,0:T(8,128)(2,1)}) %all-reduce.3.cloned.1.call-update) | async-done | bytes 21265936
  505.4 1.1 dynamic-slice_convert_fusion
  512.9 1.4 copy.100
  (278 shorter events, 30.9 us)
Async XLA Ops:
  7.2 5.8 %copy-start = (bf16[768,2304]{1,0:T(8,128)(2,1)S(1)}, bf16[768,2304]{1,0:T(8,128)(2,1)}, u32[]{:S(2)}) copy-start(bf16[768,2304]{1,0:T(8,128)(2,1)} %param.26) | copy-start | bytes 10616836
  7.2 498.2 %all-reduce.3.cloned.1.call-start = ((), (), s32[]{:S(2)}) async-start(), calls=%async_computation | async-start | bytes 42860544
  16.6 29.3 %copy-start.38 = (f32[128,768]{1,0:T(8,128)S(1)}, f32[128,768]{1,0:T(8,128)}, u32[]{:S(2)}) copy-start(f32[128,768]{1,0:T(8,128)} %copy-done.37) | copy-start | bytes 1179652
  16.6 29.3 %copy-start.44 = (bf16[768,768]{1,0:T(8,128)(2,1)S(1)}, bf16[768,768]{1,0:T(8,128)(2,1)}, u32[]{:S(2)}) copy-start(bf16[768,768]{1,0:T(8,128)(2,1)} %param.28) | copy-start | bytes 3538948
  19.6 38.2 %copy-start.60 = (f32[768]{0:T(1024)}, f32[768]{0:T(1024)S(1)}, u32[]{:S(2)}) copy-start(f32[768]{0:T(1024)S(1)} %get-tuple-element.169) | copy-start | bytes 9220
  19.6 77.4 %copy-start.58 = (f32[768]{0:T(1024)}, f32[768]{0:T(1024)S(1)}, u32[]{:S(2)}) copy-start(f32[768]{0:T(1024)S(1)} %get-tuple-element.114) | copy-start | bytes 9220
  19.6 27.0 %copy-start.98 = (f32[3072]{0:T(1024)S(1)}, f32[3072]{0:T(1024)}, u32[]{:S(2)}) copy-start(f32[3072]{0:T(1024)} %param.31) | copy-start | bytes 36868
  45.9 10.1 %copy-start.5 = (bf16[192,2048]{1,0:T(8,128)(2,1)}, bf16[192,2048]{1,0:T(8,128)(2,1)S(1)}, u32[]{:S(2)}) copy-start(bf16[192,2048]{1,0:T(8,128)(2,1)S(1)} %get-tuple-element.34.buf) | copy-start | bytes 2359300
  45.9 10.1 %copy-start.7 = (bf16[12,64,128]{2,1,0:T(8,128)(2,1)}, bf16[12,64,128]{2,1,0:T(8,128)(2,1)S(1)}, u32[]{:S(2)}) copy-start(bf16[12,64,128]{2,1,0:T(8,128)(2,1)S(1)} %get-tuple-element.26) | copy-start | bytes 589828
  45.9 10.1 %copy-start.9 = (bf16[128,2048]{1,0:T(8,128)(2,1)}, bf16[128,2048]{1,0:T(8,128)(2,1)S(1)}, u32[]{:S(2)}) copy-start(bf16[128,2048]{1,0:T(8,128)(2,1)S(1)} %get-tuple-element.29.dist) | copy-start | bytes 1572868
  45.9 10.1 %copy-start.17 = (f32[8,2048]{1,0:T(8,128)}, f32[8,2048]{1,0:T(8,128)S(1)}, u32[]{:S(2)}) copy-start(f32[8,2048]{1,0:T(8,128)S(1)} %get-tuple-element.35.lse) | copy-start | bytes 196612
  45.9 10.1 %copy-start.19 = (f32[8,2048]{1,0:T(8,128)}, f32[8,2048]{1,0:T(8,128)S(1)}, u32[]{:S(2)}) copy-start(f32[8,2048]{1,0:T(8,128)S(1)} %get-tuple-element.31.lse_d) | copy-start | bytes 196612
  45.9 10.1 %slice-start = ((s8[4718592]{0:T(1024)(128)(4,1)}), s8[4194304]{0:T(1024)(128)(4,1)S(1)}, s32[]{:S(2)}) async-start(s8[4718592]{0:T(1024)(128)(4,1)} %bitcast.113), calls=%async_computation.1 | async-start | bytes 8388608
  46.4 9.7 %copy-start.24 = (f32[128,768]{1,0:T(8,128)}, f32[128,768]{1,0:T(8,128)S(1)}, u32[]{:S(2)}) copy-start(f32[128,768]{1,0:T(8,128)S(1)} %get-tuple-element.153) | copy-start | bytes 1179652
  46.4 9.6 %copy-start.65 = (f32[128]{0:T(128)}, f32[128]{0:T(128)S(1)}, u32[]{:S(2)}) copy-start(f32[128]{0:T(128)S(1)} %broadcast_multiply_fusion.3) | copy-start | bytes 1540
  46.6 9.4 %copy-start.94 = (f32[128]{0:T(128)}, f32[128]{0:T(128)S(1)}, u32[]{:S(2)}) copy-start(f32[128]{0:T(128)S(1)} %multiply_reduce_fusion.9) | copy-start | bytes 1540
  46.6 9.4 %copy-start.71 = (f32[128]{0:T(128)}, f32[128]{0:T(128)S(1)}, u32[]{:S(2)}) copy-start(f32[128]{0:T(128)S(1)} %fusion.40) | copy-start | bytes 1540
  46.7 9.4 %slice-start.1 = ((s8[4718592]{0:T(1024)(128)(4,1)}), s8[524288]{0:T(1024)(128)(4,1)S(1)}, s32[]{:S(2)}) async-start(s8[4718592]{0:T(1024)(128)(4,1)} %bitcast.113), calls=%async_computation.2 | async-start | bytes 1048576
  60.9 29.5 %copy-start.52 = (bf16[768,1536]{1,0:T(8,128)(2,1)S(1)}, bf16[768,1536]{1,0:T(8,128)(2,1)}, u32[]{:S(2)}) copy-start(bf16[768,1536]{1,0:T(8,128)(2,1)} %param.36) | copy-start | bytes 7077892
  60.9 29.5 %copy-start.62 = (f32[768]{0:T(1024)S(1)}, f32[768]{0:T(1024)}, u32[]{:S(2)}) copy-start(f32[768]{0:T(1024)} %get-tuple-element.113) | copy-start | bytes 9220
  60.9 29.5 %copy-start.99 = (f32[1536]{0:T(1024)S(1)}, f32[1536]{0:T(1024)}, u32[]{:S(2)}) copy-start(f32[1536]{0:T(1024)} %param.38) | copy-start | bytes 18436
  88.2 4.3 copy-start.1
  88.2 4.3 copy-start.11
  88.2 4.3 copy-start.14
  90.1 8.4 %copy-start.26 = (f32[128,768]{1,0:T(8,128)}, f32[128,768]{1,0:T(8,128)S(1)}, u32[]{:S(2)}) copy-start(f32[128,768]{1,0:T(8,128)S(1)} %get-tuple-element.158) | copy-start | bytes 1179652
  90.2 8.4 %copy-start.73 = (f32[128]{0:T(128)}, f32[128]{0:T(128)S(1)}, u32[]{:S(2)}) copy-start(f32[128]{0:T(128)S(1)} %broadcast_multiply_fusion.1) | copy-start | bytes 1540
  90.4 8.2 %copy-start.77 = (f32[128]{0:T(128)}, f32[128]{0:T(128)S(1)}, u32[]{:S(2)}) copy-start(f32[128]{0:T(128)S(1)} %fusion.42) | copy-start | bytes 1540
  97.0 3.3 copy-start.50
  98.6 4.3 copy-start.21
  107.6 25.6 %copy-start.23 = (f32[128,768]{1,0:T(8,128)S(1)}, f32[128,768]{1,0:T(8,128)}, u32[]{:S(2)}) copy-start(f32[128,768]{1,0:T(8,128)} %copy-done.22) | copy-start | bytes 1179652
  107.6 25.6 %copy-start.31 = (f32[128,768]{1,0:T(8,128)S(1)}, f32[128,768]{1,0:T(8,128)}, u32[]{:S(2)}) copy-start(f32[128,768]{1,0:T(8,128)} %copy-done.30) | copy-start | bytes 1179652
  107.6 25.6 %copy-start.36 = (bf16[768,1152]{1,0:T(8,128)(2,1)S(1)}, bf16[768,1152]{1,0:T(8,128)(2,1)}, u32[]{:S(2)}) copy-start(bf16[768,1152]{1,0:T(8,128)(2,1)} %param.33) | copy-start | bytes 5308420
  107.6 25.6 %copy-start.68 = (f32[128]{0:T(128)S(1)}, f32[128]{0:T(128)}, u32[]{:S(2)}) copy-start(f32[128]{0:T(128)} %copy-done.67) | copy-start | bytes 1540
  107.6 25.6 %copy-start.76 = (f32[128]{0:T(128)S(1)}, f32[128]{0:T(128)}, u32[]{:S(2)}) copy-start(f32[128]{0:T(128)} %copy-done.75) | copy-start | bytes 1540
  107.7 25.6 %copy-start.84 = (f32[128]{0:T(128)S(1)}, f32[128]{0:T(128)}, u32[]{:S(2)}) copy-start(f32[128]{0:T(128)} %copy-done.83) | copy-start | bytes 1540
  134.6 5.8 %slice-start.2 = ((s8[4718592]{0:T(1024)(128)(4,1)}), s8[4194304]{0:T(1024)(128)(4,1)S(1)}, s32[]{:S(2)}) async-start(s8[4718592]{0:T(1024)(128)(4,1)} %bitcast.115), calls=%async_computation.3 | async-start | bytes 8388608
  134.8 14.7 %copy-start.33 = (f32[128,768]{1,0:T(8,128)}, f32[128,768]{1,0:T(8,128)S(1)}, u32[]{:S(2)}) copy-start(f32[128,768]{1,0:T(8,128)S(1)} %get-tuple-element.126) | copy-start | bytes 1179652
  134.9 14.7 %copy-start.79 = (f32[128]{0:T(128)}, f32[128]{0:T(128)S(1)}, u32[]{:S(2)}) copy-start(f32[128]{0:T(128)S(1)} %negate_multiply_fusion.3) | copy-start | bytes 1540
  135.2 5.2 copy-start.25
  135.2 5.2 slice-start.3
  135.2 5.2 copy-start.66
  135.2 5.2 copy-start.72
  140.4 2.4 copy-start.95
  140.4 2.7 copy-start.45
  143.1 2.8 copy-start.28
  143.1 2.8 copy-start.86
  145.8 3.7 copy-start.47
  149.5 3.7 copy-start.61
  153.3 3.3 copy-start.27
  153.3 3.3 copy-start.57
  153.3 3.3 copy-start.59
  153.3 3.3 copy-start.63
  153.3 3.2 copy-start.74
  153.3 3.2 copy-start.78
  156.6 2.3 copy-start.41
  167.8 34.1 %copy-start.29 = (f32[128,768]{1,0:T(8,128)S(1)}, f32[128,768]{1,0:T(8,128)}, u32[]{:S(2)}) copy-start(f32[128,768]{1,0:T(8,128)} %copy-done.28) | copy-start | bytes 1179652
  167.8 34.1 %copy-start.87 = (f32[128]{0:T(128)S(1)}, f32[128]{0:T(128)}, u32[]{:S(2)}) copy-start(f32[128]{0:T(128)} %copy-done.86) | copy-start | bytes 1540
  201.3 2.7 copy-start.32
  201.4 2.7 copy-start.85
  201.4 3.4 copy-start.42
  201.4 4.1 copy-start.39
  201.4 4.0 copy-start.43
  271.7 2.5 copy-start.91
  271.7 2.5 copy-start.93
  (43 other events, 55.8 us)
Sparse Core Ops, SparseCore 0:
  271.2 234.1 all-reduce.2

commit v2 on v1

--- a/solution.py
+++ b/solution.py
@@ -584,6 +584,295 @@
         2, (lengths, flags, src, buf, other, lse, lse_s),
     )[0]
 
+CUTS = ((0, 12, 12), (12, 6, 6), (18, 2, 1), (20, 12, 12), (32, 5, 4), (37, 3, 3), (40, 9, 9), (49, 6, 6))
+PARTS = ((0, 20), (20, 20), (40, 16))
+MEMBERS = ((0, 1, 2), (3, 4, 5), (6, 7))
+TILES = 56
+WIDE = TILES * 128
+
+
+def where_am_i():
+    dp, blk = lax.axis_index("dp"), lax.axis_index("blk")
+    return dp // 2, lax.rem(dp, 2), blk // 4, lax.rem(blk, 4)
+
+
+def at_axis(axis, v):
+    x, c, y, z = where_am_i()
+    if axis == "x":
+        return {"dp": 2 * v + c, "blk": 4 * y + z}
+    if axis == "y":
+        return {"dp": 2 * x + c, "blk": 4 * v + z}
+    return {"dp": 2 * x + c, "blk": 4 * y + v}
+
+
+def send_to(src, dst, send_sem, recv_sem, device):
+    return pltpu.make_async_remote_copy(
+        src_ref=src, dst_ref=dst, send_sem=send_sem, recv_sem=recv_sem,
+        device_id=device, device_id_type=MESH,
+    )
+
+
+ORDERS = ("xyz", "yzx", "zxy")
+
+
+def reduce_kernel(*refs):
+    narrow, wide, small = refs[0:8], refs[8:16], refs[16]
+    out = refs[17]
+    (nt, cf, smp, pb, l1, a1, l2, a2, l3, a3,
+     own_sem, n_send, n_recv, c_send, c_recv, s_sem,
+     st_send, st_recv, f_send, f_recv) = refs[18:]
+    x, c, y, z = where_am_i()
+    here = {"x": x, "y": y, "z": z}
+    dp, blk = 2 * x + c, 4 * y + z
+    me = 16 * dp + blk
+    partner = {"dp": 2 * x + 1 - c, "blk": blk}
+
+    def holder(p, q, core):
+        first, second = me // 32, lax.rem(me // 8, 4)
+        at = dict(zip(ORDERS[p], (first, second, q)))
+        return 2 * at["x"] + core, 4 * at["y"] + at["z"]
+
+    def owner(p, k):
+        i = 32 * here[ORDERS[p][0]] + 8 * here[ORDERS[p][1]] + k
+        return i, {"dp": i // 16, "blk": lax.rem(i, 16)}
+
+    barrier = pltpu.get_barrier_semaphore()
+    pl.semaphore_signal(barrier, inc=1, device_id=partner, device_id_type=MESH)
+    for axis in "xyz":
+        for j in range(1, 4):
+            pl.semaphore_signal(
+                barrier, inc=1, device_id=at_axis(axis, lax.rem(here[axis] + j, 4)), device_id_type=MESH
+            )
+    for p in range(3):
+        for q in range(4):
+            for core in range(2):
+                hd, hb = holder(p, q, core)
+
+                pl.semaphore_signal(
+                    barrier, inc=1, device_id={"dp": hd, "blk": hb}, device_id_type=MESH
+                )
+    pl.semaphore_wait(barrier, 34)
+
+    small_copy = send_to(small, smp, s_sem.at[0], s_sem.at[1], partner)
+    small_copy.start()
+    n_copies, c_copies, own_copies = [], [], []
+    for m, (first, count, step) in enumerate(CUTS):
+        cols = slice(first * 128, (first + count) * 128)
+        keep = pltpu.make_async_copy(
+            wide[m].at[:, lanes(c * step * 128, count * 128)], cf.at[0:128, cols], own_sem.at[m]
+        )
+        keep.start()
+        own_copies.append(keep)
+        give = send_to(
+            wide[m].at[:, lanes((1 - c) * step * 128, count * 128)], cf.at[128:256, cols],
+            c_send.at[m], c_recv.at[m], partner,
+        )
+        give.start()
+        c_copies.append(give)
+        nt[m, :, 0:128] = narrow[m][...].T
+        give = send_to(
+            nt.at[m, :, 0:128], nt.at[m, :, 128:256], n_send.at[m], n_recv.at[m], partner
+        )
+        give.start()
+        n_copies.append(give)
+
+    def part_cols(p):
+        return slice(PARTS[p][0] * 128, (PARTS[p][0] + PARTS[p][1]) * 128)
+
+    def stage_copies(p, stage):
+        axis = ORDERS[p][stage]
+        copies = []
+        for j in range(1, 4):
+            v = lax.rem(here[axis] + j, 4)
+            if stage == 0:
+                src = pb.at[pl.ds(pl.multiple_of(192 * v, 16), 192), part_cols(p)]
+                dst = l1.at[j - 1, :, part_cols(p)]
+            elif stage == 1:
+                src = a1.at[pl.ds(pl.multiple_of(48 * v, 16), 48), part_cols(p)]
+                dst = l2.at[j - 1, :, part_cols(p)]
+            else:
+                q = PARTS[p][1] * 32
+                src = a2.at[:, lanes(PARTS[p][0] * 128 + v * q, q)]
+                dst = l3.at[j - 1, :, slice(PARTS[p][0] * 32, PARTS[p][0] * 32 + q)]
+            n = 9 * stage + 3 * p + j - 1
+            copies.append(send_to(src, dst, st_send.at[n], st_recv.at[n], at_axis(axis, v)))
+        return copies
+
+    copies = {}
+    for p in range(3):
+        for m in MEMBERS[p]:
+            first, count, _ = CUTS[m]
+            own_copies[m].wait()
+            c_copies[m].wait_recv()
+            n_copies[m].wait_recv()
+            size = 3 if count % 3 == 0 else count
+
+            def piece(i, carry, m=m, first=first, size=size):
+                cols = lanes((first + i * size) * 128, size * 128)
+                pb[:, cols] = dot(nt[m], cf[:, cols]).astype(BF)
+                return carry
+
+            lax.fori_loop(0, count // size, piece, 0)
+        if p == 2:
+            small_copy.wait_recv()
+            pb[:, (TILES - 1) * 128 :] = (small[...].astype(F32) + smp[...].astype(F32)).astype(BF)
+        copies[p, 0] = stage_copies(p, 0)
+        for copy in copies[p, 0]:
+            copy.start()
+
+    for p in range(3):
+        cols = part_cols(p)
+        base = 192 * here[ORDERS[p][0]]
+        for copy in copies[p, 0]:
+            copy.wait_recv()
+
+        def add1(r, carry, cols=cols, base=base):
+            rows = pl.ds(pl.multiple_of(16 * r, 16), 16)
+            own = pl.ds(pl.multiple_of(base + 16 * r, 16), 16)
+            total = pb[own, cols].astype(F32)
+            for j in range(3):
+                total = total + l1[j, rows, cols].astype(F32)
+            a1[rows, cols] = total.astype(BF)
+            return carry
+
+        lax.fori_loop(0, 12, add1, 0)
+        copies[p, 1] = stage_copies(p, 1)
+        for copy in copies[p, 1]:
+            copy.start()
+
+    for p in range(3):
+        cols = part_cols(p)
+        base = 48 * here[ORDERS[p][1]]
+        for copy in copies[p, 1]:
+            copy.wait_recv()
+
+        def add2(r, carry, cols=cols, base=base):
+            rows = pl.ds(pl.multiple_of(16 * r, 16), 16)
+            own = pl.ds(pl.multiple_of(base + 16 * r, 16), 16)
+            total = a1[own, cols].astype(F32)
+            for j in range(3):
+                total = total + l2[j, rows, cols].astype(F32)
+            a2[rows, cols] = total.astype(BF)
+            return carry
+
+        lax.fori_loop(0, 3, add2, 0)
+        copies[p, 2] = stage_copies(p, 2)
+        for copy in copies[p, 2]:
+            copy.start()
+
+    for p in range(3):
+        q = PARTS[p][1] * 32
+        off = PARTS[p][0] * 32
+        third = here[ORDERS[p][2]]
+        for copy in copies[p, 2]:
+            copy.wait_recv()
+        total = a2[:, lanes(PARTS[p][0] * 128 + third * q, q)].astype(F32)
+        for j in range(3):
+            total = total + l3[j, :, off : off + q].astype(F32)
+        for k in range(8):
+            a3[k, 0:6, off : off + q] = total[6 * k : 6 * k + 6, :]
+
+    def final(p, k):
+        q = PARTS[p][1] * 32
+        off = PARTS[p][0] * 32
+        third = here[ORDERS[p][2]]
+        i, device = owner(p, k)
+        src = a3.at[k, :, slice(off, off + q)]
+        dst = out.at[:, lanes((c * TILES + PARTS[p][0]) * 128 + third * q, q)]
+        slot = f_recv.at[(c * 3 + p) * 4 + third]
+        return i, src, dst, slot, send_to(src, dst, f_send.at[8 * p + k], slot, device)
+
+    for p in range(3):
+        for k in range(8):
+            i, src, dst, slot, copy = final(p, k)
+
+            @pl.when(i != me)
+            def _():
+                copy.start()
+
+            @pl.when(i == me)
+            def _():
+                pltpu.make_async_copy(src, dst, slot).start()
+
+    for core in range(2):
+        for p in range(3):
+            q = PARTS[p][1] * 32
+            for third in range(4):
+                start = (core * TILES + PARTS[p][0]) * 128 + third * q
+                got(out.at[:, start : start + q], f_recv.at[(core * 3 + p) * 4 + third])
+    for p in range(3):
+        for k in range(8):
+            i, src, dst, slot, copy = final(p, k)
+
+            @pl.when(i != me)
+            def _():
+                copy.wait_send()
+    small_copy.wait_send()
+    for copy in n_copies + c_copies + sum(copies.values(), []):
+        copy.wait_send()
+
+
+def reduce_all(narrow, wide, small):
+    return pl.pallas_call(
+        reduce_kernel,
+        out_shape=jax.ShapeDtypeStruct((8, 2 * WIDE), F32),
+        in_specs=[VMEM] * 17,
+        out_specs=VMEM,
+        scratch_shapes=[
+            pltpu.VMEM((8, 768, 256), BF), pltpu.VMEM((256, WIDE), BF), pltpu.VMEM((768, 128), BF),
+            pltpu.VMEM((768, WIDE), BF), pltpu.VMEM((3, 192, WIDE), BF), pltpu.VMEM((192, WIDE), BF),
+            pltpu.VMEM((3, 48, WIDE), BF), pltpu.VMEM((48, WIDE), BF),
+            pltpu.VMEM((3, 48, WIDE // 4), BF), pltpu.VMEM((8, 8, WIDE // 4), F32),
+            DMA((8,)), DMA((8,)), DMA((8,)), DMA((8,)), DMA((8,)), DMA((2,)),
+            DMA((27,)), DMA((27,)), DMA((24,)), DMA((24,)),
+        ],
+        compiler_params=pltpu.CompilerParams(
+            collective_id=5, has_side_effects=True, vmem_limit_bytes=56 * MIB
+        ),
+    )(*narrow, *wide, small)
+
+
+def unpack_kernel(whole, *outs):
+    def columns(m):
+        first, count, step = CUTS[m]
+        both = [whole[:, first * 128 : (first + count) * 128]]
+        skip = count - step
+        start = TILES + first + skip
+        both.append(whole[:, start * 128 : (start + count - skip) * 128])
+        return jnp.concatenate(both, axis=1)
+
+    for m, o in ((6, 0), (0, 3), (4, 7), (1, 10)):
+        outs[o][...] = columns(m)[0:6]
+    for m, o in ((5, 2), (3, 4), (2, 9), (7, 11)):
+        outs[o][...] = columns(m).T[:, 0:6]
+    tiny = whole[:, (TILES - 1) * 128 : TILES * 128]
+    outs[1][...] = tiny[0:6, 0:2]
+    outs[5][...] = tiny[0:6, 2:6]
+    outs[8][...] = tiny[0:6, 12:13]
+    outs[12][...] = tiny[0:6, 13:15]
+    turned = tiny.T
+    outs[6][...] = turned[6:12, 0:6]
+    outs[13][...] = turned[15:21, 0:6]
+
+
+def unpack(whole):
+    shapes = (
+        (6, 2304), (6, 2), (768, 6), (6, 3072), (3072, 6), (6, 4), (6, 6),
+        (6, 1152), (6, 1), (384, 6), (6, 1536), (1536, 6), (6, 2), (6, 6),
+    )
+    outs = list(
+        pl.pallas_call(
+            unpack_kernel,
+            out_shape=tuple(jax.ShapeDtypeStruct(s, F32) for s in shapes),
+            in_specs=[VMEM],
+            out_specs=tuple(VMEM for _ in shapes),
+            compiler_params=pltpu.CompilerParams(vmem_limit_bytes=40 * MIB),
+        )(whole)
+    )
+    for i in (1, 5, 8, 12):
+        outs[i] = outs[i].reshape(-1)
+    return tuple(outs)
+
 
 def layer_norm(values, norm_gain, norm_shift):
     center = values - jnp.mean(values, axis=-1, keepdims=True)
@@ -644,15 +933,12 @@
     attended_low, normed_low, activated_low, first_back, gelu_back, second_back = kept
     grad_second, grad_gain_two, grad_shift_two = second_back(grad_result)
     down_low = grad_second.astype(jnp.bfloat16)
-    grad_down = outer_rows(down_low, activated_low)
     (grad_upward,) = gelu_back(times_transpose(down_low, down_weight))
     upward_low = grad_upward.astype(jnp.bfloat16)
-    grad_up = outer_rows(normed_low, upward_low)
     grad_first, grad_gain_one, grad_shift_one = first_back(
         grad_second + times_transpose(upward_low, up_weight)
     )
     first_low = grad_first.astype(jnp.bfloat16)
-    grad_out = outer_rows(first_low, attended_low)
     grad_attended = times_transpose(first_low, out_weight).astype(jnp.bfloat16)
     grad_vectors = jnp.stack(
         [
@@ -667,7 +953,7 @@
     return (
         grad_first,
         grad_attended,
-        (grad_out, grad_up, grad_down, jnp.sum(grad_upward, axis=0), grad_vectors),
+        ((first_low, attended_low), (normed_low, upward_low), (down_low, activated_low), jnp.sum(grad_upward, axis=0), grad_vectors),
     )
 
 
@@ -675,7 +961,7 @@
     span = weight.shape[1] // 3
     low_sums = jnp.sum(joined.astype(jnp.float32), axis=0)
     grad_bias = jnp.concatenate([low_sums[:span], low_sums[2 * span :]])
-    return (outer_rows(hidden_low, joined), grad_bias, times_transpose(joined, weight))
+    return ((hidden_low, joined), grad_bias, times_transpose(joined, weight))
 
 
 def per_device(
@@ -729,19 +1015,10 @@
         ],
         axis=1,
     )
-    wide = [g_qkv_t, dense_t[0], dense_t[1], dense_t[2], g_qkv_s, dense_s[0], dense_s[1], dense_s[2], small]
-    cuts = [sum(w.shape[1] for w in wide[:i]) for i in range(10)]
-    whole = jnp.concatenate([w.astype(BF) for w in wide], axis=1)
-    mine = lax.psum_scatter(whole, ("dp", "blk"), scatter_dimension=0, tiled=True).astype(F32)
-    parts = [mine[:, cuts[i] : cuts[i + 1]] for i in range(9)]
-    tiny = parts[8]
-    return (
-        output[None], grad_inputs[None],
-        parts[0], tiny[:, 0:2].reshape(12), parts[1].T, parts[2], parts[3].T,
-        tiny[:, 2:6].reshape(24), tiny[:, 6:12].T,
-        parts[4], tiny[:, 12:13].reshape(6), parts[5].T, parts[6], parts[7].T,
-        tiny[:, 13:15].reshape(12), tiny[:, 15:21].T,
-    )
+    small = jnp.pad(small, ((0, 0), (0, 107))).astype(BF)
+    pairs = (dense_t[1], dense_s[1], dense_s[0], dense_t[2], g_qkv_s, dense_t[0], g_qkv_t, dense_s[2])
+    whole = reduce_all([n for n, _ in pairs], [w for _, w in pairs], small)
+    return (output[None], grad_inputs[None]) + unpack(whole)
 
 
 def solution(mesh):

time: 533 us -> 343 us (0.64); the launches traced: 523 us -> 342 us
  waiting for transfers between devices: 230 us -> 0 us
  Pallas kernels: 111 us -> 217 us
  matrix products: 56.6 us -> 34.3 us
  local copies, waits for them, and re-layouts: 96.1 us -> 75.7 us
  between operations: 16.2 us -> 2.3 us
    unnamed x2 -> x0, waiting for transfers between devices: 230 us -> none
    pallas_call x0 -> x2, Pallas kernels: none -> 106 us  [the longest x1 104 us: reduce_all(): pl.pallas_call(reduce_kernel, out_shape=jax.ShapeDtypeStruct((8, 2 * WIDE...]
    concatenate x1, local copies, waits for them, and re-layouts: 32.9 us -> 2.24 us  [per_device(): jnp.concatenate([g_bias_t.reshape(768, 2), dense_t[3].reshape(768, 4), de...]
    dot_general x8 -> x0, matrix products: 19.6 us -> none  [outer_rows(): lax.dot_general(left_side, right_side, (((0,), (0,)), ((), ())), preferre...]
    unnamed x214 -> x180, local copies, waits for them, and re-layouts: 15.2 us -> 28.2 us
    reshape x2 -> x6, local copies, waits for them, and re-layouts: 0.06 us -> 7.4 us  [from_heads(): blocks.reshape(heads, parts, 64, 128).transpose(3, 1, 0, 2).reshape(128, -1)]
  transfers between devices with their start and end apart: 1 -> 0, of which waited for: 1 -> 0; matrix products, arithmetic and copies ran while one was open for 1% -> 0% of each run, Pallas kernels for 0% -> 0%
where the time goes in v2:
time: 343 us; the launch traced here: 342 us
  Pallas kernels  217 us (63%)
  local copies, waits for them, and re-layouts  75.7 us (22%)
  matrix products  34.3 us (10%)
  other arithmetic  12.5 us (4%)
    pallas_call x4, Pallas kernels, remote_call(): pl.pallas_call(kernel, out_shape=tuple((jax.ShapeDtypeStruct(s, t) for s,...  111 us
    pallas_call x1, Pallas kernels, reduce_all(): pl.pallas_call(reduce_kernel, out_shape=jax.ShapeDtypeStruct((8, 2 * WIDE...  104 us
    unnamed x180, local copies, waits for them, and re-layouts  28.2 us
    dot_general x8, matrix products, times_transpose(): lax.dot_general(left_side, right_side, (((1,), (1,)), ((), ())), preferre...  15.2 us
    reshape x8, local copies, waits for them, and re-layouts, layer_norm(): return center * lax.rsqrt(spread + 1e-06) * norm_gain + norm_shift  9.39 us
    dot_general x2, matrix products, dense_forward(): jnp.dot(normed_low, up_weight, preferred_element_type=jnp.float32) + up_bias  7.43 us
    reshape x6, local copies, waits for them, and re-layouts, from_heads(): blocks.reshape(heads, parts, 64, 128).transpose(3, 1, 0, 2).reshape(128, -1)  7.4 us

profile of v2, /device:TPU:5, one launch (start us, length us, event | category | flops | bytes accessed | tf_op | source)
XLA Modules:
  0.0 341.5 jit_solution(10451420200080239377)
XLA Ops:
  0.7 1.8 slice_reduce_fusion.1
  3.8 2.0 fusion.50
  6.7 1.5 fusion
  8.1 2.1 copy.120
  10.2 1.3 copy.121
  11.5 26.4 %shard_map.315 = (bf16[192,2048]{1,0:T(8,128)(2,1)S(1)}, bf16[128,2048]{1,0:T(8,128)(2,1)S(1)}, bf16[12,64,128]{2,1,0:T(8,128)(2,1)S(1)}, f32[8,2048]{1,0:T(8,128)S(1)}, f32[8,2048]{1,0:T(8,128)S(1)}) custom-call(s32[1]{0:T(128)S(6)} %copy.141.len_ref, bf16[12,192,128]{2,1,0:T(8,128)(2,1)S(1)} %bitcast.93), custom_call_target="tpu_custom_call" | custom-call | tf_op jit(solution)/shard_map/pallas_call | solution.py:522
  38.0 2.3 fusion.51
  41.3 5.3 %multiply_convert_fusion = (bf16[128,3072]{1,0:T(8,128)(2,1)S(1)}, f32[128,3072]{1,0:T(8,128)}, f32[128,3072]{1,0:T(8,128)}) fusion(f32[3072]{0:T(1024)S(1)} %copy-done.80, bf16[128,768]{1,0:T(8,128)(2,1)S(1)} %fusion.23.refs_0_, bf16[768,3072]{1,0:T(8,128)(2,1)S(1)} %copy-done.33), kind=kOutput, calls=%fused_computation.9 | convolution fusion | flops 629932032 | bytes 8859648 | tf_op jit(solution)/shard_map/dot_general | solution.py:922
  46.7 0.9 fusion.52
  49.2 1.2 fusion.1
  50.4 1.8 copy.122
  52.2 1.1 copy.123
  53.4 26.1 %shard_map.316 = (bf16[192,2048]{1,0:T(8,128)(2,1)S(1)}, bf16[6,64,128]{2,1,0:T(8,128)(2,1)S(1)}, f32[8,2048]{1,0:T(8,128)S(1)}) custom-call(s32[1]{0:T(128)S(6)} %copy.141.len_ref, bf16[6,192,128]{2,1,0:T(8,128)(2,1)S(1)} %bitcast.94), custom_call_target="tpu_custom_call" | custom-call | tf_op jit(solution)/shard_map/pallas_call | solution.py:522
  79.5 1.9 fusion.53
  81.9 2.2 multiply_convert_fusion.1
  86.0 1.0 fusion.43
  87.6 1.6 fusion.38
  89.3 1.5 multiply_reduce_fusion
  93.2 1.0 convolution_convert_fusion.1
  94.2 1.6 copy.124
  95.8 1.1 copy-done.3
  96.9 1.0 copy-done.13
  98.0 0.9 copy-done.16
  100.6 25.4 %shard_map.317 = (bf16[6,64,128]{2,1,0:T(8,128)(2,1)S(1)}, bf16[12,128,128]{2,1,0:T(8,128)(2,1)S(1)}) custom-call(s32[1]{0:T(128)S(6)} %copy.141.len_ref, s32[6]{0:T(128)S(1)} %copy-done.25, bf16[6,64,128]{2,1,0:T(8,128)(2,1)S(1)} %bitcast.100, bf16[192,2048]{1,0:T(8,128)(2,1)S(1)} %copy-done.3, bf16[128,2048]{1,0:T(8,128)(2,1)S(1)} %copy-done.13, ...), custom_call_target="tpu_custom_call" | custom-call | tf_op jit(solution)/shard_map/pallas_call | solution.py:522
  126.2 1.3 multiply_reduce_fusion.1
  127.9 1.1 copy-done.82
  129.0 4.9 %fusion.39 = (bf16[3072]{0:T(1024)(128)(2,1)}, bf16[128,3072]{1,0:T(8,128)(2,1)S(1)}) fusion(f32[128,3072]{1,0:T(8,128)S(1)} %copy-done.82, f32[128,3072]{1,0:T(8,128)S(1)} %copy-done.83, bf16[128,768]{1,0:T(8,128)(2,1)S(1)} %get-tuple-element.189.refs_3_, bf16[3072,768]{1,0:T(8,128)(2,1)} %param.30), kind=kOutput, calls=%fused_computation.141 | convolution fusion | flops 609874944 | bytes 8853504 | tf_op jit(solution)/shard_map/dot_general | solution.py:894
  134.0 2.4 multiply_reduce_fusion.2
  138.8 1.2 convolution_convert_fusion
  140.0 1.7 copy.126
  141.7 1.1 copy-done.4
  142.9 0.9 copy-done.8
  143.8 1.1 copy-done.11
  146.6 33.1 %shard_map.318 = bf16[12,192,128]{2,1,0:T(8,128)(2,1)S(1)} custom-call(s32[1]{0:T(128)S(6)} %copy.141.len_ref, s32[6]{0:T(128)S(1)} %copy-done.25, bf16[12,64,128]{2,1,0:T(8,128)(2,1)S(1)} %bitcast.97, bf16[192,2048]{1,0:T(8,128)(2,1)S(1)} %copy-done.11, bf16[192,2048]{1,0:T(8,128)(2,1)S(1)} %copy-done.4, f32[8,2048]{1,0:T(8,128)S(1)} %copy-done.22, ...), custom_call_target="tpu_custom_call" | custom-call | tf_op jit(solution)/shard_map/pallas_call | solution.py:522
  179.8 1.3 convolution_add_fusion.7
  181.2 1.2 fusion.8
  182.4 1.6 copy.131.refs_10_
  184.0 1.8 copy.132.refs_12_
  185.9 1.7 copy.133.refs_13_
  187.6 2.1 copy.134.refs_14_
  189.7 1.4 bitcast_reduce_fusion
  192.9 1.6 pad_maximum_fusion.1
  194.6 1.8 reshape.286
  197.1 1.3 reshape.287
  198.3 1.3 reshape.288
  200.2 1.3 reshape.289
  201.4 1.2 reshape.290
  204.3 1.2 bitcast_reduce_fusion.1
  206.5 1.8 reshape.292
  209.0 1.3 reshape.293
  210.2 1.3 reshape.294
  211.5 1.3 stack.44
  212.7 1.3 reshape.295
  214.0 1.0 reduce.5
  217.2 2.2 concatenate.27
  219.4 1.6 pad.5.refs_16_
  221.1 104.2 %shard_map.319.whole = f32[8,14336]{1,0:T(8,128)} custom-call(bf16[128,768]{1,0:T(8,128)(2,1)} %copy-done.53, bf16[128,768]{1,0:T(8,128)(2,1)} %copy-done.54, bf16[128,768]{1,0:T(8,128)(2,1)} %copy-done.48, bf16[128,768]{1,0:T(8,128)(2,1)} %copy-done.56, bf16[128,768]{1,0:T(8,128)(2,1)} %copy-done.47, bf16[128,768]{1,0:T(8,128)(2,1)} %copy-done.49, ...), custom_call_target="tpu_custom_call" | custom-call | tf_op jit(solution)/shard_map/pallas_call | solution.py:816
  325.3 1.0 copy-done.5
  326.3 1.5 shard_map.320
  327.7 1.2 copy-done.6
  331.8 1.8 copy.135
  333.5 2.5 copy.136
  337.3 1.6 copy.137
  338.9 2.0 copy.138
  (232 shorter events, 28.8 us)
Async XLA Ops:
  0.6 6.0 %copy-start = (bf16[768,2304]{1,0:T(8,128)(2,1)S(1)}, bf16[768,2304]{1,0:T(8,128)(2,1)}, u32[]{:S(2)}) copy-start(bf16[768,2304]{1,0:T(8,128)(2,1)} %param.26) | copy-start | bytes 10616836
  3.8 2.8 copy-start.74
  10.2 27.7 %copy-start.63 = (f32[768]{0:T(1024)S(1)}, f32[768]{0:T(1024)}, u32[]{:S(2)}) copy-start(f32[768]{0:T(1024)} %get-tuple-element.216) | copy-start | bytes 9220
  10.2 30.8 %copy-start.59 = (f32[768]{0:T(1024)S(1)}, f32[768]{0:T(1024)}, u32[]{:S(2)}) copy-start(f32[768]{0:T(1024)} %get-tuple-element.218) | copy-start | bytes 9220
  10.2 31.0 %copy-start.33 = (bf16[768,3072]{1,0:T(8,128)(2,1)S(1)}, bf16[768,3072]{1,0:T(8,128)(2,1)}, u32[]{:S(2)}) copy-start(bf16[768,3072]{1,0:T(8,128)(2,1)} %param.29) | copy-start | bytes 14155780
  37.9 3.3 copy-start.7
  37.9 3.3 copy-start.10
  37.9 3.3 copy-start.12
  37.9 3.3 copy-start.21
  37.9 3.3 copy-start.23
  37.9 3.3 copy-start.80
  40.3 6.3 %copy-start.26 = (f32[128,768]{1,0:T(8,128)}, f32[128,768]{1,0:T(8,128)S(1)}, u32[]{:S(2)}) copy-start(f32[128,768]{1,0:T(8,128)S(1)} %get-tuple-element.203) | copy-start | bytes 1179652
  40.3 6.2 %copy-start.64 = (f32[128]{0:T(128)}, f32[128]{0:T(128)S(1)}, u32[]{:S(2)}) copy-start(f32[128]{0:T(128)S(1)} %broadcast_multiply_fusion.3) | copy-start | bytes 1540
  41.1 5.5 %copy-start.68 = (f32[128]{0:T(128)}, f32[128]{0:T(128)S(1)}, u32[]{:S(2)}) copy-start(f32[128]{0:T(128)S(1)} %fusion.34) | copy-start | bytes 1540
  41.1 5.5 %slice-start = ((s8[4718592]{0:T(1024)(128)(4,1)}), s8[4194304]{0:T(1024)(128)(4,1)S(1)}, s32[]{:S(2)}) async-start(s8[4718592]{0:T(1024)(128)(4,1)} %bitcast.103), calls=%async_computation | async-start | bytes 8388608
  41.3 5.3 %copy-start.53 = (bf16[128,768]{1,0:T(8,128)(2,1)}, bf16[128,768]{1,0:T(8,128)(2,1)S(1)}, u32[]{:S(2)}) copy-start(bf16[128,768]{1,0:T(8,128)(2,1)S(1)} %fusion.23.refs_0_) | copy-start | bytes 589828
  41.3 5.3 %slice-start.1 = ((s8[4718592]{0:T(1024)(128)(4,1)}), s8[524288]{0:T(1024)(128)(4,1)S(1)}, s32[]{:S(2)}) async-start(s8[4718592]{0:T(1024)(128)(4,1)} %bitcast.103), calls=%async_computation.1 | async-start | bytes 1048576
  41.3 5.3 %copy-start.62 = (f32[768]{0:T(1024)S(1)}, f32[768]{0:T(1024)}, u32[]{:S(2)}) copy-start(f32[768]{0:T(1024)} %get-tuple-element.219) | copy-start | bytes 9220
  46.6 1.7 copy-start.58
  46.6 1.8 copy-start.72
  46.7 2.6 copy-start.30
  47.6 1.2 copy-start.66
  52.2 29.4 %copy-start.57 = (f32[768]{0:T(1024)S(1)}, f32[768]{0:T(1024)}, u32[]{:S(2)}) copy-start(f32[768]{0:T(1024)} %get-tuple-element.157) | copy-start | bytes 9220
  52.2 29.6 %copy-start.45 = (bf16[768,1536]{1,0:T(8,128)(2,1)S(1)}, bf16[768,1536]{1,0:T(8,128)(2,1)}, u32[]{:S(2)}) copy-start(bf16[768,1536]{1,0:T(8,128)(2,1)} %param.36) | copy-start | bytes 7077892
  52.2 29.6 %copy-start.81 = (f32[1536]{0:T(1024)S(1)}, f32[1536]{0:T(1024)}, u32[]{:S(2)}) copy-start(f32[1536]{0:T(1024)} %param.38) | copy-start | bytes 18436
  79.5 4.6 %copy-start.2 = (bf16[192,2048]{1,0:T(8,128)(2,1)}, bf16[192,2048]{1,0:T(8,128)(2,1)S(1)}, u32[]{:S(2)}) copy-start(bf16[192,2048]{1,0:T(8,128)(2,1)S(1)} %get-tuple-element.42.buf.other) | copy-start | bytes 2359300
  79.5 4.6 %copy-start.15 = (bf16[6,64,128]{2,1,0:T(8,128)(2,1)}, bf16[6,64,128]{2,1,0:T(8,128)(2,1)S(1)}, u32[]{:S(2)}) copy-start(bf16[6,64,128]{2,1,0:T(8,128)(2,1)S(1)} %get-tuple-element.41) | copy-start | bytes 294916
  79.5 4.6 %copy-start.17 = (f32[8,2048]{1,0:T(8,128)}, f32[8,2048]{1,0:T(8,128)S(1)}, u32[]{:S(2)}) copy-start(f32[8,2048]{1,0:T(8,128)S(1)} %get-tuple-element.44.lse.lse_s) | copy-start | bytes 196612
  81.9 2.3 copy-start.54
  81.9 2.3 copy-start.44
  81.9 2.3 copy-start.61
  84.2 1.8 copy-start.60
  87.6 1.6 copy-start.55
  89.3 1.5 copy-start.52
  90.8 2.4 copy-start.43
  90.8 5.0 %copy-start.25 = (s32[6]{0:T(128)S(1)}, s32[6]{0:T(128)}, u32[]{:S(2)}) copy-start(s32[6]{0:T(128)} %flag_ref.3) | copy-start | bytes 76
  95.8 1.1 copy-start.3
  100.6 25.6 %copy-start.29 = (f32[128,768]{1,0:T(8,128)S(1)}, f32[128,768]{1,0:T(8,128)}, u32[]{:S(2)}) copy-start(f32[128,768]{1,0:T(8,128)} %copy-done.28) | copy-start | bytes 1179652
  100.6 25.6 %copy-start.31 = (bf16[768,1152]{1,0:T(8,128)(2,1)S(1)}, bf16[768,1152]{1,0:T(8,128)(2,1)}, u32[]{:S(2)}) copy-start(bf16[768,1152]{1,0:T(8,128)(2,1)} %param.33) | copy-start | bytes 5308420
  100.6 25.6 %copy-start.38 = (f32[128,768]{1,0:T(8,128)S(1)}, f32[128,768]{1,0:T(8,128)}, u32[]{:S(2)}) copy-start(f32[128,768]{1,0:T(8,128)} %copy-done.37) | copy-start | bytes 1179652
  100.6 25.6 %copy-start.67 = (f32[128]{0:T(128)S(1)}, f32[128]{0:T(128)}, u32[]{:S(2)}) copy-start(f32[128]{0:T(128)} %copy-done.66) | copy-start | bytes 1540
  100.6 25.6 %copy-start.71 = (f32[128]{0:T(128)S(1)}, f32[128]{0:T(128)}, u32[]{:S(2)}) copy-start(f32[128]{0:T(128)} %copy-done.70) | copy-start | bytes 1540
  126.1 1.4 copy-start.41
  126.1 1.4 copy-start.42
  126.2 1.3 copy-start.79
  126.2 1.7 copy-start.83
  127.5 1.5 copy-start.82
  127.5 6.5 %slice-start.2 = ((s8[4718592]{0:T(1024)(128)(4,1)}), s8[4194304]{0:T(1024)(128)(4,1)S(1)}, s32[]{:S(2)}) async-start(s8[4718592]{0:T(1024)(128)(4,1)} %bitcast.105), calls=%async_computation.2 | async-start | bytes 8388608
  127.9 6.1 %copy-start.56 = (bf16[128,768]{1,0:T(8,128)(2,1)}, bf16[128,768]{1,0:T(8,128)(2,1)S(1)}, u32[]{:S(2)}) copy-start(bf16[128,768]{1,0:T(8,128)(2,1)S(1)} %get-tuple-element.189.refs_3_) | copy-start | bytes 589828
  129.0 4.9 %copy-start.27 = (f32[128,768]{1,0:T(8,128)S(1)}, f32[128,768]{1,0:T(8,128)}, u32[]{:S(2)}) copy-start(f32[128,768]{1,0:T(8,128)} %copy-done.26) | copy-start | bytes 1179652
  129.0 5.0 %slice-start.3 = ((s8[4718592]{0:T(1024)(128)(4,1)}), s8[524288]{0:T(1024)(128)(4,1)S(1)}, s32[]{:S(2)}) async-start(s8[4718592]{0:T(1024)(128)(4,1)} %bitcast.105), calls=%async_computation.3 | async-start | bytes 1048576
  129.0 5.0 %copy-start.65 = (f32[128]{0:T(128)S(1)}, f32[128]{0:T(128)}, u32[]{:S(2)}) copy-start(f32[128]{0:T(128)} %copy-done.64) | copy-start | bytes 1540
  129.0 5.0 %copy-start.69 = (f32[128]{0:T(128)S(1)}, f32[128]{0:T(128)}, u32[]{:S(2)}) copy-start(f32[128]{0:T(128)} %copy-done.68) | copy-start | bytes 1540
  134.0 2.4 copy-start.40
  134.0 2.4 copy-start.77
  136.4 2.4 copy-start.34
  141.7 1.1 copy-start.4
  143.8 1.1 copy-start.11
  146.6 33.2 %copy-start.36 = (f32[128,768]{1,0:T(8,128)S(1)}, f32[128,768]{1,0:T(8,128)}, u32[]{:S(2)}) copy-start(f32[128,768]{1,0:T(8,128)} %copy-done.35) | copy-start | bytes 1179652
  179.7 1.4 copy-start.1
  179.8 1.4 copy-start.32
  179.8 1.4 copy-start.73
  179.8 1.4 copy-start.75
  327.7 1.2 copy-start.6
  (24 other events, 19.1 us)

commit v3 on v2

v3 whole, which is shorter than its diff:
```python
import jax
import jax.numpy as jnp
from jax import lax
from jax.experimental import pallas as pl
from jax.experimental.pallas import tpu as pltpu
from jax.sharding import PartitionSpec as P

MESH = pl.DeviceIdType.MESH
LOG2E = 1.4426950408889634
C2 = 0.125 * LOG2E
SEQ = 2048
QC = 256
KT = 256
NKT = SEQ // KT
MIB = 1 << 20


def dot(a, b):
    return jnp.dot(a, b, preferred_element_type=jnp.float32)


def place():
    b = lax.axis_index("blk")
    r = lax.rem(lax.rem(b, 4) - b // 4 + 7, 4)
    return b, 3 * (b // 4) + r, r < 3


def owner_of(hh):
    y = hh // 3
    return 4 * y + lax.rem(y + lax.rem(hh, 3) + 1, 4)


def copy_to(src, dst, send_sem, recv_sem, d):
    return pltpu.make_async_remote_copy(
        src_ref=src,
        dst_ref=dst,
        send_sem=send_sem,
        recv_sem=recv_sem,
        device_id={"blk": d},
        device_id_type=MESH,
    )


def start_to(src, dst, send_sem, recv_sem, d, b):
    @pl.when(d != b)
    def _():
        copy_to(src, dst, send_sem, recv_sem, d).start()

    @pl.when(d == b)
    def _():
        pltpu.make_async_copy(src, dst, recv_sem).start()


def sent_to(src, dst, send_sem, recv_sem, d, b):
    @pl.when(d != b)
    def _():
        copy_to(src, dst, send_sem, recv_sem, d).wait_send()


def got(dst, recv_sem):
    pltpu.make_async_copy(dst, dst, recv_sem).wait()


def lanes(start, size):
    return pl.ds(pl.multiple_of(start, 128), size)


def fold(v):
    return jnp.sum(v.reshape(v.shape[0] // 8, 8, v.shape[1]), axis=0)


def key_ok(length):
    rows = lax.broadcasted_iota(jnp.int32, (KT, QC), 0) + (SEQ - KT)
    return rows < length


def natural(x):
    return x.astype(jnp.float32).T.astype(jnp.bfloat16)


def weight_row(len_ref, flag_ref, head, first, use):
    q = lax.broadcasted_iota(jnp.int32, (1, QC), 1) + first
    factor = jnp.where(use, flag_ref[head].astype(jnp.float32) * (2.0 * SEQ), 0.0)
    return jnp.where(q < len_ref[0], factor, 0.0)


SMEM = pl.BlockSpec(memory_space=pltpu.SMEM)
VMEM = pl.BlockSpec(memory_space=pltpu.VMEM)
DMA = pltpu.SemaphoreType.DMA
BF = jnp.bfloat16
F32 = jnp.float32


SQRT_HALF = 0.7071067811865476
INV_SQRT_2PI = 0.3989422804014327


def dot_t(a, b):
    return lax.dot_general(a, b, (((1,), (1,)), ((), ())), preferred_element_type=F32)


def norm_forward(v, gain, shift):
    center = v - jnp.mean(v, axis=-1, keepdims=True)
    scale = lax.rsqrt(jnp.mean(center * center, axis=-1, keepdims=True) + 1e-06)
    unit = center * scale
    return unit * gain + shift, unit, scale


def norm_backward(grad, gain, unit, scale):
    scaled = grad * gain
    mean_one = jnp.mean(scaled, axis=-1, keepdims=True)
    mean_two = jnp.mean(scaled * unit, axis=-1, keepdims=True)
    return (
        (scaled - mean_one - unit * mean_two) * scale,
        jnp.sum(grad * unit, axis=0, keepdims=True),
        jnp.sum(grad, axis=0, keepdims=True),
    )


def qkv_blocks(low, w, bias, src, heads):
    span = heads * 64
    for part in range(3):
        joint = dot(low, w[:, part * span : (part + 1) * span])
        if part != 1:
            first = 0 if part == 0 else span
            joint = joint + bias[:, first : first + span]
        src[:, part * 64 : (part + 1) * 64, :] = joint.T.astype(BF).reshape(heads, 64, 128)


def dense_up(residual, attended, w_out, w_up, w_down, up_bias, vec, act, slope, unit1, scale1, normed_low):
    ff = up_bias.shape[1]
    first = residual + dot(attended, w_out) + vec[0:1, :]
    normed, unit, scale = norm_forward(first, vec[1:2, :], vec[2:3, :])
    unit1[...] = unit
    scale1[...] = jnp.broadcast_to(scale, (128, 128))
    low = normed.astype(BF)
    normed_low[...] = low
    step = 512
    for j in range(ff // step):
        cols = slice(j * step, (j + 1) * step)
        u = dot(low, w_up[:, cols]) + up_bias[:, cols]
        cdf = 0.5 + 0.5 * lax.erf(u * SQRT_HALF)
        act[:, cols] = (u * cdf).astype(BF)
        slope[:, cols] = (cdf + u * (jnp.exp(-0.5 * u * u) * INV_SQRT_2PI)).astype(slope.dtype)
    second = normed + dot(act[...], w_down) + vec[3:4, :]
    return norm_forward(second, vec[4:5, :], vec[5:6, :])


def dense_down(grad, unit2, scale2, unit1, scale1, w_out, w_up, w_down, vec, slope, gu, g2r, g1r, sums, row):
    ff = w_up.shape[1]
    g2, gain_two, shift_two = norm_backward(grad, vec[4:5, :], unit2, scale2)
    low2 = g2.astype(BF)
    g2r[...] = low2
    step = 512
    for j in range(ff // step):
        cols = slice(j * step, (j + 1) * step)
        g = dot_t(low2, w_down[cols, :]) * slope[:, cols].astype(F32)
        gu[:, cols] = g.astype(BF)
        total = jnp.sum(g, axis=0, keepdims=True)
        done = 0
        while done < step:
            at = j * step + done
            size = min(step - done, 768 - at % 768)
            sums[row + 6 + at // 768 : row + 7 + at // 768, at % 768 : at % 768 + size] = total[:, done : done + size]
            done += size
    g1, gain_one, shift_one = norm_backward(g2 + dot_t(gu[...], w_up[...]), vec[1:2, :], unit1, scale1)
    low1 = g1.astype(BF)
    g1r[...] = low1
    rows = (
        jnp.sum(g1, axis=0, keepdims=True), gain_one, shift_one,
        jnp.sum(g2, axis=0, keepdims=True), gain_two, shift_two,
    )
    for i, value in enumerate(rows):
        sums[row + i : row + i + 1, :] = value
    return g1, dot_t(low1, w_out[...])


def load_all(pairs, sem):
    copies = [pltpu.make_async_copy(a, b, sem.at[i]) for i, (a, b) in enumerate(pairs)]
    for copy in copies:
        copy.start()
    return copies


def forward_stage(c_score, c_exp, c_out, do, par, q_at, kn, v_ref, s_ref, p_ref, st, put, length):
    if do[0]:
        q = q_at(c_score)
    m8 = jnp.full((8, QC), -3e38, F32)
    l8 = jnp.zeros((8, QC), F32)
    out = jnp.zeros((64, QC), F32)
    top = st[1 - par, 0:1, :]
    for t in range(NKT):
        rows = slice(t * KT, (t + 1) * KT)
        if do[0]:
            s = dot(kn[rows, :], q)
            if t == NKT - 1:
                s = jnp.where(key_ok(length), s, -1e30)
            s_ref[par, rows, :] = s
            m8 = jnp.maximum(m8, jnp.max(s.reshape(KT // 8, 8, QC), axis=0))
        if do[1]:
            p = jnp.exp2(s_ref[1 - par, rows, :] * C2 - top)
            l8 = l8 + fold(p)
            p_ref[1 - par, rows, :] = p.astype(BF)
        if do[2]:
            out = out + dot(v_ref[128:192, rows], p_ref[par, rows, :])
    if do[2]:
        put(c_out, out / st[2 + par, 0:1, :], st[4 + par, 0:1, :])
    if do[1]:
        total = jnp.sum(l8, axis=0, keepdims=True)
        st[3 - par] = jnp.broadcast_to(total, (8, QC))
        st[5 - par] = jnp.broadcast_to(top + jnp.log2(total), (8, QC))
    if do[0]:
        st[par] = jnp.broadcast_to(jnp.max(m8, axis=0, keepdims=True) * C2, (8, QC))


def forward_chunks(n, *rest):
    forward_stage(0, 0, 0, (1, 0, 0), 0, *rest)
    forward_stage(1, 0, 0, (1, 1, 0), 1, *rest)

    def body(i, carry):
        forward_stage(2 * i, 2 * i - 1, 2 * i - 2, (1, 1, 1), 0, *rest)
        forward_stage(2 * i + 1, 2 * i, 2 * i - 1, (1, 1, 1), 1, *rest)
        return carry

    lax.fori_loop(1, n // 2, body, 0)
    forward_stage(0, n - 1, n - 2, (0, 1, 1), 0, *rest)
    forward_stage(0, 0, n - 1, (0, 0, 1), 1, *rest)


def backward_chunk(c, prev, par, at, kn, k2n, vn, kt_ref, length, pf, gf, x_ref, acc, put):
    q, q2, do, lse, lse2, weight = at(c)
    pq, _, pdo, _, _, _ = at(prev)
    both = jnp.concatenate([pq, pdo], axis=0).astype(F32).T
    col = lax.broadcasted_iota(jnp.int32, (QC, 128), 1)
    rhs = jnp.concatenate(
        [jnp.where(col < 64, both, 0.0), jnp.where(col < 64, 0.0, both)], axis=0
    ).astype(BF)
    d8 = jnp.zeros((8, QC), F32)
    dq = jnp.zeros((64, QC), F32)
    for t in range(NKT):
        rows = slice(t * KT, (t + 1) * KT)
        p = jnp.exp2(dot(kn[rows, :], q) * C2 - lse)
        p2 = jnp.exp2(dot(k2n[rows, :], q2) * C2 - lse2)
        if t == NKT - 1:
            ok = key_ok(length)
            p = jnp.where(ok, p, 0.0)
            p2 = jnp.where(ok, p2, 0.0)
        g = dot(vn[rows, :], do) + weight * (p - p2)
        d8 = d8 + fold(p * g)
        pf[rows, :] = p
        gf[rows, :] = g
        x_ref[par, rows, QC:] = p.astype(BF)
        acc[rows, :] += dot(x_ref[1 - par, rows, :], rhs)
        dq = dq + dot(kt_ref[64:128, rows], x_ref[1 - par, rows, :QC])
    put(prev, dq * 0.125)
    delta = jnp.sum(d8, axis=0, keepdims=True)
    for t in range(NKT):
        rows = slice(t * KT, (t + 1) * KT)
        x_ref[par, rows, :QC] = (pf[rows, :] * (gf[rows, :] - delta)).astype(BF)


def backward_last(prev, par, at, kt_ref, x_ref, acc, put):
    pq, _, pdo, _, _, _ = at(prev)
    both = jnp.concatenate([pq, pdo], axis=0).astype(F32).T
    col = lax.broadcasted_iota(jnp.int32, (QC, 128), 1)
    rhs = jnp.concatenate(
        [jnp.where(col < 64, both, 0.0), jnp.where(col < 64, 0.0, both)], axis=0
    ).astype(BF)
    dq = jnp.zeros((64, QC), F32)
    for t in range(NKT):
        rows = slice(t * KT, (t + 1) * KT)
        acc[rows, :] += dot(x_ref[par, rows, :], rhs)
        dq = dq + dot(kt_ref[64:128, rows], x_ref[par, rows, :QC])
    put(prev, dq * 0.125)


def back_blocks(acc, dkv_buf):
    row = lax.broadcasted_iota(jnp.int32, (128, SEQ), 0)
    total = acc[...].T
    dkv_buf[...] = jnp.where(row < 64, total * 0.125, total).astype(BF)


def natural_wide(blocks):
    return blocks.astype(F32).T.astype(BF)


def loop(n, body):
    def step(i, carry):
        body(i)
        return carry

    lax.fori_loop(0, n, step, 0)


def greet_start():
    b = lax.axis_index("blk")
    sem = pltpu.get_barrier_semaphore()
    loop(15, lambda i: pl.semaphore_signal(
        sem, inc=1, device_id={"blk": lax.rem(b + 1 + i, 16)}, device_id_type=MESH
    ))


def greet_end():
    pl.semaphore_wait(pltpu.get_barrier_semaphore(), 15)


def forward_kernel(
    len_ref, x_in, source, flags, cot,
    w_qkv_t, w_out_t, w_up_t, w_down_t, w_qkv_s, w_out_s, w_up_s, w_down_s,
    bias_t, upb_t, vec_t, bias_s, upb_s, vec_s,
    output, buf_t, dist, buf_s, lse_t, lse_d, lse_s,
    x0_low, normed_low_t, hidden_low, normed_low_s, g1r_s, g2r_s,
    att_t, act_t, att_s, act_s, gu_s,
    slope_t, unit1_t, scale1_t, unit2_t, scale2_t, g1_s, datt_s, sums,
    v_qkv_t, v_out_t, v_up_t, v_down_t, v_qkv_s, v_out_s, v_up_s, v_down_s,
    x0_ref, src_t, src_s, land_t, land_s, o_t, o_s, kn, s_ref, p_ref, st,
    slope_s, unit1_s, scale1_s,
    w_sem, t_send, t_recv, d_send, d_recv, a_send, a_recv, lse_sem,
    s_send, s_recv, b_send, b_recv, local_sem,
):
    b, hh, owner = place()
    half, head = hh // 6, lax.rem(hh, 6)
    greet_start()
    weights = load_all(
        [
            (w_qkv_t, v_qkv_t), (w_out_t, v_out_t), (w_up_t, v_up_t), (w_down_t, v_down_t),
            (w_qkv_s, v_qkv_s), (w_out_s, v_out_s), (w_up_s, v_up_s), (w_down_s, v_down_s),
        ],
        w_sem,
    )
    length = len_ref[0]
    replaced = flags[...] == 1
    place_of = lax.broadcasted_iota(jnp.int32, (128, 128), 0)
    turned = jnp.where((place_of == source[...]) & replaced, 1.0, 0.0)
    chooser = turned.T
    taken = dot(chooser.astype(BF), x_in[...])
    x0 = jnp.where(jnp.sum(chooser, axis=1, keepdims=True) > 0.5, taken, x_in[...].astype(F32))
    x0_ref[...] = x0
    low = x0.astype(BF)
    x0_low[...] = low
    weights[0].wait()
    qkv_blocks(low, v_qkv_t, bias_t, src_t, 12)
    greet_end()

    mine = lanes(b * 128, 128)

    def t_copy(h):
        return src_t.at[h], buf_t.at[:, mine], t_send.at[h], t_recv.at[b], owner_of(h), b

    def d_copy(h):
        return src_t.at[h, 0:128], dist.at[:, mine], d_send.at[h], d_recv.at[b], owner_of(h + 6), b

    loop(12, lambda j: start_to(*t_copy(lax.rem(j + b, 12))))
    loop(6, lambda j: start_to(*d_copy(lax.rem(j + b, 6))))

    def a_copy(d):
        return o_t.at[:, lanes(d * 128, 128)], land_t.at[hh], a_send.at[d], a_recv.at[hh], d, b

    @pl.when(owner)
    def _():
        loop(16, lambda i: got(buf_t.at[:, lanes(i * 128, 128)], t_recv.at[i]))
        kn[...] = natural(buf_t[64:128, :])

        def put(c, o, stat):
            here = lanes(c * QC, QC)
            o_t[:, here] = o.astype(BF)
            lse_t[:, here] = jnp.broadcast_to(stat, (8, QC))
            for i in range(2):
                start_to(*a_copy(2 * c + i))

        forward_chunks(
            SEQ // QC, lambda c: buf_t[0:64, lanes(c * QC, QC)], kn, buf_t, s_ref, p_ref, st, put, length
        )

    @pl.when(owner & (hh < 6))
    def _():
        lse_d[:, 0:1024] = lse_t[:, 0:1024]
        copy_to(
            lse_t.at[:, 1024:2048], lse_d.at[:, 1024:2048], lse_sem.at[0], lse_sem.at[1], owner_of(hh + 6)
        ).start()
        pltpu.make_async_copy(buf_t.at[0:128], dist, local_sem.at[0]).start()

    loop(12, lambda h: got(land_t.at[h], a_recv.at[h]))
    att_t[...] = natural_wide(land_t[...].reshape(768, 128))
    for i in (1, 2, 3):
        weights[i].wait()
    hidden, unit, scale = dense_up(
        x0_ref[...], att_t[...], v_out_t[...], v_up_t, v_down_t[...], upb_t, vec_t,
        act_t, slope_t, unit1_t, scale1_t, normed_low_t,
    )
    unit2_t[...] = unit
    scale2_t[...] = jnp.broadcast_to(scale, (128, 128))
    x0_ref[...] = hidden
    low = hidden.astype(BF)
    hidden_low[...] = low
    weights[4].wait()
    qkv_blocks(low, v_qkv_s, bias_s, src_s, 6)

    def s_copy(h):
        return src_s.at[lax.rem(h, 6)], buf_s.at[:, mine], s_send.at[h], s_recv.at[b], owner_of(h), b

    loop(12, lambda j: start_to(*s_copy(lax.rem(j + b, 12))))

    def b_copy(j):
        return o_s.at[:, lanes(j * 128, 128)], land_s.at[head], b_send.at[j], b_recv.at[head], 8 * half + j, b

    @pl.when(owner)
    def _():
        lse_s[:, 0:1024] = jnp.full((8, 1024), 1e30, F32)
        loop(16, lambda i: got(buf_s.at[:, lanes(i * 128, 128)], s_recv.at[i]))
        kn[...] = natural(buf_s[64:128, :])

        def put(c, o, stat):
            o_s[:, lanes(c * QC, QC)] = o.astype(BF)
            lse_s[:, lanes(half * 1024 + c * QC, QC)] = jnp.broadcast_to(stat, (8, QC))
            for i in range(2):
                start_to(*b_copy(2 * c + i))

        forward_chunks(
            1024 // QC, lambda c: buf_s[0:64, lanes(half * 1024 + c * QC, QC)],
            kn, buf_s, s_ref, p_ref, st, put, length,
        )

    @pl.when(owner & (hh >= 6))
    def _():
        copy_to(
            lse_s.at[:, 1024:2048], lse_s.at[:, 1024:2048], lse_sem.at[2], lse_sem.at[3], owner_of(hh - 6)
        ).start()

    loop(6, lambda h: got(land_s.at[h], b_recv.at[h]))
    att_s[...] = natural_wide(land_s[...].reshape(384, 128))
    for i in (5, 6, 7):
        weights[i].wait()
    result, unit, scale = dense_up(
        x0_ref[...], att_s[...], v_out_s[...], v_up_s, v_down_s[...], upb_s, vec_s,
        act_s, slope_s, unit1_s, scale1_s, normed_low_s,
    )
    output[...] = result
    sums[...] = jnp.zeros((24, 768), F32)
    g1, datt = dense_down(
        cot[...].astype(F32), unit, scale, unit1_s[...], scale1_s[:, 0:1],
        v_out_s, v_up_s, v_down_s, vec_s, slope_s, gu_s, g2r_s, g1r_s, sums, 12,
    )
    g1_s[...] = g1
    datt_s[...] = datt.T.astype(BF).reshape(6, 64, 128)

    @pl.when(owner)
    def _():
        loop(16, lambda d: sent_to(*a_copy(d)))
        loop(8, lambda j: sent_to(*b_copy(j)))

    @pl.when(owner & (hh < 6))
    def _():
        copy_to(
            lse_t.at[:, 1024:2048], lse_d.at[:, 1024:2048], lse_sem.at[0], lse_sem.at[1], owner_of(hh + 6)
        ).wait_send()
        pltpu.make_async_copy(buf_t.at[0:128], dist, local_sem.at[0]).wait()
        got(lse_s.at[:, 1024:2048], lse_sem.at[3])

    @pl.when(owner & (hh >= 6))
    def _():
        loop(16, lambda i: got(dist.at[:, lanes(i * 128, 128)], d_recv.at[i]))
        got(lse_d.at[:, 1024:2048], lse_sem.at[1])
        copy_to(
            lse_s.at[:, 1024:2048], lse_s.at[:, 1024:2048], lse_sem.at[2], lse_sem.at[3], owner_of(hh - 6)
        ).wait_send()

    loop(12, lambda h: sent_to(*t_copy(h)))
    loop(6, lambda h: sent_to(*d_copy(h)))
    loop(12, lambda h: sent_to(*s_copy(h)))


def backward_kernel(
    len_ref, flag_ref, source, flags,
    w_qkv_s, w_down_t, w_up_t, w_out_t, w_qkv_t, vec_t,
    buf_t, dist, buf_s, lse_t, lse_d, lse_s,
    slope_t, unit1_t, scale1_t, unit2_t, scale2_t, g1_s, datt_s, sums_s,
    grad_in, joined_t, joined_s, gu_t, g1r_t, g2r_t, sums,
    v_qkv_s, v_down_t, v_up_t, v_out_t, v_qkv_t,
    src_t, do_s, do_t, dq_s, dkv_s, dqkv_t, dq_buf, dq_buf2, dkv_buf, dkv_buf2,
    kn, k2n, vn, pf, gf, x_ref, acc, g1_ref,
    w_sem, s1, r1, s2, r2, s3, r3, s4, r4, s5, r5, s6, r6,
):
    b, hh, owner = place()
    half, head = hh // 6, lax.rem(hh, 6)
    greet_start()
    weights = load_all(
        [(w_qkv_s, v_qkv_s), (w_down_t, v_down_t), (w_up_t, v_up_t), (w_out_t, v_out_t), (w_qkv_t, v_qkv_t)],
        w_sem,
    )
    length = len_ref[0]
    greet_end()

    def c1(h):
        return (
            datt_s.at[h], do_s.at[:, lanes(lax.rem(b, 8) * 128, 128)],
            s1.at[h], r1.at[lax.rem(b, 8)], owner_of(h + 6 * (b // 8)), b,
        )

    def c2(j):
        return dq_buf.at[:, lanes(j * 128, 128)], dq_s.at[head], s2.at[j], r2.at[head], 8 * half + j, b

    def c3(d):
        return dkv_buf.at[:, lanes(d * 128, 128)], dkv_s.at[hh], s3.at[d], r3.at[hh], d, b

    def c4(h):
        return src_t.at[h], do_t.at[:, lanes(b * 128, 128)], s4.at[h], r4.at[b], owner_of(h), b

    def c5(d):
        return dq_buf2.at[:, lanes(d * 128, 128)], dqkv_t.at[hh, 0:64], s5.at[d], r5.at[hh], d, b

    def c6(d):
        return dkv_buf2.at[:, lanes(d * 128, 128)], dqkv_t.at[hh, 64:192], s6.at[d], r6.at[hh], d, b

    def run_chunks(n, at, kt_ref, put):
        acc[...] = jnp.zeros_like(acc)
        x_ref[1] = jnp.zeros((SEQ, 2 * QC), BF)
        rest = (at, kn, k2n, vn, kt_ref, length, pf, gf, x_ref, acc)

        def pair(i):
            backward_chunk(
                2 * i, jnp.maximum(2 * i - 1, 0), 0, *rest, lambda c, g: put(c, g, i > 0)
            )
            backward_chunk(2 * i + 1, 2 * i, 1, *rest, lambda c, g: put(c, g, True))

        loop(n // 2, pair)
        backward_last(n - 1, 1, at, kt_ref, x_ref, acc, lambda c, g: put(c, g, True))

    def send_pair(copy, c, real):
        if real is True:
            for i in range(2):
                start_to(*copy(2 * c + i))
        else:
            @pl.when(real)
            def _():
                for i in range(2):
                    start_to(*copy(2 * c + i))

    loop(6, lambda j: start_to(*c1(lax.rem(j + b, 6))))

    @pl.when(owner)
    def _():
        kn[...] = natural(buf_s[64:128, :])
        vn[...] = natural(buf_s[128:192, :])
        k2n[...] = natural(dist[64:128, :])
        loop(8, lambda i: got(do_s.at[:, lanes(i * 128, 128)], r1.at[i]))

        def at(c):
            first = half * 1024 + c * QC
            here = lanes(first, QC)
            return (
                buf_s[0:64, here], dist[0:64, here], do_s[:, lanes(c * QC, QC)],
                lse_s[0:1, here], lse_d[0:1, here], weight_row(len_ref, flag_ref, head, first, True),
            )

        def put(c, g, real):
            dq_buf[:, lanes(c * QC, QC)] = g.astype(BF)
            send_pair(c2, c, real)

        run_chunks(1024 // QC, at, buf_s, put)
        back_blocks(acc, dkv_buf)
        loop(16, lambda i: start_to(*c3(lax.rem(b + i, 16))))

    loop(6, lambda h: got(dq_s.at[h], r2.at[h]))
    loop(12, lambda h: got(dkv_s.at[h], r3.at[h]))
    joined_s[:, 0:384] = natural_wide(dq_s[...].reshape(384, 128))
    for part in range(2):
        rows = slice(64 * part, 64 * part + 64)
        both = dkv_s[0:6, rows, :].astype(F32) + dkv_s[6:12, rows, :].astype(F32)
        joined_s[:, 384 * (part + 1) : 384 * (part + 2)] = both.reshape(384, 128).T.astype(BF)
    sums[...] = sums_s[...]
    low_sums = jnp.sum(joined_s[...].astype(F32), axis=0, keepdims=True)
    sums[20:21, 0:384] = low_sums[:, 0:384]
    sums[20:21, 384:768] = low_sums[:, 768:1152]
    weights[0].wait()
    grad_hidden = g1_s[...] + dot_t(joined_s[...], v_qkv_s[...])
    for i in (1, 2, 3):
        weights[i].wait()
    g1, datt = dense_down(
        grad_hidden, unit2_t[...], scale2_t[:, 0:1], unit1_t[...], scale1_t[:, 0:1],
        v_out_t, v_up_t, v_down_t, vec_t, slope_t, gu_t, g2r_t, g1r_t, sums, 0,
    )
    g1_ref[...] = g1
    src_t[...] = datt.T.astype(BF).reshape(12, 64, 128)
    loop(12, lambda j: start_to(*c4(lax.rem(j + b, 12))))

    @pl.when(owner)
    def _():
        kn[...] = natural(buf_t[64:128, :])
        vn[...] = natural(buf_t[128:192, :])
        k2n[...] = natural(buf_s[64:128, :])
        loop(16, lambda i: got(do_t.at[:, lanes(i * 128, 128)], r4.at[i]))

        def at(c):
            here = lanes(c * QC, QC)
            return (
                buf_t[0:64, here], buf_s[0:64, here], do_t[:, here],
                lse_t[0:1, here], lse_s[0:1, here], weight_row(len_ref, flag_ref, head, c * QC, hh < 6),
            )

        def put(c, g, real):
            dq_buf2[:, lanes(c * QC, QC)] = g.astype(BF)
            send_pair(c5, c, real)

        run_chunks(SEQ // QC, at, buf_t, put)
        back_blocks(acc, dkv_buf2)
        loop(16, lambda i: start_to(*c6(lax.rem(b + i, 16))))

    loop(12, lambda h: got(dqkv_t.at[h, 0:64], r5.at[h]))
    loop(12, lambda h: got(dqkv_t.at[h, 64:192], r6.at[h]))
    for part in range(3):
        joined_t[:, 768 * part : 768 * (part + 1)] = natural_wide(
            dqkv_t[:, 64 * part : 64 * (part + 1), :].reshape(768, 128)
        )
    for row, part in ((10, 0), (11, 2)):
        sums[row : row + 1, :] = jnp.sum(
            joined_t[:, 768 * part : 768 * (part + 1)].astype(F32), axis=0, keepdims=True
        )
    weights[4].wait()
    grad = g1_ref[...] + dot_t(joined_t[...], v_qkv_t[...])
    place_of = lax.broadcasted_iota(jnp.int32, (128, 128), 0)
    turned = jnp.where((place_of == source[...]) & (flags[...] == 1), 1.0, 0.0)
    back = turned.astype(BF)
    one = grad.astype(BF)
    rest = grad - one.astype(F32)
    two = rest.astype(BF)
    three = (rest - two.astype(F32)).astype(BF)
    copied = dot(back, one) + dot(back, two) + dot(back, three)
    kept = jnp.sum(turned.T, axis=1, keepdims=True) < 0.5
    grad_in[...] = jnp.where(kept, grad, 0.0) + copied

    @pl.when(owner)
    def _():
        loop(8, lambda j: sent_to(*c2(j)))
        loop(16, lambda d: sent_to(*c3(d)))
        loop(16, lambda d: sent_to(*c5(d)))
        loop(16, lambda d: sent_to(*c6(d)))

    loop(6, lambda h: sent_to(*c1(h)))
    loop(12, lambda h: sent_to(*c4(h)))


ANY = pl.BlockSpec(memory_space=pl.ANY)


def mega_call(kernel, ident, specs, outs, scratch, args, name):
    return pl.pallas_call(
        kernel,
        name=name,
        out_shape=tuple(jax.ShapeDtypeStruct(s, t) for s, t in outs),
        in_specs=specs,
        out_specs=tuple(VMEM for _ in outs),
        scratch_shapes=scratch,
        compiler_params=pltpu.CompilerParams(
            collective_id=ident, has_side_effects=True, vmem_limit_bytes=60 * MIB
        ),
    )(*args)


def vb(*shape):
    return pltpu.VMEM(shape, BF)


def vf(*shape):
    return pltpu.VMEM(shape, F32)


def run_forward(lengths, x_in, source, flags, cot, weights, smalls):
    outs = [
        ((128, 768), F32), ((192, SEQ), BF), ((128, SEQ), BF), ((192, SEQ), BF),
        ((8, SEQ), F32), ((8, SEQ), F32), ((8, SEQ), F32),
        ((128, 768), BF), ((128, 768), BF), ((128, 768), BF), ((128, 768), BF), ((128, 768), BF), ((128, 768), BF),
        ((128, 768), BF), ((128, 3072), BF), ((128, 384), BF), ((128, 1536), BF), ((128, 1536), BF),
        ((128, 3072), BF), ((128, 768), F32), ((128, 128), F32), ((128, 768), F32), ((128, 128), F32),
        ((128, 768), F32), ((6, 64, 128), BF), ((24, 768), F32),
    ]
    scratch = [
        vb(768, 2304), vb(768, 768), vb(768, 3072), vb(3072, 768),
        vb(768, 1152), vb(384, 768), vb(768, 1536), vb(1536, 768),
        vf(128, 768), vb(12, 192, 128), vb(6, 192, 128), vb(12, 64, 128), vb(6, 64, 128),
        vb(64, SEQ), vb(64, 1024), vb(SEQ, 64), vf(2, SEQ, QC), vb(2, SEQ, QC), vf(6, 8, QC),
        vb(128, 1536), vf(128, 768), vf(128, 128),
        DMA((8,)), DMA((12,)), DMA((16,)), DMA((6,)), DMA((16,)), DMA((16,)), DMA((12,)), DMA((4,)),
        DMA((12,)), DMA((16,)), DMA((8,)), DMA((6,)), DMA((1,)),
    ]
    specs = [SMEM] + [VMEM] * 4 + [ANY] * 8 + [VMEM] * 6
    return mega_call(
        forward_kernel, 1, specs, outs, scratch, (lengths, x_in, source, flags, cot, *weights, *smalls), "forward"
    )


def run_backward(lengths, head_flags, source, flags, weights, vec_t, kept):
    outs = [
        ((128, 768), F32), ((128, 2304), BF), ((128, 1152), BF), ((128, 3072), BF),
        ((128, 768), BF), ((128, 768), BF), ((24, 768), F32),
    ]
    scratch = [
        vb(768, 1152), vb(3072, 768), vb(768, 3072), vb(768, 768), vb(768, 2304),
        vb(12, 64, 128), vb(64, 1024), vb(64, SEQ), vb(6, 64, 128), vb(12, 128, 128), vb(12, 192, 128),
        vb(64, 1024), vb(64, SEQ), vb(128, SEQ), vb(128, SEQ),
        vb(SEQ, 64), vb(SEQ, 64), vb(SEQ, 64), vf(SEQ, QC), vf(SEQ, QC), vb(2, SEQ, 2 * QC), vf(SEQ, 128),
        vf(128, 768),
        DMA((5,)), DMA((6,)), DMA((8,)), DMA((8,)), DMA((6,)), DMA((16,)), DMA((12,)),
        DMA((12,)), DMA((16,)), DMA((16,)), DMA((12,)), DMA((16,)), DMA((12,)),
    ]
    specs = [SMEM] * 2 + [VMEM] * 2 + [ANY] * 5 + [VMEM] * (1 + len(kept))
    return mega_call(
        backward_kernel, 2, specs, outs, scratch,
        (lengths, head_flags, source, flags, *weights, vec_t, *kept), "backward",
    )

CUTS = ((0, 12, 12), (12, 6, 6), (18, 2, 1), (20, 12, 12), (32, 5, 4), (37, 3, 3), (40, 9, 9), (49, 6, 6))
PARTS = ((0, 20), (20, 20), (40, 16))
MEMBERS = ((0, 1, 2), (3, 4, 5), (6, 7))
TILES = 56
WIDE = TILES * 128


def where_am_i():
    dp, blk = lax.axis_index("dp"), lax.axis_index("blk")
    return dp // 2, lax.rem(dp, 2), blk // 4, lax.rem(blk, 4)


def at_axis(axis, v):
    x, c, y, z = where_am_i()
    if axis == "x":
        return {"dp": 2 * v + c, "blk": 4 * y + z}
    if axis == "y":
        return {"dp": 2 * x + c, "blk": 4 * v + z}
    return {"dp": 2 * x + c, "blk": 4 * y + v}


def send_to(src, dst, send_sem, recv_sem, device):
    return pltpu.make_async_remote_copy(
        src_ref=src, dst_ref=dst, send_sem=send_sem, recv_sem=recv_sem,
        device_id=device, device_id_type=MESH,
    )


ORDERS = ("xyz", "yzx", "zxy")


def reduce_kernel(*refs):
    narrow, wide, small = refs[0:8], refs[8:16], refs[16]
    out, sums = refs[17:19]
    (nt, cf, sml, sma, pb, l1, a1, l2, a2, l3, a3,
     own_sem, n_send, n_recv, c_send, c_recv, s_send, s_recv,
     st_send, st_recv, f_send, f_recv) = refs[19:]
    x, c, y, z = where_am_i()
    here = {"x": x, "y": y, "z": z}
    dp, blk = 2 * x + c, 4 * y + z
    me = 16 * dp + blk
    partner = {"dp": 2 * x + 1 - c, "blk": blk}

    def holder(p, q, core):
        first, second = me // 32, lax.rem(me // 8, 4)
        at = dict(zip(ORDERS[p], (first, second, q)))
        return 2 * at["x"] + core, 4 * at["y"] + at["z"]

    def owner(p, k):
        i = 32 * here[ORDERS[p][0]] + 8 * here[ORDERS[p][1]] + k
        return i, {"dp": i // 16, "blk": lax.rem(i, 16)}

    barrier = pltpu.get_barrier_semaphore()
    pl.semaphore_signal(barrier, inc=1, device_id=partner, device_id_type=MESH)
    for axis in "xyz":
        for j in range(1, 4):
            pl.semaphore_signal(
                barrier, inc=1, device_id=at_axis(axis, lax.rem(here[axis] + j, 4)), device_id_type=MESH
            )
    for p in range(3):
        for q in range(4):
            for core in range(2):
                hd, hb = holder(p, q, core)

                pl.semaphore_signal(
                    barrier, inc=1, device_id={"dp": hd, "blk": hb}, device_id_type=MESH
                )
    pl.semaphore_wait(barrier, 34)

    small_copies = [send_to(small, sml.at[0], s_send.at[0], s_recv.at[0], partner)]
    small_copies[0].start()

    def small_step(axis, n):
        src = sma.at[n // 3]
        for j in range(1, 4):
            slot = n + j
            copy = send_to(
                src, sml.at[slot], s_send.at[slot], s_recv.at[slot],
                at_axis(axis, lax.rem(here[axis] + j, 4)),
            )
            copy.start()
            small_copies.append(copy)

    def small_sum(n):
        for j in range(1, 4):
            small_copies[n + j].wait_recv()
        return sma[n // 3] + sml[n + 1] + sml[n + 2] + sml[n + 3]

    n_copies, c_copies, own_copies = [], [], []
    for m, (first, count, step) in enumerate(CUTS):
        cols = slice(first * 128, (first + count) * 128)
        keep = pltpu.make_async_copy(
            wide[m].at[:, lanes(c * step * 128, count * 128)], cf.at[0:128, cols], own_sem.at[m]
        )
        keep.start()
        own_copies.append(keep)
        give = send_to(
            wide[m].at[:, lanes((1 - c) * step * 128, count * 128)], cf.at[128:256, cols],
            c_send.at[m], c_recv.at[m], partner,
        )
        give.start()
        c_copies.append(give)
        nt[m, :, 0:128] = narrow[m][...].T
        give = send_to(
            nt.at[m, :, 0:128], nt.at[m, :, 128:256], n_send.at[m], n_recv.at[m], partner
        )
        give.start()
        n_copies.append(give)

    def part_cols(p):
        return slice(PARTS[p][0] * 128, (PARTS[p][0] + PARTS[p][1]) * 128)

    def stage_copies(p, stage):
        axis = ORDERS[p][stage]
        copies = []
        for j in range(1, 4):
            v = lax.rem(here[axis] + j, 4)
            if stage == 0:
                src = pb.at[pl.ds(pl.multiple_of(192 * v, 16), 192), part_cols(p)]
                dst = l1.at[j - 1, :, part_cols(p)]
            elif stage == 1:
                src = a1.at[pl.ds(pl.multiple_of(48 * v, 16), 48), part_cols(p)]
                dst = l2.at[j - 1, :, part_cols(p)]
            else:
                q = PARTS[p][1] * 32
                src = a2.at[:, lanes(PARTS[p][0] * 128 + v * q, q)]
                dst = l3.at[j - 1, :, slice(PARTS[p][0] * 32, PARTS[p][0] * 32 + q)]
            n = 9 * stage + 3 * p + j - 1
            copies.append(send_to(src, dst, st_send.at[n], st_recv.at[n], at_axis(axis, v)))
        return copies

    copies = {}
    for p in range(3):
        for m in MEMBERS[p]:
            first, count, _ = CUTS[m]
            own_copies[m].wait()
            c_copies[m].wait_recv()
            n_copies[m].wait_recv()
            size = 3 if count % 3 == 0 else count

            def piece(i, carry, m=m, first=first, size=size):
                cols = lanes((first + i * size) * 128, size * 128)
                pb[:, cols] = dot(nt[m], cf[:, cols]).astype(BF)
                return carry

            lax.fori_loop(0, count // size, piece, 0)
        copies[p, 0] = stage_copies(p, 0)
        for copy in copies[p, 0]:
            copy.start()

    small_copies[0].wait_recv()
    sma[0] = small[...] + sml[0]
    small_step("x", 0)

    for p in range(3):
        cols = part_cols(p)
        base = 192 * here[ORDERS[p][0]]
        for copy in copies[p, 0]:
            copy.wait_recv()

        def add1(r, carry, cols=cols, base=base):
            rows = pl.ds(pl.multiple_of(16 * r, 16), 16)
            own = pl.ds(pl.multiple_of(base + 16 * r, 16), 16)
            total = pb[own, cols].astype(F32)
            for j in range(3):
                total = total + l1[j, rows, cols].astype(F32)
            a1[rows, cols] = total.astype(BF)
            return carry

        lax.fori_loop(0, 12, add1, 0)
        copies[p, 1] = stage_copies(p, 1)
        for copy in copies[p, 1]:
            copy.start()

    sma[1] = small_sum(0)
    small_step("y", 3)

    for p in range(3):
        cols = part_cols(p)
        base = 48 * here[ORDERS[p][1]]
        for copy in copies[p, 1]:
            copy.wait_recv()

        def add2(r, carry, cols=cols, base=base):
            rows = pl.ds(pl.multiple_of(16 * r, 16), 16)
            own = pl.ds(pl.multiple_of(base + 16 * r, 16), 16)
            total = a1[own, cols].astype(F32)
            for j in range(3):
                total = total + l2[j, rows, cols].astype(F32)
            a2[rows, cols] = total.astype(BF)
            return carry

        lax.fori_loop(0, 3, add2, 0)
        copies[p, 2] = stage_copies(p, 2)
        for copy in copies[p, 2]:
            copy.start()

    sma[2] = small_sum(3)
    small_step("z", 6)

    for p in range(3):
        q = PARTS[p][1] * 32
        off = PARTS[p][0] * 32
        third = here[ORDERS[p][2]]
        for copy in copies[p, 2]:
            copy.wait_recv()
        total = a2[:, lanes(PARTS[p][0] * 128 + third * q, q)].astype(F32)
        for j in range(3):
            total = total + l3[j, :, off : off + q].astype(F32)
        for k in range(8):
            a3[k, 0:6, off : off + q] = total[6 * k : 6 * k + 6, :]

    def final(p, k):
        q = PARTS[p][1] * 32
        off = PARTS[p][0] * 32
        third = here[ORDERS[p][2]]
        i, device = owner(p, k)
        src = a3.at[k, :, slice(off, off + q)]
        dst = out.at[:, lanes((c * TILES + PARTS[p][0]) * 128 + third * q, q)]
        slot = f_recv.at[(c * 3 + p) * 4 + third]
        return i, src, dst, slot, send_to(src, dst, f_send.at[8 * p + k], slot, device)

    for p in range(3):
        for k in range(8):
            i, src, dst, slot, copy = final(p, k)

            @pl.when(i != me)
            def _():
                copy.start()

            @pl.when(i == me)
            def _():
                pltpu.make_async_copy(src, dst, slot).start()

    for core in range(2):
        for p in range(3):
            q = PARTS[p][1] * 32
            for third in range(4):
                start = (core * TILES + PARTS[p][0]) * 128 + third * q
                got(out.at[:, start : start + q], f_recv.at[(core * 3 + p) * 4 + third])
    for p in range(3):
        for k in range(8):
            i, src, dst, slot, copy = final(p, k)

            @pl.when(i != me)
            def _():
                copy.wait_send()
    sums[...] = small_sum(6)
    for copy in small_copies + n_copies + c_copies + sum(copies.values(), []):
        copy.wait_send()


def reduce_all(narrow, wide, small):
    return pl.pallas_call(
        reduce_kernel,
        name="reduce",
        out_shape=(jax.ShapeDtypeStruct((8, 2 * WIDE), F32), jax.ShapeDtypeStruct((24, 768), F32)),
        in_specs=[VMEM] * 17,
        out_specs=(VMEM, VMEM),
        scratch_shapes=[
            pltpu.VMEM((8, 768, 256), BF), pltpu.VMEM((256, WIDE), BF), pltpu.VMEM((10, 24, 768), F32), pltpu.VMEM((3, 24, 768), F32),
            pltpu.VMEM((768, WIDE), BF), pltpu.VMEM((3, 192, WIDE), BF), pltpu.VMEM((192, WIDE), BF),
            pltpu.VMEM((3, 48, WIDE), BF), pltpu.VMEM((48, WIDE), BF),
            pltpu.VMEM((3, 48, WIDE // 4), BF), pltpu.VMEM((8, 8, WIDE // 4), F32),
            DMA((8,)), DMA((8,)), DMA((8,)), DMA((8,)), DMA((8,)), DMA((10,)), DMA((10,)),
            DMA((27,)), DMA((27,)), DMA((24,)), DMA((24,)),
        ],
        compiler_params=pltpu.CompilerParams(
            collective_id=5, has_side_effects=True, vmem_limit_bytes=56 * MIB
        ),
    )(*narrow, *wide, small)


def unpack_kernel(whole, sums, *outs):
    def columns(m):
        first, count, step = CUTS[m]
        both = [whole[:, first * 128 : (first + count) * 128]]
        skip = count - step
        start = TILES + first + skip
        both.append(whole[:, start * 128 : (start + count - skip) * 128])
        return jnp.concatenate(both, axis=1)

    for m, o in ((6, 0), (5, 2), (0, 3), (3, 4), (4, 7), (2, 9), (1, 10), (7, 11)):
        outs[o][...] = columns(m)[0:6]
    i = 16 * lax.axis_index("dp") + lax.axis_index("blk")

    def turn(rows, by):
        return pltpu.roll(rows, lax.rem(768 - by, 768), 1)

    def pick(first, count, per):
        row = first + (i * per) // 768
        wide = jnp.broadcast_to(sums[pl.ds(row, 1), :], (8, 768))
        return turn(wide, lax.rem(i * per, 768))[0:1, 0:per]

    outs[1][...] = pick(10, 2, 12)
    outs[5][...] = pick(6, 4, 24)
    outs[8][...] = pick(20, 1, 6)
    outs[12][...] = pick(18, 2, 12)
    outs[6][...] = turn(sums[0:8, :], i * 6)[0:6, 0:6]
    outs[13][...] = turn(sums[8:24, :], i * 6)[4:10, 0:6]


def unpack(whole, sums):
    shapes = (
        (6, 2304), (1, 12), (6, 768), (6, 3072), (6, 3072), (1, 24), (6, 6),
        (6, 1152), (1, 6), (6, 384), (6, 1536), (6, 1536), (1, 12), (6, 6),
    )
    outs = list(
        pl.pallas_call(
            unpack_kernel,
            name="unpack",
            out_shape=tuple(jax.ShapeDtypeStruct(s, F32) for s in shapes),
            in_specs=[VMEM] * 2,
            out_specs=tuple(VMEM for _ in shapes),
            compiler_params=pltpu.CompilerParams(vmem_limit_bytes=40 * MIB),
        )(whole, sums)
    )
    for i in (1, 5, 8, 12):
        outs[i] = outs[i].reshape(-1)
    for i in (2, 4, 9, 11):
        outs[i] = outs[i].T
    return tuple(outs)


def per_device(
    inputs, aug_source, aug_flags, lengths, head_flags, cotangent,
    qkv_teacher, qv_bias_teacher, out_teacher, up_teacher, down_teacher, up_bias_teacher, vectors_teacher,
    qkv_student, qv_bias_student, out_student, up_student, down_student, up_bias_student, vectors_student,
):
    (
        output, buf_t, dist, buf_s, lse_t, lse_d, lse_s,
        x0_low, normed_low_t, hidden_low, normed_low_s, g1r_s, g2r_s,
        att_t, act_t, att_s, act_s, gu_s,
        slope_t, unit1_t, scale1_t, unit2_t, scale2_t, g1_s, datt_s, sums_s,
    ) = run_forward(
        lengths, inputs[0], aug_source, aug_flags, cotangent[0],
        (qkv_teacher, out_teacher, up_teacher, down_teacher, qkv_student, out_student, up_student, down_student),
        (
            qv_bias_teacher[None], up_bias_teacher[None], vectors_teacher,
            qv_bias_student[None], up_bias_student[None], vectors_student,
        ),
    )
    grad_in, joined_t, joined_s, gu_t, g1r_t, g2r_t, sums = run_backward(
        lengths, head_flags, aug_source, aug_flags,
        (qkv_student, down_teacher, up_teacher, out_teacher, qkv_teacher), vectors_teacher,
        (
            buf_t, dist, buf_s, lse_t, lse_d, lse_s,
            slope_t, unit1_t, scale1_t, unit2_t, scale2_t, g1_s, datt_s, sums_s,
        ),
    )
    pairs = (
        (normed_low_t, gu_t), (normed_low_s, gu_s), (g1r_s, att_s), (g2r_t, act_t),
        (hidden_low, joined_s), (g1r_t, att_t), (x0_low, joined_t), (g2r_s, act_s),
    )
    whole, total = reduce_all([n for n, _ in pairs], [w for _, w in pairs], sums)
    return (output[None], grad_in[None]) + unpack(whole, total)


def solution(mesh):
    both = ("dp", "blk")
    row, flat, col = P(both, None), P(both), P(None, both)
    tokens, marks = P("dp", "blk", None), P("dp", "blk")
    return jax.shard_map(
        per_device,
        mesh=mesh,
        in_specs=(tokens, marks, marks, P("dp"), P(), tokens) + (P(),) * 14,
        out_specs=(tokens, tokens) + (row, flat, col, row, col, flat, col) * 2,
        check_vma=False,
    )
```

time: 343 us -> 233 us (0.68)
  local copies, waits for them, and re-layouts: 75.7 us -> 7.25 us
  matrix products: 34.3 us -> 0 us
  other arithmetic: 12.5 us -> 0 us
  Pallas kernels: 217 us -> 224 us
    dot_general x18 -> x0, matrix products: 34.3 us -> none  [the longest x8 15.2 us: times_transpose(): lax.dot_general(left_side, right_side, (((1,), (1,)), ((), ())), preferre...]
    unnamed x180 -> x10, local copies, waits for them, and re-layouts: 28.2 us -> 3.4 us
    reshape x20 -> x0, local copies, waits for them, and re-layouts: 23 us -> none  [the longest x8 9.39 us: layer_norm(): return center * lax.rsqrt(spread + 1e-06) * norm_gain + norm_shift]
    reduce_sum x16 -> x0, other arithmetic: 8.98 us -> none  [the longest x2 2.64 us: qkv_backward(): low_sums = jnp.sum(joined.astype(jnp.float32), axis=0)]
    pallas_call x6 -> x4, Pallas kernels: 217 us -> 224 us  [the longest x2 121 us: mega_call(): pl.pallas_call(kernel, name=name, out_shape=tuple((jax.ShapeDtypeStruct(s...]
    convert_element_type x4 -> x0, local copies, waits for them, and re-layouts: 7.33 us -> none  [the longest x2 3.95 us: qkv_forward(): return (joined + bias).astype(BF)]
    another operation x8 -> x0, local copies, waits for them, and re-layouts: 6.43 us -> none  [dense_backward(): jnp.stack([jnp.sum(grad_first, axis=0), grad_gain_one, grad_shift_one, jn...]
    slice x9 -> x0, local copies, waits for them, and re-layouts: 4.5 us -> none  [the longest x6 1.9 us: qkv_backward(): grad_bias = jnp.concatenate([low_sums[:span], low_sums[2 * span:]])]
where the time goes in v3:
time: 233 us
  Pallas kernels  224 us (96%)
  local copies, waits for them, and re-layouts  7.25 us (3%)
    pallas_call x2, Pallas kernels, mega_call(): pl.pallas_call(kernel, name=name, out_shape=tuple((jax.ShapeDtypeStruct(s...  121 us
    pallas_call x1, Pallas kernels, reduce_all(): pl.pallas_call(reduce_kernel, name='reduce', out_shape=(jax.ShapeDtypeStr...  102 us

profile of v3, /device:TPU:5, one launch (start us, length us, event | category | flops | bytes accessed | tf_op | source)
XLA Modules:
  0.0 232.9 jit_solution(5574591130941600734)
XLA Ops:
  1.3 1.3 broadcast_in_dim.20.bias_s
  2.6 1.3 broadcast_in_dim.18.bias_t
  3.9 1.3 broadcast_in_dim.21.upb_s
  5.1 58.9 %forward.1 = (f32[128,768]{1,0:T(8,128)}, bf16[192,2048]{1,0:T(8,128)(2,1)}, bf16[128,2048]{1,0:T(8,128)(2,1)}, bf16[192,2048]{1,0:T(8,128)(2,1)}, f32[8,2048]{1...) custom-call(s32[1]{0:T(128)S(6)} %copy.38.len_ref, ...), custom_call_target="tpu_custom_call" | custom-call | tf_op jit(solution)/shard_map/forward/pallas_call | solution.py:647
  64.1 62.5 %backward.1 = (f32[128,768]{1,0:T(8,128)}, bf16[128,2304]{1,0:T(8,128)(2,1)}, bf16[128,1152]{1,0:T(8,128)(2,1)}, bf16[128,3072]{1,0:T(8,128)(2,1)}, bf16[128,768...) custom-call(s32[1]{0:T(128)S(6)} %copy.38.len_ref, s32[6]{0:T(128)} %flag_ref.1, s32[1,128]{1,0:T(1,128)} %source.3, ...), custom_call_target="tpu_custom_call" | custom-call | tf_op jit(solution)/shard_map/backward/pallas_call | solution.py:647
  126.6 0.0 copy-start.2
  126.6 0.0 copy-start.3
  126.6 102.1 %reduce.1 = (f32[8,14336]{1,0:T(8,128)}, f32[24,768]{1,0:T(8,128)}) custom-call(bf16[128,768]{1,0:T(8,128)(2,1)} %get-tuple-element.81.refs_0_, bf16[128,768]{1,0:T(8,128)(2,1)} %get-tuple-element.82.refs_1_, bf16[128,768]{1,0:T(8,128)(2,1)} %get-tuple-element.83.refs_2_, bf16[128,768]{1,0:T(8,128)(2,1)} %get-tuple-element.84.refs_3_, ...), custom_call_target="tpu_custom_call" | custom-call | tf_op jit(solution)/shard_map/reduce/pallas_call | solution.py:965
  228.7 0.0 copy-start
  228.7 1.0 copy-done
  229.7 0.0 copy-start.1
  229.7 0.9 copy-done.1
  230.6 0.8 unpack.1
  231.4 0.0 copy-done.2
  231.4 0.7 copy.39
  232.2 0.0 copy-done.3
  232.2 0.7 copy.40
Async XLA Ops:
  126.6 104.8 %copy-start.2 = (f32[128,768]{1,0:T(8,128)S(1)}, f32[128,768]{1,0:T(8,128)}, u32[]{:S(2)}) copy-start(f32[128,768]{1,0:T(8,128)} %get-tuple-element.65) | copy-start | bytes 1179652
  126.6 105.6 %copy-start.3 = (f32[128,768]{1,0:T(8,128)S(1)}, f32[128,768]{1,0:T(8,128)}, u32[]{:S(2)}) copy-start(f32[128,768]{1,0:T(8,128)} %get-tuple-element.80) | copy-start | bytes 1179652
  228.7 1.0 copy-start
  229.7 0.9 copy-start.1
